TPU v7x, 512 devices: a whole 4x4x16 slice. The times are simulated.
512 devices in a mesh: blk: 256 (over y, x, z), pair: 2 (over core).
Axes of the slice: x: 4, y: 4, z: 16, core: 2. Of those that a mesh axis runs over, the one named last changes fastest.
Arguments:
- features: bfloat16 [524288, 128], P('blk'), may hold values from -6 to 6
- subspace: float32 [128, 524288], P(None, 'blk'), may hold values from -18 to 18
- offsets: int32 [2, 256], P('pair', 'blk'), may hold values from -3 to 3, as said below
- counts: int32 [2, 256], P('pair', 'blk'), may hold values from 1 to 2048
Outputs:
- new_field: float32 [128, 524288], P(None, 'blk')
- ritz_gram: float32 [128, 128], replicated
Inputs may be any that keep to these rules, and one draw needn't show every extreme that they name: offsets are never 0 and b + offsets[r, b] is always one of the 256 blocks.
All inputs are finite; a program needn't handle non-finite values.
Results may differ from a plain program's by a relative error of at most 0.003.
The roundings to bfloat16 on the way count: a program that leaves them out, or rounds other values in their place, can miss the bound.
Values may be sent and summed in bfloat16 or wider, within the bound.
No kernel may reach another device: no remote copies, remote signals or barrier semaphores. Data moves between devices by JAX's collectives and lax.ppermute only.
A program may use at most 64 MiB of HBM per device.

v0:
```python
import jax
import jax.numpy as jnp
from jax import lax
from jax.sharding import PartitionSpec as P

REACH = 3


def from_behind(shard, axis, by):
    length = lax.axis_size(axis)
    pairs = [(i, i + by) for i in range(length) if 0 <= i + by < length]
    return lax.ppermute(shard, axis, pairs)


def kernel_apply(particles, columns, col_values, col_keep, row_ids, col_ids):
    kernel_width = 2.0 * particles.shape[1]
    row_norms = jnp.sum(jnp.square(particles.astype(jnp.float32)), axis=1)
    col_norms = jnp.sum(jnp.square(columns.astype(jnp.float32)), axis=1)
    inner_prod = jnp.dot(particles, columns.T, preferred_element_type=jnp.float32)
    distance_sq = row_norms[:, None] + col_norms[None, :] - 2.0 * inner_prod
    distinct = (row_ids[:, None] != col_ids[None, :]).astype(jnp.float32)
    weight = jnp.exp(-distance_sq / kernel_width) * col_keep[None, :] * distinct
    degree = jnp.sum(weight, axis=1)
    weighted = lax.dot_general(
        col_values,
        weight.astype(jnp.bfloat16),
        (((1,), (1,)), ((), ())),
        preferred_element_type=jnp.float32,
    )
    return (weighted, degree)


def apply_tiles(particles, columns, col_values, col_keep, row_ids, col_ids):
    block_len, feat_len = particles.shape
    sub_len = col_values.shape[0]
    tile_len = 512
    tile_count = block_len // tile_len

    def per_tile(tile_args):
        return kernel_apply(tile_args[0], columns, col_values, col_keep, tile_args[1], col_ids)

    weighted, degree = lax.map(
        per_tile,
        (particles.reshape(tile_count, tile_len, feat_len), row_ids.reshape(tile_count, tile_len)),
    )
    weighted = jnp.transpose(weighted, (1, 0, 2)).reshape(sub_len, block_len)
    return (weighted, degree.reshape(block_len))


def slot_of(distance):
    return distance + REACH - (distance > 0).astype(jnp.int32)


def per_device(features, subspace, offsets, counts):
    block_len, feat_len = features.shape
    sub_len = subspace.shape[0]
    pairs = lax.axis_size("pair")
    core_index = lax.axis_index("pair")
    values = subspace.astype(jnp.bfloat16)
    offset = offsets[0, 0]
    used_count = counts[0, 0]
    chosen = slot_of(offset)
    packed = jnp.concatenate(
        [features, values.reshape(sub_len * block_len // feat_len, feat_len)], axis=0
    )
    nearby = []
    for position in range(2 * REACH + 1):
        distance = position - REACH
        if distance != 0:
            nearby.append(from_behind(packed, "blk", -distance))
    stacked = jnp.stack(nearby)
    picked = lax.dynamic_index_in_dim(stacked, chosen, 0, keepdims=False)
    partner_feats = picked[:block_len]
    partner_values = picked[block_len:].reshape(sub_len, block_len)
    self_len = block_len // pairs
    self_start = core_index * self_len
    self_feats = lax.dynamic_slice_in_dim(features, self_start, self_len, 0)
    self_values = lax.dynamic_slice_in_dim(values, self_start, self_len, 1)
    row_ids = jnp.arange(block_len, dtype=jnp.int32)
    columns = jnp.concatenate([partner_feats, self_feats], axis=0)
    col_values = jnp.concatenate([partner_values, self_values], axis=1)
    col_keep = jnp.concatenate(
        [(row_ids < used_count).astype(jnp.float32), jnp.ones((self_len,), jnp.float32)]
    )
    col_ids = jnp.concatenate(
        [jnp.full((block_len,), -1, jnp.int32), self_start + jnp.arange(self_len, dtype=jnp.int32)]
    )
    weighted, degree = apply_tiles(features, columns, col_values, col_keep, row_ids, col_ids)
    particle_total = float(lax.axis_size("blk") * block_len)
    weighted, degree = lax.psum((weighted, degree), "pair")
    new_field = weighted / degree[None, :]
    local_gram = jnp.dot(
        new_field, new_field.T, precision=lax.Precision.HIGHEST, preferred_element_type=jnp.float32
    )
    ritz_gram = lax.psum(local_gram, "blk") / particle_total
    return (new_field, ritz_gram)


def solution(mesh):
    placed = (P("blk", None), P(None, "blk"), P("pair", "blk"), P("pair", "blk"))
    return jax.shard_map(
        per_device, mesh=mesh, in_specs=placed, out_specs=(P(None, "blk"), P()), check_vma=False
    )
```

profile of v0, /device:TPU:1, one launch (start us, length us, event | category | flops | bytes accessed | tf_op | source)
XLA Modules:
  0.0 625.6 jit_solution(8193477951986404436)
XLA Ops:
  8.8 1.9 constant_dynamic-update-slice_fusion.1
  11.5 8.1 %collective-permute-start = (bf16[4096,128]{1,0:T(8,128)(2,1)}, bf16[4096,128]{1,0:T(8,128)(2,1)}, u32[]{:S(2)}, u32[]{:S(2)}) collective-permute-start(bf16[4096,128]{1,0:T(8,128)(2,1)} %constant_dynamic-update-slice_fusion), channel_id=1, source_target_pairs={{0,6},{2,8},{4,10},{6,12},{8,14},{10,16},{12,18},{14,20},{16,22},{... | collective-permute-start | bytes 3145736 | tf_op jit(solution)/shard_map/ppermute | solution.py:12
  19.5 7.1 %collective-permute-start.1 = (bf16[4096,128]{1,0:T(8,128)(2,1)}, bf16[4096,128]{1,0:T(8,128)(2,1)}, u32[]{:S(2)}, u32[]{:S(2)}) collective-permute-start(bf16[4096,128]{1,0:T(8,128)(2,1)} %constant_dynamic-update-slice_fusion), channel_id=1, source_target_pairs={{0,4},{2,6},{4,8},{6,10},{8,12},{10,14},{12,16},{14,18},{16,20},{1... | collective-permute-start | bytes 3145736 | tf_op jit(solution)/shard_map/ppermute | solution.py:12
  26.6 3.6 collective-permute-start.2
  34.9 1.7 constant_dynamic-slice_fusion.2
  36.6 39.1 %collective-permute-done = bf16[4096,128]{1,0:T(8,128)(2,1)} collective-permute-done((bf16[4096,128]{1,0:T(8,128)(2,1)}, bf16[4096,128]{1,0:T(8,128)(2,1)}, u32[]{:S(2)}, u32[]{:S(2)}) %collective-permute-start) | collective-permute-done | bytes 1048608 | tf_op jit(solution)/shard_map/ppermute | solution.py:12
  78.3 34.9 %collective-permute-done.1 = bf16[4096,128]{1,0:T(8,128)(2,1)} collective-permute-done((bf16[4096,128]{1,0:T(8,128)(2,1)}, bf16[4096,128]{1,0:T(8,128)(2,1)}, u32[]{:S(2)}, u32[]{:S(2)}) %collective-permute-start.1) | collective-permute-done | bytes 1048608 | tf_op jit(solution)/shard_map/ppermute | solution.py:12
  113.2 1.4 bitcast_dynamic-update-slice_fusion.4
  114.6 38.9 %collective-permute-done.2 = bf16[4096,128]{1,0:T(8,128)(2,1)} collective-permute-done((bf16[4096,128]{1,0:T(8,128)(2,1)}, bf16[4096,128]{1,0:T(8,128)(2,1)}, u32[]{:S(2)}, u32[]{:S(2)}) %collective-permute-start.2) | collective-permute-done | bytes 1048608 | tf_op jit(solution)/shard_map/ppermute | solution.py:12
  153.5 1.4 bitcast_dynamic-update-slice_fusion.3
  154.9 1.4 bitcast_dynamic-update-slice_fusion.2
  156.9 1.9 pad_maximum_fusion.1
  159.8 18.7 %while.12 = (s32[]{:T(128)}, f32[4,128,512]{1,2,0:T(8,128)S(1)}, f32[4,512]{1,0:T(4,128)S(1)}, s32[4,512]{1,0:T(4,128)S(1)}, s32[3072]{0:T(1024)S(1)}, /*index=5...) while((s32[]{:T(128)}, f32[4,128,512]{1,2,0:T(8,128)S(1)}, ...), condition=%wide.region_4.5_spmd, body=%wide.region_0.4_spmd.sunk | while | flops 822407168 | bytes 12386461 | solution.py:42
  160.5 2.9 fusion.26
  165.2 2.9 fusion.26
  169.8 2.9 fusion.26
  174.5 2.9 fusion.26
  178.5 1.3 copy.7
  179.9 3.9 psum.22
  183.8 51.6 %all-reduce.5.cloned.1.call-done = f32[128,2048]{1,0:T(8,128)} async-done(((f32[128,2048]{1,0:T(8,128)}), f32[128,2048]{1,0:T(8,128)}) %all-reduce.5.cloned.1.call-update) | async-done | bytes 1048592 | tf_op jit(solution)/shard_map/psum | solution.py:90
  235.3 1.3 broadcast_divide_fusion
  236.7 1.6 fusion.12
  238.3 379.0 %all-reduce.7.cloned.1.call-done = f32[128,128]{1,0:T(8,128)} async-done(((f32[128,128]{1,0:T(8,128)}), f32[128,128]{1,0:T(8,128)}) %all-reduce.7.cloned.1.call-update) | async-done | bytes 65552 | tf_op jit(solution)/shard_map/psum | solution.py:95
  617.3 1.5 broadcast_multiply_fusion
  (60 shorter events, 16.7 us)
Async XLA Ops:
  7.2 228.2 %all-reduce.5.cloned.1.call-start = ((), (), s32[]{:S(2)}) async-start(), calls=%async_computation | async-start | bytes 2097152 | tf_op jit(solution)/shard_map/psum | solution.py:90
  11.5 64.2 %collective-permute-start = (bf16[4096,128]{1,0:T(8,128)(2,1)}, bf16[4096,128]{1,0:T(8,128)(2,1)}, u32[]{:S(2)}, u32[]{:S(2)}) collective-permute-start(bf16[4096,128]{1,0:T(8,128)(2,1)} %constant_dynamic-update-slice_fusion), channel_id=1, source_target_pairs={{0,6},{2,8},{4,10},{6,12},{8,14},{10,16},{12,18},{14,20},{16,22},{... | collective-permute-start | bytes 3145736 | tf_op jit(solution)/shard_map/ppermute | solution.py:12
  19.5 93.7 %collective-permute-start.1 = (bf16[4096,128]{1,0:T(8,128)(2,1)}, bf16[4096,128]{1,0:T(8,128)(2,1)}, u32[]{:S(2)}, u32[]{:S(2)}) collective-permute-start(bf16[4096,128]{1,0:T(8,128)(2,1)} %constant_dynamic-update-slice_fusion), channel_id=1, source_target_pairs={{0,4},{2,6},{4,8},{6,10},{8,12},{10,14},{12,16},{14,18},{16,20},{1... | collective-permute-start | bytes 3145736 | tf_op jit(solution)/shard_map/ppermute | solution.py:12
  26.6 126.8 %collective-permute-start.2 = (bf16[4096,128]{1,0:T(8,128)(2,1)}, bf16[4096,128]{1,0:T(8,128)(2,1)}, u32[]{:S(2)}, u32[]{:S(2)}) collective-permute-start(bf16[4096,128]{1,0:T(8,128)(2,1)} %constant_dynamic-update-slice_fusion), channel_id=1, source_target_pairs={{0,2},{2,4},{4,6},{6,8},{8,10},{10,12},{12,14},{14,16},{16,18},{18... | collective-permute-start | bytes 3145736 | tf_op jit(solution)/shard_map/ppermute | solution.py:12
  30.2 124.6 %collective-permute-start.3 = (bf16[4096,128]{1,0:T(8,128)(2,1)}, bf16[4096,128]{1,0:T(8,128)(2,1)}, u32[]{:S(2)}, u32[]{:S(2)}) collective-permute-start(bf16[4096,128]{1,0:T(8,128)(2,1)} %constant_dynamic-update-slice_fusion), channel_id=1, source_target_pairs={{2,0},{4,2},{6,4},{8,6},{10,8},{12,10},{14,12},{16,14},{18,16},{20... | collective-permute-start | bytes 3145736 | tf_op jit(solution)/shard_map/ppermute | solution.py:12
  31.5 124.8 %collective-permute-start.4 = (bf16[4096,128]{1,0:T(8,128)(2,1)}, bf16[4096,128]{1,0:T(8,128)(2,1)S(1)}, u32[]{:S(2)}, u32[]{:S(2)}) collective-permute-start(bf16[4096,128]{1,0:T(8,128)(2,1)} %constant_dynamic-update-slice_fusion), channel_id=1, source_target_pairs={{4,0},{6,2},{8,4},{10,6},{12,8},{14,10},{16,12},{18,14},{20,16},{2... | collective-permute-start | bytes 3145736 | tf_op jit(solution)/shard_map/ppermute | solution.py:12
  75.7 80.7 %collective-permute-start.5 = (bf16[4096,128]{1,0:T(8,128)(2,1)}, bf16[4096,128]{1,0:T(8,128)(2,1)S(1)}, u32[]{:S(2)}, u32[]{:S(2)}) collective-permute-start(bf16[4096,128]{1,0:T(8,128)(2,1)} %constant_dynamic-update-slice_fusion), channel_id=1, source_target_pairs={{6,0},{8,2},{10,4},{12,6},{14,8},{16,10},{18,12},{20,14},{22,16},{... | collective-permute-start | bytes 3145736 | tf_op jit(solution)/shard_map/ppermute | solution.py:12
  154.8 5.0 copy-start.1
  160.5 3.0 copy-start.2
  165.1 2.9 copy-start.2
  169.8 2.9 copy-start.2
  174.5 2.9 copy-start.2
  179.8 437.5 %all-reduce.7.cloned.1.call-start = ((), (), s32[]{:S(2)}) async-start(), calls=%async_computation.1 | async-start | bytes 131072 | tf_op jit(solution)/shard_map/psum | solution.py:95
  236.7 382.1 %copy-start = (f32[128,2048]{1,0:T(8,128)}, f32[128,2048]{1,0:T(8,128)S(1)}, u32[]{:S(2)}) copy-start(f32[128,2048]{1,0:T(8,128)S(1)} %broadcast_divide_fusion) | copy-start | bytes 3145732
Sparse Core Ops, SparseCore 0:
  180.0 55.3 all-reduce.4
  242.2 375.0 all-reduce.6
where the time goes:
time: 636 us; the launch traced here: 626 us
  waiting for transfers between devices  544 us (86%)
  starting transfers between devices  22.7 us (4%)
  matrix products  17.3 us (3%)
  between operations  15.6 us (2%)
  local copies, waits for them, and re-layouts  12.9 us (2%)
  other arithmetic  9.52 us (1%)
    psum x1, waiting for transfers between devices, per_device(): ritz_gram = lax.psum(local_gram, 'blk') / particle_total  379 us
    ppermute x6, waiting for transfers between devices, from_behind(): return lax.ppermute(shard, axis, pairs)  113 us
    psum x1, waiting for transfers between devices, per_device(): weighted, degree = lax.psum((weighted, degree), 'pair')  51.6 us
    ppermute x6, starting transfers between devices, from_behind(): return lax.ppermute(shard, axis, pairs)  22.6 us
  transfers between devices with their start and end apart: 8, of which 5 were waited for; matrix products, arithmetic and copies ran while one was open for 1% of the time, Pallas kernels for 0%

commit v1 on v0

v1 whole, which is shorter than its diff:
```python
import functools

import jax
import jax.numpy as jnp
from jax import lax
from jax.experimental import pallas as pl
from jax.experimental.pallas import tpu as pltpu
from jax.sharding import PartitionSpec as P

REACH = 3
CHUNKS = 2
TILE = 256
FAR = 1e30
NT = (((1,), (1,)), ((), ()))
PARAMS = pltpu.CompilerParams(vmem_limit_bytes=40 * 2**20)


def pack_kernel(core_ref, feats_ref, field_ref, *packed_refs):
    rows = feats_ref.shape[0] // CHUNKS
    for chunk, packed_ref in enumerate(packed_refs):
        packed_ref[:rows, :] = feats_ref[chunk * rows : (chunk + 1) * rows, :]
        for at in range(0, rows, 128):
            start = chunk * rows + at
            packed_ref[rows + at : rows + at + 128, :] = field_ref[:, start : start + 128].astype(
                jnp.bfloat16
            )


def pack(core, features, subspace):
    block, feat = features.shape
    sub = subspace.shape[0]
    half = block // 2
    piece = jax.ShapeDtypeStruct((block // CHUNKS, feat), jnp.bfloat16)
    return pl.pallas_call(
        pack_kernel,
        grid_spec=pltpu.PrefetchScalarGridSpec(
            num_scalar_prefetch=1,
            grid=(1,),
            in_specs=[
                pl.BlockSpec((half, feat), lambda i, core: (core[0], 0)),
                pl.BlockSpec((sub, half), lambda i, core: (0, core[0])),
            ],
            out_specs=[pl.BlockSpec(piece.shape, lambda i, core: (0, 0))] * CHUNKS,
        ),
        out_shape=[piece] * CHUNKS,
        compiler_params=PARAMS,
        cost_estimate=pl.CostEstimate(flops=0, bytes_accessed=2 * 2**20, transcendentals=0),
        name="pack",
    )(core, features, subspace)


def norms_of(part):
    wide = part.astype(jnp.float32)
    return jnp.sum(wide * wide, axis=1, keepdims=True) * (1.0 / 256.0)


def add_columns(feats, vals, col_norms, rows_t, row_norms, acc, deg, apart=None):
    inner = jnp.dot(feats, rows_t, preferred_element_type=jnp.float32)
    weight = jnp.exp(inner - col_norms - row_norms)
    if apart is not None:
        weight = jnp.where(apart, weight, 0.0)
    deg[...] += jnp.sum(weight.reshape(TILE // 8, 8, weight.shape[1]), axis=0)
    acc[...] += jnp.dot(vals, weight.astype(jnp.bfloat16), preferred_element_type=jnp.float32)


def side_by_side(read, start):
    return jnp.concatenate([read(start), read(start + 128)], axis=1)


def self_kernel(core_ref, feats_ref, *refs):
    packed = refs[:CHUNKS]
    acc, deg, rows_t, row_norms = refs[CHUNKS:]
    block = feats_ref.shape[0]
    for at in range(0, block, TILE):
        wide = feats_ref[at : at + TILE, :].astype(jnp.float32).T
        row_norms[:, at : at + TILE] = jnp.sum(wide * wide, axis=0, keepdims=True) * (1.0 / 256.0)
        rows_t[:, at : at + TILE] = (wide * (1.0 / 128.0)).astype(jnp.bfloat16)
    acc[...] = jnp.zeros_like(acc)
    deg[...] = jnp.zeros_like(deg)
    cols = packed[0].shape[0] // 2
    for chunk in range(CHUNKS):
        held = packed[chunk]

        @pl.loop(0, cols // TILE)
        def _(step):
            at = pl.multiple_of(step * TILE, TILE)
            feats = held[pl.ds(at, TILE), :]
            vals = side_by_side(
                lambda start: held[pl.ds(pl.multiple_of(start, 128), 128), :], cols + at
            )
            first = core_ref[0] * (block // 2) + chunk * cols + at
            col_ids = first + lax.broadcasted_iota(jnp.int32, (TILE, block), 0)
            row_ids = lax.broadcasted_iota(jnp.int32, (TILE, block), 1)
            add_columns(
                feats, vals, norms_of(feats), rows_t[...], row_norms[...], acc, deg, col_ids != row_ids
            )


def apply_self(core, features, packed):
    block, feat = features.shape
    outs = [
        jax.ShapeDtypeStruct((feat, block), jnp.float32),
        jax.ShapeDtypeStruct((8, block), jnp.float32),
        jax.ShapeDtypeStruct((feat, block), jnp.bfloat16),
        jax.ShapeDtypeStruct((1, block), jnp.float32),
    ]
    whole = lambda i, core: (0, 0)
    return pl.pallas_call(
        self_kernel,
        grid_spec=pltpu.PrefetchScalarGridSpec(
            num_scalar_prefetch=1,
            grid=(1,),
            in_specs=[pl.BlockSpec(x.shape, whole) for x in (features, *packed)],
            out_specs=[pl.BlockSpec(x.shape, whole) for x in outs],
        ),
        out_shape=outs,
        compiler_params=PARAMS,
        cost_estimate=pl.CostEstimate(
            flops=2 * 2 * block * block // 2 * feat,
            bytes_accessed=4 * 2**20,
            transcendentals=block * block // 2,
        ),
        name="own_block",
    )(core, features, *packed)


def partner_kernel(scalars, rows_t, row_norms, own_acc, own_deg, *refs):
    near = refs[: 2 * REACH * CHUNKS]
    acc, deg, held, sems = refs[2 * REACH * CHUNKS :]
    cols = held.shape[2] // 2
    for turn in range(2):
        for slot in range(2 * REACH):

            @pl.when(scalars[turn] == slot)
            def _():
                for chunk in range(CHUNKS):
                    pltpu.make_async_copy(
                        near[slot * CHUNKS + chunk], held.at[turn, chunk], sems.at[turn, chunk]
                    ).start()

    acc[...] = own_acc[...]
    deg[...] = own_deg[...]
    for turn in range(2):
        for chunk in range(CHUNKS):
            pltpu.make_async_copy(near[chunk], held.at[turn, chunk], sems.at[turn, chunk]).wait()
            first = scalars[4] * (CHUNKS * cols) + chunk * cols

            @pl.loop(0, cols // TILE)
            def _(step):
                at = pl.multiple_of(step * TILE, TILE)
                feats = held[turn, chunk, pl.ds(at, TILE), :]
                vals = side_by_side(
                    lambda start: held[turn, chunk, pl.ds(pl.multiple_of(start, 128), 128), :],
                    cols + at,
                )
                ids = first + at + lax.broadcasted_iota(jnp.int32, (TILE, 1), 0)
                norms = jnp.where(ids < scalars[2 + turn], norms_of(feats), FAR)
                add_columns(feats, vals, norms, rows_t[...], row_norms[...], acc, deg)


def apply_partners(scalars, rows_t, row_norms, own_acc, own_deg, near):
    feat, block = rows_t.shape
    half = block // 2
    outs = [
        jax.ShapeDtypeStruct((feat, half), jnp.float32),
        jax.ShapeDtypeStruct((8, half), jnp.float32),
    ]
    picked = lambda i, scalars: (0, scalars[5])
    whole = lambda i, scalars: (0, 0)
    return pl.pallas_call(
        partner_kernel,
        grid_spec=pltpu.PrefetchScalarGridSpec(
            num_scalar_prefetch=1,
            grid=(1,),
            in_specs=[
                pl.BlockSpec((feat, half), picked),
                pl.BlockSpec((1, half), picked),
                pl.BlockSpec((feat, half), picked),
                pl.BlockSpec((8, half), picked),
            ]
            + [pl.BlockSpec(memory_space=pl.ANY)] * len(near),
            out_specs=[pl.BlockSpec(x.shape, whole) for x in outs],
            scratch_shapes=[
                pltpu.VMEM((2, CHUNKS, *near[0].shape), jnp.bfloat16),
                pltpu.SemaphoreType.DMA((2, CHUNKS)),
            ],
        ),
        out_shape=outs,
        compiler_params=PARAMS,
        cost_estimate=pl.CostEstimate(
            flops=2 * 2 * half * block * feat,
            bytes_accessed=3 * 2**20,
            transcendentals=half * block,
        ),
        name="partners",
    )(scalars, rows_t, row_norms, own_acc, own_deg, *near)


def field_kernel(acc, deg, far_acc, far_deg, field, gram):
    degree = jnp.sum(deg[...] + far_deg[...], axis=0, keepdims=True)
    field[...] = (acc[...] + far_acc[...]) / degree
    gram[...] = lax.dot_general(
        field[...],
        field[...],
        NT,
        precision=lax.Precision.HIGHEST,
        preferred_element_type=jnp.float32,
    )


def make_field(acc, deg, far_acc, far_deg):
    sub = acc.shape[0]
    outs = [
        jax.ShapeDtypeStruct(acc.shape, jnp.float32),
        jax.ShapeDtypeStruct((sub, sub), jnp.float32),
    ]
    return pl.pallas_call(
        field_kernel,
        out_shape=outs,
        compiler_params=PARAMS,
        cost_estimate=pl.CostEstimate(
            flops=12 * sub * sub * acc.shape[1], bytes_accessed=2 * 2**20, transcendentals=0
        ),
        name="field",
    )(acc, deg, far_acc, far_deg)


def join_kernel(core_ref, own, other, out):
    @pl.when(pl.program_id(0) == core_ref[0])
    def _():
        out[...] = own[...]

    @pl.when(pl.program_id(0) != core_ref[0])
    def _():
        out[...] = other[...]


def join(core, own, other):
    sub, half = own.shape
    return pl.pallas_call(
        join_kernel,
        grid_spec=pltpu.PrefetchScalarGridSpec(
            num_scalar_prefetch=1,
            grid=(2,),
            in_specs=[pl.BlockSpec((sub, half), lambda i, core: (0, 0))] * 2,
            out_specs=pl.BlockSpec((sub, half), lambda i, core: (0, i)),
        ),
        out_shape=jax.ShapeDtypeStruct((sub, 2 * half), jnp.float32),
        compiler_params=PARAMS,
        cost_estimate=pl.CostEstimate(flops=0, bytes_accessed=2 * 2**20, transcendentals=0),
        name="join",
    )(core, own, other)


def swap(x):
    return lax.ppermute(x, "pair", [(0, 1), (1, 0)])


def shift(x, by):
    length = lax.axis_size("blk")
    return lax.ppermute(x, "blk", [(i, (i + by) % length) for i in range(length)])


def slot_of(distance):
    return distance + REACH - (distance > 0).astype(jnp.int32)


def per_device(features, subspace, offsets, counts):
    block = features.shape[0]
    core = lax.axis_index("pair").astype(jnp.int32)
    core_arg = core.reshape(1)
    here = jnp.concatenate([slot_of(offsets), counts], axis=1)
    there = swap(here)
    packed = pack(core_arg, features, subspace)
    up, down = [list(packed)], [list(packed)]
    for _ in range(REACH):
        up.append([shift(x, 1) for x in up[-1]])
        down.append([shift(x, -1) for x in down[-1]])
    near = up[3] + up[2] + up[1] + down[1] + down[2] + down[3]
    own_acc, own_deg, rows_t, row_norms = apply_self(core_arg, features, packed)
    table = jnp.stack([here[0, 0], there[0, 0], here[0, 1], there[0, 1], core])
    sums = {}
    for name, half in (("far", 1 - core), ("near", core)):
        scalars = jnp.concatenate([table, half.reshape(1)])
        sums[name] = apply_partners(scalars, rows_t, row_norms, own_acc, own_deg, near)
        if name == "far":
            far_acc, far_deg = [swap(x) for x in sums["far"]]
    field, gram = make_field(*sums["near"], far_acc, far_deg)
    other = swap(field)
    total = lax.psum(gram.reshape(-1), ("blk", "pair")).reshape(gram.shape)
    ritz_gram = total * (1.0 / float(lax.axis_size("blk") * block))
    return (join(core_arg, field, other), ritz_gram)


def solution(mesh):
    placed = (P("blk", None), P(None, "blk"), P("pair", "blk"), P("pair", "blk"))
    return jax.shard_map(
        per_device, mesh=mesh, in_specs=placed, out_specs=(P(None, "blk"), P()), check_vma=False
    )
```

time: 636 us -> 549 us (0.86); the launches traced: 626 us -> 548 us
  waiting for transfers between devices: 544 us -> 431 us
  starting transfers between devices: 22.7 us -> 71.3 us
  Pallas kernels: 0 us -> 18.7 us
  matrix products: 17.3 us -> 0 us
  other arithmetic: 9.52 us -> 1.55 us
    ppermute x6 -> x16, waiting for transfers between devices: 113 us -> 0.04 us  [the longest x12 0.03 us: shift(): lax.ppermute(x, 'blk', [(i, (i + by) % length) for i in range(length)])]
    ppermute x6 -> x16, starting transfers between devices: 22.6 us -> 71.3 us  [the longest x12 55.8 us: shift(): lax.ppermute(x, 'blk', [(i, (i + by) % length) for i in range(length)])]
    pallas_call x0 -> x6, Pallas kernels: none -> 18.7 us  [the longest x2 10.7 us: apply_partners(): pl.pallas_call(partner_kernel, grid_spec=pltpu.PrefetchScalarGridSpec(num...]
    dot_general x9 -> x0, matrix products: 17.3 us -> none  [the longest x4 11.7 us: kernel_apply(): jnp.dot(particles, columns.T, preferred_element_type=jnp.float32)]
    psum x2 -> x1, waiting for transfers between devices: 431 us -> 431 us  [per_device(): total = lax.psum(gram.reshape(-1), ('blk', 'pair')).reshape(gram.shape)]
  transfers between devices with their start and end apart: 8 -> 17, of which waited for: 5 -> 1; matrix products, arithmetic and copies ran while one was open for 1% -> 1% of each run, Pallas kernels for 0% -> 2%
where the time goes in v1:
time: 549 us; the launch traced here: 548 us
  waiting for transfers between devices  431 us (79%)
  starting transfers between devices  71.3 us (13%)
  Pallas kernels  18.7 us (3%)
  between operations  15.6 us (3%)
  local copies, waits for them, and re-layouts  9.69 us (2%)
    psum x1, waiting for transfers between devices, per_device(): total = lax.psum(gram.reshape(-1), ('blk', 'pair')).reshape(gram.shape)  431 us
    ppermute x12, starting transfers between devices, shift(): lax.ppermute(x, 'blk', [(i, (i + by) % length) for i in range(length)])  55.8 us
    ppermute x4, starting transfers between devices, swap(): return lax.ppermute(x, 'pair', [(0, 1), (1, 0)])  15.5 us
  transfers between devices with their start and end apart: 17, of which 1 were waited for; matrix products, arithmetic and copies ran while one was open for 1% of the time, Pallas kernels for 2%

profile of v1, /device:TPU:1, one launch (start us, length us, event | category | flops | bytes accessed | tf_op | source)
XLA Modules:
  0.0 548.4 jit_solution(12636434655607068109)
XLA Ops:
  9.5 16.6 %collective-permute-start.7 = (bf16[1024,128]{1,0:T(8,128)(2,1)S(1)}, bf16[1024,128]{1,0:T(8,128)(2,1)S(1)}, u32[]{:S(2)}, u32[]{:S(2)}) collective-permute-start(bf16[1024,128]{1,0:T(8,128)(2,1)S(1)} %get-tuple-element.14.refs_0_), channel_id=1, source_target_pairs={{0,510},{2,0},{4,2},{6,4},{8,6},{10,8},{12,10},{14,12},{16,14},{18... | collective-permute-start | bytes 786440 | tf_op jit(solution)/shard_map/ppermute | solution.py:261
  26.1 2.6 collective-permute-start.8
  28.8 2.6 collective-permute-start.1
  32.1 1.9 collective-permute-start.4
  34.8 8.8 %collective-permute-start.9 = (bf16[1024,128]{1,0:T(8,128)(2,1)S(1)}, bf16[1024,128]{1,0:T(8,128)(2,1)S(1)}, u32[]{:S(2)}, u32[]{:S(2)}) collective-permute-start(bf16[1024,128]{1,0:T(8,128)(2,1)S(1)} %collective-permute-done.7.refs_6_), channel_id=1, source_target_pairs={{0,510},{2,0},{4,2},{6,4},{8,6},{10,8},{12,10},{14,12},{16,14},{18... | collective-permute-start | bytes 786440 | tf_op jit(solution)/shard_map/ppermute | solution.py:261
  43.6 2.7 collective-permute-start.10
  46.3 2.6 collective-permute-start.2
  48.9 1.9 collective-permute-start.5
  52.1 8.8 %collective-permute-start.11 = (bf16[1024,128]{1,0:T(8,128)(2,1)S(1)}, bf16[1024,128]{1,0:T(8,128)(2,1)}, u32[]{:S(2)}, u32[]{:S(2)}) collective-permute-start(bf16[1024,128]{1,0:T(8,128)(2,1)S(1)} %collective-permute-done.9.refs_8_), channel_id=1, source_target_pairs={{0,510},{2,0},{4,2},{6,4},{8,6},{10,8},{12,10},{14,12},{16,14},{18... | collective-permute-start | bytes 786440 | tf_op jit(solution)/shard_map/ppermute | solution.py:261
  60.9 2.7 collective-permute-start.12
  63.6 2.6 collective-permute-start.3
  66.3 1.9 collective-permute-start.6
  68.3 5.7 %collective-permute-start = (s32[1,2]{1,0:T(1,128)S(1)}, s32[1,2]{1,0:T(1,128)S(1)}, u32[]{:S(2)}, u32[]{:S(2)}) collective-permute-start(s32[1,2]{1,0:T(1,128)S(1)} %pad_add_fusion), channel_id=1, source_target_pairs={{0,1},{1,0},{2,3},{3,2},{4,5},{5,4},{6,7},{7,6},{8,9},{9,8},{10,11... | collective-permute-start | bytes 32 | tf_op jit(solution)/shard_map/ppermute | solution.py:256
  76.9 4.7 own_block.1
  82.1 1.3 concatenate.13.scalars
  83.4 5.7 %partners.3 = (f32[128,1024]{1,0:T(8,128)}, f32[8,1024]{1,0:T(8,128)S(1)}) custom-call(s32[6]{0:T(128)S(1)} %concatenate.13.scalars, bf16[128,2048]{1,0:T(8,128)(2,1)S(1)} %get-tuple-element.16.rows_t, f32[1,2048]{1,0:T(1,128)S(1)} %get-tuple-element.17.row_norms, f32[128,2048]{1,0:T(8,128)S(1)} %get-tuple-element.18.own_acc, ...), custom_call_target="tpu_custom_call" | custom-call | flops 1073741824 | bytes 3145728 | tf_op jit(solution)/shard_map/partners/pallas_call | solution.py:170
  89.2 4.7 collective-permute-start.13
  93.9 1.3 concatenate.12.scalars
  95.2 1.9 collective-permute-start.14
  97.1 5.0 partners.2
  102.1 2.3 field.1
  104.4 3.2 collective-permute-start.15
  107.7 431.4 %all-reduce.2.cloned.1.call-done = f32[16384]{0:T(1024)} async-done(((f32[16384]{0:T(1024)}), f32[16384]{0:T(1024)}) %all-reduce.2.cloned.1.call-update) | async-done | bytes 65552 | tf_op jit(solution)/shard_map/psum | solution.py:290
  539.1 1.5 multiply_bitcast_fusion
  (36 shorter events, 8.4 us)
Async XLA Ops:
  7.2 531.9 %all-reduce.2.cloned.1.call-start = ((), (), s32[]{:S(2)}) async-start(), calls=%async_computation | async-start | bytes 131072 | tf_op jit(solution)/shard_map/psum | solution.py:290
  7.2 1.2 copy-start
  8.4 1.0 copy-start.1
  9.5 25.2 %collective-permute-start.7 = (bf16[1024,128]{1,0:T(8,128)(2,1)S(1)}, bf16[1024,128]{1,0:T(8,128)(2,1)S(1)}, u32[]{:S(2)}, u32[]{:S(2)}) collective-permute-start(bf16[1024,128]{1,0:T(8,128)(2,1)S(1)} %get-tuple-element.14.refs_0_), channel_id=1, source_target_pairs={{0,510},{2,0},{4,2},{6,4},{8,6},{10,8},{12,10},{14,12},{16,14},{18... | collective-permute-start | bytes 786440 | tf_op jit(solution)/shard_map/ppermute | solution.py:261
  26.1 17.4 %collective-permute-start.8 = (bf16[1024,128]{1,0:T(8,128)(2,1)S(1)}, bf16[1024,128]{1,0:T(8,128)(2,1)S(1)}, u32[]{:S(2)}, u32[]{:S(2)}) collective-permute-start(bf16[1024,128]{1,0:T(8,128)(2,1)S(1)} %get-tuple-element.15.refs_1_), channel_id=1, source_target_pairs={{0,510},{2,0},{4,2},{6,4},{8,6},{10,8},{12,10},{14,12},{16,14},{18... | collective-permute-start | bytes 786440 | tf_op jit(solution)/shard_map/ppermute | solution.py:261
  28.8 17.5 %collective-permute-start.1 = (bf16[1024,128]{1,0:T(8,128)(2,1)S(1)}, bf16[1024,128]{1,0:T(8,128)(2,1)S(1)}, u32[]{:S(2)}, u32[]{:S(2)}) collective-permute-start(bf16[1024,128]{1,0:T(8,128)(2,1)S(1)} %get-tuple-element.14.refs_0_), channel_id=1, source_target_pairs={{0,2},{2,4},{4,6},{6,8},{8,10},{10,12},{12,14},{14,16},{16,18},{18... | collective-permute-start | bytes 786440 | tf_op jit(solution)/shard_map/ppermute | solution.py:261
  31.4 0.7 copy-start.3
  32.1 16.7 %collective-permute-start.4 = (bf16[1024,128]{1,0:T(8,128)(2,1)S(1)}, bf16[1024,128]{1,0:T(8,128)(2,1)S(1)}, u32[]{:S(2)}, u32[]{:S(2)}) collective-permute-start(bf16[1024,128]{1,0:T(8,128)(2,1)S(1)} %get-tuple-element.15.refs_1_), channel_id=1, source_target_pairs={{0,2},{2,4},{4,6},{6,8},{8,10},{10,12},{12,14},{14,16},{16,18},{18... | collective-permute-start | bytes 786440 | tf_op jit(solution)/shard_map/ppermute | solution.py:261
  34.1 0.7 copy-start.5
  34.8 17.3 %collective-permute-start.9 = (bf16[1024,128]{1,0:T(8,128)(2,1)S(1)}, bf16[1024,128]{1,0:T(8,128)(2,1)S(1)}, u32[]{:S(2)}, u32[]{:S(2)}) collective-permute-start(bf16[1024,128]{1,0:T(8,128)(2,1)S(1)} %collective-permute-done.7.refs_6_), channel_id=1, source_target_pairs={{0,510},{2,0},{4,2},{6,4},{8,6},{10,8},{12,10},{14,12},{16,14},{18... | collective-permute-start | bytes 786440 | tf_op jit(solution)/shard_map/ppermute | solution.py:261
  43.6 17.4 %collective-permute-start.10 = (bf16[1024,128]{1,0:T(8,128)(2,1)S(1)}, bf16[1024,128]{1,0:T(8,128)(2,1)S(1)}, u32[]{:S(2)}, u32[]{:S(2)}) collective-permute-start(bf16[1024,128]{1,0:T(8,128)(2,1)S(1)} %collective-permute-done.8.refs_7_), channel_id=1, source_target_pairs={{0,510},{2,0},{4,2},{6,4},{8,6},{10,8},{12,10},{14,12},{16,14},{18... | collective-permute-start | bytes 786440 | tf_op jit(solution)/shard_map/ppermute | solution.py:261
  46.3 17.4 %collective-permute-start.2 = (bf16[1024,128]{1,0:T(8,128)(2,1)S(1)}, bf16[1024,128]{1,0:T(8,128)(2,1)S(1)}, u32[]{:S(2)}, u32[]{:S(2)}) collective-permute-start(bf16[1024,128]{1,0:T(8,128)(2,1)S(1)} %collective-permute-done.1.refs_4_), channel_id=1, source_target_pairs={{0,2},{2,4},{4,6},{6,8},{8,10},{10,12},{12,14},{14,16},{16,18},{18... | collective-permute-start | bytes 786440 | tf_op jit(solution)/shard_map/ppermute | solution.py:261
  48.9 17.4 %collective-permute-start.5 = (bf16[1024,128]{1,0:T(8,128)(2,1)S(1)}, bf16[1024,128]{1,0:T(8,128)(2,1)}, u32[]{:S(2)}, u32[]{:S(2)}) collective-permute-start(bf16[1024,128]{1,0:T(8,128)(2,1)S(1)} %collective-permute-done.4.refs_5_), channel_id=1, source_target_pairs={{0,2},{2,4},{4,6},{6,8},{8,10},{10,12},{12,14},{14,16},{16,18},{18... | collective-permute-start | bytes 786440 | tf_op jit(solution)/shard_map/ppermute | solution.py:261
  52.1 31.3 %collective-permute-start.11 = (bf16[1024,128]{1,0:T(8,128)(2,1)S(1)}, bf16[1024,128]{1,0:T(8,128)(2,1)}, u32[]{:S(2)}, u32[]{:S(2)}) collective-permute-start(bf16[1024,128]{1,0:T(8,128)(2,1)S(1)} %collective-permute-done.9.refs_8_), channel_id=1, source_target_pairs={{0,510},{2,0},{4,2},{6,4},{8,6},{10,8},{12,10},{14,12},{16,14},{18... | collective-permute-start | bytes 786440 | tf_op jit(solution)/shard_map/ppermute | solution.py:261
  60.9 22.5 %collective-permute-start.12 = (bf16[1024,128]{1,0:T(8,128)(2,1)S(1)}, bf16[1024,128]{1,0:T(8,128)(2,1)}, u32[]{:S(2)}, u32[]{:S(2)}) collective-permute-start(bf16[1024,128]{1,0:T(8,128)(2,1)S(1)} %collective-permute-done.10.refs_9_), channel_id=1, source_target_pairs={{0,510},{2,0},{4,2},{6,4},{8,6},{10,8},{12,10},{14,12},{16,14},{18... | collective-permute-start | bytes 786440 | tf_op jit(solution)/shard_map/ppermute | solution.py:261
  63.6 19.8 %collective-permute-start.3 = (bf16[1024,128]{1,0:T(8,128)(2,1)S(1)}, bf16[1024,128]{1,0:T(8,128)(2,1)}, u32[]{:S(2)}, u32[]{:S(2)}) collective-permute-start(bf16[1024,128]{1,0:T(8,128)(2,1)S(1)} %collective-permute-done.2.refs_2_), channel_id=1, source_target_pairs={{0,2},{2,4},{4,6},{6,8},{8,10},{10,12},{12,14},{14,16},{16,18},{18... | collective-permute-start | bytes 786440 | tf_op jit(solution)/shard_map/ppermute | solution.py:261
  66.3 17.2 %collective-permute-start.6 = (bf16[1024,128]{1,0:T(8,128)(2,1)}, bf16[1024,128]{1,0:T(8,128)(2,1)}, u32[]{:S(2)}, u32[]{:S(2)}) collective-permute-start(bf16[1024,128]{1,0:T(8,128)(2,1)} %collective-permute-done.5.refs_3_), channel_id=1, source_target_pairs={{0,2},{2,4},{4,6},{6,8},{8,10},{10,12},{12,14},{14,16},{16,18},{18... | collective-permute-start | bytes 786440 | tf_op jit(solution)/shard_map/ppermute | solution.py:261
  68.3 13.3 %collective-permute-start = (s32[1,2]{1,0:T(1,128)S(1)}, s32[1,2]{1,0:T(1,128)S(1)}, u32[]{:S(2)}, u32[]{:S(2)}) collective-permute-start(s32[1,2]{1,0:T(1,128)S(1)} %pad_add_fusion), channel_id=1, source_target_pairs={{0,1},{1,0},{2,3},{3,2},{4,5},{5,4},{6,7},{7,6},{8,9},{9,8},{10,11... | collective-permute-start | bytes 32 | tf_op jit(solution)/shard_map/ppermute | solution.py:256
  73.9 1.0 copy-start.2
  75.0 0.9 copy-start.4
  75.9 0.9 copy-start.6
  89.2 12.9 %collective-permute-start.13 = (f32[128,1024]{1,0:T(8,128)}, f32[128,1024]{1,0:T(8,128)}, u32[]{:S(2)}, u32[]{:S(2)}) collective-permute-start(f32[128,1024]{1,0:T(8,128)} %get-tuple-element.22), channel_id=1, source_target_pairs={{0,1},{1,0},{2,3},{3,2},{4,5},{5,4},{6,7},{7,6},{8,9},{9,8},{10,11... | collective-permute-start | bytes 1572872 | tf_op jit(solution)/shard_map/ppermute | solution.py:256
  95.2 6.9 %collective-permute-start.14 = (f32[8,1024]{1,0:T(8,128)S(1)}, f32[8,1024]{1,0:T(8,128)S(1)}, u32[]{:S(2)}, u32[]{:S(2)}) collective-permute-start(f32[8,1024]{1,0:T(8,128)S(1)} %get-tuple-element.23), channel_id=1, source_target_pairs={{0,1},{1,0},{2,3},{3,2},{4,5},{5,4},{6,7},{7,6},{8,9},{9,8},{10,11... | collective-permute-start | bytes 98312 | tf_op jit(solution)/shard_map/ppermute | solution.py:256
  104.4 436.2 %collective-permute-start.15 = (f32[128,1024]{1,0:T(8,128)S(1)}, f32[128,1024]{1,0:T(8,128)S(1)}, u32[]{:S(2)}, u32[]{:S(2)}) collective-permute-start(f32[128,1024]{1,0:T(8,128)S(1)} %get-tuple-element.24.own), channel_id=1, source_target_pairs={{0,1},{1,0},{2,3},{3,2},{4,5},{5,4},{6,7},{7,6},{8,9},{9,8},{10,11... | collective-permute-start | bytes 1572872 | tf_op jit(solution)/shard_map/ppermute | solution.py:256
Sparse Core Ops, SparseCore 0:
  107.8 431.2 all-reduce.1

commit v2 on v1

v2 whole, which is shorter than its diff:
```python
import functools

import jax
import jax.numpy as jnp
from jax import lax
from jax.experimental import pallas as pl
from jax.experimental.pallas import tpu as pltpu
from jax.sharding import PartitionSpec as P

REACH = 3
TILE = 256
FAR = 1e30
NT = (((1,), (1,)), ((), ()))
PARAMS = pltpu.CompilerParams(vmem_limit_bytes=32 * 2**20)


def pack_kernel(core_ref, feats_ref, field_ref, packed_ref, field_part, sems):
    half, feat = feats_ref.shape[0] // 2, feats_ref.shape[1]
    start = pl.multiple_of(core_ref[0] * half, half)
    feats_copy = pltpu.make_async_copy(
        feats_ref.at[pl.ds(start, half), :], packed_ref.at[pl.ds(0, half), :], sems.at[0]
    )
    field_copy = pltpu.make_async_copy(field_ref.at[:, pl.ds(start, half)], field_part, sems.at[1])
    feats_copy.start()
    field_copy.start()
    field_copy.wait()
    for at in range(0, half, feat):
        packed_ref[half + at : half + at + feat, :] = field_part[:, at : at + feat].astype(
            jnp.bfloat16
        )
    feats_copy.wait()


def pack(core, features, subspace):
    block, feat = features.shape
    sub = subspace.shape[0]
    return pl.pallas_call(
        pack_kernel,
        grid_spec=pltpu.PrefetchScalarGridSpec(
            num_scalar_prefetch=1,
            grid=(1,),
            in_specs=[pl.BlockSpec(memory_space=pltpu.HBM)] * 2,
            out_specs=pl.BlockSpec((block, feat), lambda i, core: (0, 0)),
            scratch_shapes=[
                pltpu.VMEM((sub, block // 2), jnp.float32),
                pltpu.SemaphoreType.DMA((2,)),
            ],
        ),
        out_shape=jax.ShapeDtypeStruct((block, feat), jnp.bfloat16),
        compiler_params=PARAMS,
        cost_estimate=pl.CostEstimate(flops=0, bytes_accessed=2 * 2**20, transcendentals=0),
        name="pack",
    )(core, features, subspace)


def norms_of(part):
    wide = part.astype(jnp.float32)
    return jnp.sum(wide * wide, axis=1, keepdims=True) * (1.0 / 256.0)


def add_columns(feats, vals, col_norms, rows_t, row_norms, sums, apart=None):
    sub = vals.shape[0]
    inner = jnp.dot(feats, rows_t, preferred_element_type=jnp.float32)
    weight = jnp.exp(inner - col_norms - row_norms)
    if apart is not None:
        weight = jnp.where(apart, weight, 0.0)
    sums[sub:, :] += jnp.sum(weight.reshape(TILE // 8, 8, weight.shape[1]), axis=0)
    sums[:sub, :] += jnp.dot(vals, weight.astype(jnp.bfloat16), preferred_element_type=jnp.float32)


def values_at(held, start):
    first = held[pl.ds(pl.multiple_of(start, 128), 128), :]
    second = held[pl.ds(pl.multiple_of(start + 128, 128), 128), :]
    return jnp.concatenate([first, second], axis=1)


def self_kernel(core_ref, feats_ref, packed, sums, rows_t, row_norms, feats, sem):
    block = feats_ref.shape[0]
    half = block // 2
    copy = pltpu.make_async_copy(feats_ref, feats, sem)
    copy.start()
    sums[...] = jnp.zeros_like(sums)
    copy.wait()
    for at in range(0, block, TILE):
        wide = feats[at : at + TILE, :].astype(jnp.float32).T
        row_norms[:, at : at + TILE] = jnp.sum(wide * wide, axis=0, keepdims=True) * (1.0 / 256.0)
        rows_t[:, at : at + TILE] = (wide * (1.0 / 128.0)).astype(jnp.bfloat16)

    @pl.loop(0, half // TILE)
    def _(step):
        at = pl.multiple_of(step * TILE, TILE)
        part = packed[pl.ds(at, TILE), :]
        col_ids = core_ref[0] * half + at + lax.broadcasted_iota(jnp.int32, (TILE, block), 0)
        row_ids = lax.broadcasted_iota(jnp.int32, (TILE, block), 1)
        add_columns(
            part,
            values_at(packed, half + at),
            norms_of(part),
            rows_t[...],
            row_norms[...],
            sums,
            col_ids != row_ids,
        )


def apply_self(core, features, packed):
    block, feat = features.shape
    outs = [
        jax.ShapeDtypeStruct((feat + 8, block), jnp.float32),
        jax.ShapeDtypeStruct((feat, block), jnp.bfloat16),
        jax.ShapeDtypeStruct((1, block), jnp.float32),
    ]
    whole = lambda i, core: (0, 0)
    return pl.pallas_call(
        self_kernel,
        grid_spec=pltpu.PrefetchScalarGridSpec(
            num_scalar_prefetch=1,
            grid=(1,),
            in_specs=[pl.BlockSpec(memory_space=pltpu.HBM), pl.BlockSpec(packed.shape, whole)],
            out_specs=[pl.BlockSpec(x.shape, whole) for x in outs],
            scratch_shapes=[pltpu.VMEM((block, feat), jnp.bfloat16), pltpu.SemaphoreType.DMA],
        ),
        out_shape=outs,
        compiler_params=PARAMS,
        cost_estimate=pl.CostEstimate(
            flops=2 * 2 * block * block // 2 * feat,
            bytes_accessed=4 * 2**20,
            transcendentals=block * block // 2,
        ),
        name="own_block",
    )(core, features, packed)


def partner_kernel(core_ref, here, there, rows_t, row_norms, own_sums, *refs):
    near = refs[: 2 * REACH]
    sums, held, sems = refs[2 * REACH :]
    half = held.shape[1] // 2
    picks = (here, there)
    for turn in range(2):
        for slot in range(2 * REACH):

            @pl.when(picks[turn][0, 0] == slot)
            def _():
                pltpu.make_async_copy(near[slot], held.at[turn], sems.at[turn]).start()

    sums[...] = own_sums[...]
    for turn in range(2):
        pltpu.make_async_copy(near[0], held.at[turn], sems.at[turn]).wait()

        @pl.loop(0, half // TILE)
        def _(step):
            at = pl.multiple_of(step * TILE, TILE)
            part = held[turn, pl.ds(at, TILE), :]
            ids = core_ref[0] * half + at + lax.broadcasted_iota(jnp.int32, (TILE, 1), 0)
            norms = jnp.where(ids < picks[turn][0, 1], norms_of(part), FAR)
            vals = values_at(held.at[turn], half + at)
            add_columns(part, vals, norms, rows_t[...], row_norms[...], sums)


def apply_partners(which, core, here, there, rows_t, row_norms, own_sums, near):
    feat, block = rows_t.shape
    half = block // 2
    if which == "far":
        picked = lambda i, core, here, there: (0, 1 - core[0])
    else:
        picked = lambda i, core, here, there: (0, core[0])
    out = jax.ShapeDtypeStruct((feat + 8, half), jnp.float32)
    return pl.pallas_call(
        partner_kernel,
        grid_spec=pltpu.PrefetchScalarGridSpec(
            num_scalar_prefetch=3,
            grid=(1,),
            in_specs=[
                pl.BlockSpec((feat, half), picked),
                pl.BlockSpec((1, half), picked),
                pl.BlockSpec((feat + 8, half), picked),
            ]
            + [pl.BlockSpec(memory_space=pl.ANY)] * len(near),
            out_specs=pl.BlockSpec(out.shape, lambda i, core, here, there: (0, 0)),
            scratch_shapes=[
                pltpu.VMEM((2, *near[0].shape), jnp.bfloat16),
                pltpu.SemaphoreType.DMA((2,)),
            ],
        ),
        out_shape=out,
        compiler_params=PARAMS,
        cost_estimate=pl.CostEstimate(
            flops=2 * 2 * half * block * feat,
            bytes_accessed=3 * 2**20,
            transcendentals=half * block,
        ),
        name="partners_" + which,
    )(core, here, there, rows_t, row_norms, own_sums, *near)


def field_kernel(scale, sums, far_sums, field, upper):
    sub = field.shape[0]
    mid, low = sub // 2, sub // 4
    degree = jnp.sum(sums[sub:, :] + far_sums[sub:, :], axis=0, keepdims=True)
    field[...] = (sums[:sub, :] + far_sums[:sub, :]) / degree
    gram = lax.dot_general(
        field[...],
        field[...],
        NT,
        precision=lax.Precision.HIGHEST,
        preferred_element_type=jnp.float32,
    )
    gram = gram * scale
    upper[:mid, :] = gram[:mid, :]
    upper[mid:, :] = jnp.concatenate([gram[mid : mid + low, mid:], gram[mid + low :, mid:]], axis=1)


def make_field(particles, sums, far_sums):
    sub, half = sums.shape[0] - 8, sums.shape[1]
    outs = [
        jax.ShapeDtypeStruct((sub, half), jnp.float32),
        jax.ShapeDtypeStruct((3 * sub // 4, sub), jnp.float32),
    ]
    return pl.pallas_call(
        functools.partial(field_kernel, 1.0 / particles),
        out_shape=outs,
        compiler_params=PARAMS,
        cost_estimate=pl.CostEstimate(
            flops=12 * sub * sub * half, bytes_accessed=2 * 2**20, transcendentals=0
        ),
        name="field",
    )(sums, far_sums)


def join_kernel(core_ref, own, other, upper, out, gram):
    sub = gram.shape[0]
    mid, low = sub // 2, sub // 4

    @pl.when(pl.program_id(0) == core_ref[0])
    def _():
        out[...] = own[...]

    @pl.when(pl.program_id(0) != core_ref[0])
    def _():
        out[...] = other[...]

    @pl.when(pl.program_id(0) == 0)
    def _():
        gram[:mid, :] = upper[:mid, :]
        last = jnp.concatenate([upper[mid:, :mid], upper[mid:, mid:]], axis=0)
        gram[mid:, :] = jnp.concatenate([upper[:mid, mid:].T, last], axis=1)


def join(core, own, other, upper):
    sub, half = own.shape
    outs = [
        jax.ShapeDtypeStruct((sub, 2 * half), jnp.float32),
        jax.ShapeDtypeStruct((sub, sub), jnp.float32),
    ]
    whole = lambda i, core: (0, 0)
    return pl.pallas_call(
        join_kernel,
        grid_spec=pltpu.PrefetchScalarGridSpec(
            num_scalar_prefetch=1,
            grid=(2,),
            in_specs=[pl.BlockSpec(x.shape, whole) for x in (own, other, upper)],
            out_specs=[
                pl.BlockSpec((sub, half), lambda i, core: (0, i)),
                pl.BlockSpec((sub, sub), whole),
            ],
        ),
        out_shape=outs,
        compiler_params=PARAMS,
        cost_estimate=pl.CostEstimate(flops=0, bytes_accessed=2 * 2**20, transcendentals=0),
        name="join",
    )(core, own, other, upper)


def swap(x):
    return lax.ppermute(x, "pair", [(0, 1), (1, 0)])


def shift(x, by):
    length = lax.axis_size("blk")
    return lax.ppermute(x, "blk", [(i, (i + by) % length) for i in range(length)])


def slot_of(distance):
    return distance + REACH - (distance > 0).astype(jnp.int32)


def per_device(features, subspace, offsets, counts):
    block = features.shape[0]
    core = lax.axis_index("pair").astype(jnp.int32).reshape(1)
    here = jnp.concatenate([slot_of(offsets), counts], axis=1)
    there = swap(here)
    packed = pack(core, features, subspace)
    up, down = [packed], [packed]
    for _ in range(REACH):
        up.append(shift(up[-1], 1))
        down.append(shift(down[-1], -1))
    near = [up[3], up[2], up[1], down[1], down[2], down[3]]
    own_sums, rows_t, row_norms = apply_self(core, features, packed)
    far = apply_partners("far", core, here, there, rows_t, row_norms, own_sums, near)
    far_sums = swap(far)
    sums = apply_partners("near", core, here, there, rows_t, row_norms, own_sums, near)
    field, upper = make_field(float(lax.axis_size("blk") * block), sums, far_sums)
    other = swap(field)
    return join(core, field, other, lax.psum(upper, ("blk", "pair")))


def solution(mesh):
    placed = (P("blk", None), P(None, "blk"), P("pair", "blk"), P("pair", "blk"))
    return jax.shard_map(
        per_device, mesh=mesh, in_specs=placed, out_specs=(P(None, "blk"), P()), check_vma=False
    )
```

time: 549 us -> 196 us (0.36)
  waiting for transfers between devices: 431 us -> 21.6 us
  blocking collectives: 0 us -> 99.1 us
  starting transfers between devices: 71.3 us -> 53.5 us
  between operations: 15.6 us -> 2.09 us
  local copies, waits for them, and re-layouts: 9.69 us -> 2.26 us
    psum x1 -> x0, waiting for transfers between devices: 431 us -> none  [per_device(): total = lax.psum(gram.reshape(-1), ('blk', 'pair')).reshape(gram.shape)]
    psum x0 -> x1, blocking collectives: none -> 99.1 us  [per_device(): return join(core, field, other, lax.psum(upper, ('blk', 'pair')))]
    ppermute x12 -> x6, waiting for transfers between devices: 0.03 us -> 21.6 us  [shift(): lax.ppermute(x, 'blk', [(i, (i + by) % length) for i in range(length)])]
    ppermute x12 -> x6, starting transfers between devices: 55.8 us -> 41.4 us  [shift(): lax.ppermute(x, 'blk', [(i, (i + by) % length) for i in range(length)])]
    ppermute x4 -> x3, starting transfers between devices: 15.5 us -> 12.1 us  [swap(): return lax.ppermute(x, 'pair', [(0, 1), (1, 0)])]
  transfers between devices with their start and end apart: 17 -> 9, of which waited for: 1 -> 3; matrix products, arithmetic and copies ran while one was open for 1% -> 0% of each run, Pallas kernels for 2% -> 5%
where the time goes in v2:
time: 196 us; the launch traced here: 195 us
  blocking collectives  99.1 us (51%)
  starting transfers between devices  53.5 us (27%)
  waiting for transfers between devices  21.6 us (11%)
  Pallas kernels  16.7 us (9%)
  local copies, waits for them, and re-layouts  2.26 us (1%)
  between operations  2.09 us (1%)
    psum x1, blocking collectives, per_device(): return join(core, field, other, lax.psum(upper, ('blk', 'pair')))  99.1 us
    ppermute x6, starting transfers between devices, shift(): lax.ppermute(x, 'blk', [(i, (i + by) % length) for i in range(length)])  41.4 us
    ppermute x6, waiting for transfers between devices, shift(): lax.ppermute(x, 'blk', [(i, (i + by) % length) for i in range(length)])  21.6 us
    ppermute x3, starting transfers between devices, swap(): return lax.ppermute(x, 'pair', [(0, 1), (1, 0)])  12.1 us
    pallas_call x2, Pallas kernels, apply_partners(): pl.pallas_call(partner_kernel, grid_spec=pltpu.PrefetchScalarGridSpec(num...  9.99 us
    pallas_call x1, Pallas kernels, apply_self(): pl.pallas_call(self_kernel, grid_spec=pltpu.PrefetchScalarGridSpec(num_sc...  4.76 us
  transfers between devices with their start and end apart: 9, of which 3 were waited for; matrix products, arithmetic and copies ran while one was open for 0% of the time, Pallas kernels for 5%

profile of v2, /device:TPU:1, one launch (start us, length us, event | category | flops | bytes accessed | tf_op | source)
XLA Modules:
  0.0 195.4 jit_solution(263913453085877500)
XLA Ops:
  0.6 1.2 copy-done
  1.9 1.0 copy-done.1
  2.9 0.1 pack.1.packed
  3.0 16.6 %collective-permute-start.4 = (bf16[2048,128]{1,0:T(8,128)(2,1)S(1)}, bf16[2048,128]{1,0:T(8,128)(2,1)S(1)}, u32[]{:S(2)}, u32[]{:S(2)}) collective-permute-start(bf16[2048,128]{1,0:T(8,128)(2,1)S(1)} %pack.1.packed), channel_id=1, source_target_pairs={{0,510},{2,0},{4,2},{6,4},{8,6},{10,8},{12,10},{14,12},{16,14},{18... | collective-permute-start | bytes 1572872 | tf_op jit(solution)/shard_map/ppermute | solution.py:280
  19.6 1.9 collective-permute-start.1
  21.5 8.6 %collective-permute-done.4.refs_3_ = bf16[2048,128]{1,0:T(8,128)(2,1)S(1)} collective-permute-done((bf16[2048,128]{1,0:T(8,128)(2,1)S(1)}, bf16[2048,128]{1,0:T(8,128)(2,1)S(1)}, u32[]{:S(2)}, u32[]{:S(2)}) %collective-permute-start.4) | collective-permute-done | bytes 524320 | tf_op jit(solution)/shard_map/ppermute | solution.py:280
  30.2 9.5 %collective-permute-start.5 = (bf16[2048,128]{1,0:T(8,128)(2,1)S(1)}, bf16[2048,128]{1,0:T(8,128)(2,1)S(1)}, u32[]{:S(2)}, u32[]{:S(2)}) collective-permute-start(bf16[2048,128]{1,0:T(8,128)(2,1)S(1)} %collective-permute-done.4.refs_3_), channel_id=1, source_target_pairs={{0,510},{2,0},{4,2},{6,4},{8,6},{10,8},{12,10},{14,12},{16,14},{18... | collective-permute-start | bytes 1572872 | tf_op jit(solution)/shard_map/ppermute | solution.py:280
  39.7 0.0 collective-permute-done.1.refs_2_
  39.7 1.9 collective-permute-start.2
  41.7 7.7 %collective-permute-done.5.refs_4_ = bf16[2048,128]{1,0:T(8,128)(2,1)S(1)} collective-permute-done((bf16[2048,128]{1,0:T(8,128)(2,1)S(1)}, bf16[2048,128]{1,0:T(8,128)(2,1)S(1)}, u32[]{:S(2)}, u32[]{:S(2)}) %collective-permute-start.5) | collective-permute-done | bytes 524320 | tf_op jit(solution)/shard_map/ppermute | solution.py:280
  49.4 9.5 %collective-permute-start.6 = (bf16[2048,128]{1,0:T(8,128)(2,1)S(1)}, bf16[2048,128]{1,0:T(8,128)(2,1)S(1)}, u32[]{:S(2)}, u32[]{:S(2)}) collective-permute-start(bf16[2048,128]{1,0:T(8,128)(2,1)S(1)} %collective-permute-done.5.refs_4_), channel_id=1, source_target_pairs={{0,510},{2,0},{4,2},{6,4},{8,6},{10,8},{12,10},{14,12},{16,14},{18... | collective-permute-start | bytes 1572872 | tf_op jit(solution)/shard_map/ppermute | solution.py:280
  58.9 1.9 collective-permute-start.3
  62.1 0.1 pad_add_fusion.here
  62.2 4.6 %collective-permute-start = (s32[1,2]{1,0:T(1,128)S(1)}, s32[1,2]{1,0:T(1,128)S(1)}, u32[]{:S(2)}, u32[]{:S(2)}) collective-permute-start(s32[1,2]{1,0:T(1,128)S(1)} %pad_add_fusion.here), channel_id=1, source_target_pairs={{0,1},{1,0},{2,3},{3,2},{4,5},{5,4},{6,7},{7,6},{8,9},{9,8},{10,11... | collective-permute-start | bytes 32 | tf_op jit(solution)/shard_map/ppermute | solution.py:275
  66.9 4.8 %own_block.1 = (f32[136,2048]{1,0:T(8,128)S(1)}, bf16[128,2048]{1,0:T(8,128)(2,1)S(1)}, f32[1,2048]{1,0:T(1,128)S(1)}) custom-call(s32[1]{0:T(128)} %bitcast.core_ref, bf16[2048,128]{1,0:T(8,128)(2,1)S(1)} %copy-done.1, bf16[2048,128]{1,0:T(8,128)(2,1)S(1)} %pack.1.packed), custom_call_target="tpu_custom_call" | custom-call | flops 1073741824 | bytes 4194304 | tf_op jit(solution)/shard_map/own_block/pallas_call | solution.py:114
  71.6 0.0 collective-permute-done.6.refs_5_
  71.7 5.2 %collective-permute-done.3.refs_0_ = bf16[2048,128]{1,0:T(8,128)(2,1)S(1)} collective-permute-done((bf16[2048,128]{1,0:T(8,128)(2,1)S(1)}, bf16[2048,128]{1,0:T(8,128)(2,1)S(1)}, u32[]{:S(2)}, u32[]{:S(2)}) %collective-permute-start.3) | collective-permute-done | bytes 524320 | tf_op jit(solution)/shard_map/ppermute | solution.py:280
  76.9 5.0 %partners_far.1 = f32[136,1024]{1,0:T(8,128)S(1)} custom-call(s32[1]{0:T(128)} %bitcast.core_ref, s32[1,2]{1,0:T(1,128)S(1)} %pad_add_fusion.here, s32[1,2]{1,0:T(1,128)S(1)} %collective-permute-done.there, bf16[128,2048]{1,0:T(8,128)(2,1)S(1)} %get-tuple-element.7.rows_t, f32[1,2048]{1,0:T(1,128)S(1)} %get-tuple-element.8.row_norms, ...), custom_call_target="tpu_custom_call" | custom-call | flops 1073741824 | bytes 3145728 | tf_op jit(solution)/shard_map/partners_far/pallas_call | solution.py:168
  81.9 5.6 %collective-permute-start.7 = (f32[136,1024]{1,0:T(8,128)S(1)}, f32[136,1024]{1,0:T(8,128)S(1)}, u32[]{:S(2)}, u32[]{:S(2)}) collective-permute-start(f32[136,1024]{1,0:T(8,128)S(1)} %partners_far.1), channel_id=1, source_target_pairs={{0,1},{1,0},{2,3},{3,2},{4,5},{5,4},{6,7},{7,6},{8,9},{9,8},{10,11... | collective-permute-start | bytes 1671176 | tf_op jit(solution)/shard_map/ppermute | solution.py:275
  87.5 5.0 %partners_near.1.sums = f32[136,1024]{1,0:T(8,128)S(1)} custom-call(s32[1]{0:T(128)} %bitcast.core_ref, s32[1,2]{1,0:T(1,128)S(1)} %pad_add_fusion.here, s32[1,2]{1,0:T(1,128)S(1)} %collective-permute-done.there, bf16[128,2048]{1,0:T(8,128)(2,1)S(1)} %get-tuple-element.7.rows_t, f32[1,2048]{1,0:T(1,128)S(1)} %get-tuple-element.8.row_norms, ...), custom_call_target="tpu_custom_call" | custom-call | flops 1073741824 | bytes 3145728 | tf_op jit(solution)/shard_map/partners_near/pallas_call | solution.py:168
  92.5 0.7 field.1
  93.2 1.9 collective-permute-start.8
  95.1 99.1 %psum.7.upper = f32[96,128]{1,0:T(8,128)S(1)} all-reduce(f32[96,128]{1,0:T(8,128)S(1)} %get-tuple-element.11), channel_id=1, replica_groups=mesh['blk'=256,'pair'=2] {'blk','pair'}, use_global_device_ids=true, to_apply=%region_0.0 | all-reduce | flops 12288 | bytes 98304 | tf_op jit(solution)/shard_map/psum | solution.py:304
  194.2 1.2 join.1
  (6 shorter events, 0.0 us)
Async XLA Ops:
  0.6 1.2 copy-start
  1.9 1.0 copy-start.1
  3.0 27.2 %collective-permute-start.4 = (bf16[2048,128]{1,0:T(8,128)(2,1)S(1)}, bf16[2048,128]{1,0:T(8,128)(2,1)S(1)}, u32[]{:S(2)}, u32[]{:S(2)}) collective-permute-start(bf16[2048,128]{1,0:T(8,128)(2,1)S(1)} %pack.1.packed), channel_id=1, source_target_pairs={{0,510},{2,0},{4,2},{6,4},{8,6},{10,8},{12,10},{14,12},{16,14},{18... | collective-permute-start | bytes 1572872 | tf_op jit(solution)/shard_map/ppermute | solution.py:280
  19.6 20.1 %collective-permute-start.1 = (bf16[2048,128]{1,0:T(8,128)(2,1)S(1)}, bf16[2048,128]{1,0:T(8,128)(2,1)S(1)}, u32[]{:S(2)}, u32[]{:S(2)}) collective-permute-start(bf16[2048,128]{1,0:T(8,128)(2,1)S(1)} %pack.1.packed), channel_id=1, source_target_pairs={{0,2},{2,4},{4,6},{6,8},{8,10},{10,12},{12,14},{14,16},{16,18},{18... | collective-permute-start | bytes 1572872 | tf_op jit(solution)/shard_map/ppermute | solution.py:280
  30.2 19.2 %collective-permute-start.5 = (bf16[2048,128]{1,0:T(8,128)(2,1)S(1)}, bf16[2048,128]{1,0:T(8,128)(2,1)S(1)}, u32[]{:S(2)}, u32[]{:S(2)}) collective-permute-start(bf16[2048,128]{1,0:T(8,128)(2,1)S(1)} %collective-permute-done.4.refs_3_), channel_id=1, source_target_pairs={{0,510},{2,0},{4,2},{6,4},{8,6},{10,8},{12,10},{14,12},{16,14},{18... | collective-permute-start | bytes 1572872 | tf_op jit(solution)/shard_map/ppermute | solution.py:280
  39.7 19.2 %collective-permute-start.2 = (bf16[2048,128]{1,0:T(8,128)(2,1)S(1)}, bf16[2048,128]{1,0:T(8,128)(2,1)S(1)}, u32[]{:S(2)}, u32[]{:S(2)}) collective-permute-start(bf16[2048,128]{1,0:T(8,128)(2,1)S(1)} %collective-permute-done.1.refs_2_), channel_id=1, source_target_pairs={{0,2},{2,4},{4,6},{6,8},{8,10},{10,12},{12,14},{14,16},{16,18},{18... | collective-permute-start | bytes 1572872 | tf_op jit(solution)/shard_map/ppermute | solution.py:280
  49.4 22.3 %collective-permute-start.6 = (bf16[2048,128]{1,0:T(8,128)(2,1)S(1)}, bf16[2048,128]{1,0:T(8,128)(2,1)S(1)}, u32[]{:S(2)}, u32[]{:S(2)}) collective-permute-start(bf16[2048,128]{1,0:T(8,128)(2,1)S(1)} %collective-permute-done.5.refs_4_), channel_id=1, source_target_pairs={{0,510},{2,0},{4,2},{6,4},{8,6},{10,8},{12,10},{14,12},{16,14},{18... | collective-permute-start | bytes 1572872 | tf_op jit(solution)/shard_map/ppermute | solution.py:280
  58.9 18.0 %collective-permute-start.3 = (bf16[2048,128]{1,0:T(8,128)(2,1)S(1)}, bf16[2048,128]{1,0:T(8,128)(2,1)S(1)}, u32[]{:S(2)}, u32[]{:S(2)}) collective-permute-start(bf16[2048,128]{1,0:T(8,128)(2,1)S(1)} %collective-permute-done.2.refs_1_), channel_id=1, source_target_pairs={{0,2},{2,4},{4,6},{6,8},{8,10},{10,12},{12,14},{14,16},{16,18},{18... | collective-permute-start | bytes 1572872 | tf_op jit(solution)/shard_map/ppermute | solution.py:280
  62.2 9.4 %collective-permute-start = (s32[1,2]{1,0:T(1,128)S(1)}, s32[1,2]{1,0:T(1,128)S(1)}, u32[]{:S(2)}, u32[]{:S(2)}) collective-permute-start(s32[1,2]{1,0:T(1,128)S(1)} %pad_add_fusion.here), channel_id=1, source_target_pairs={{0,1},{1,0},{2,3},{3,2},{4,5},{5,4},{6,7},{7,6},{8,9},{9,8},{10,11... | collective-permute-start | bytes 32 | tf_op jit(solution)/shard_map/ppermute | solution.py:275
  81.9 10.6 %collective-permute-start.7 = (f32[136,1024]{1,0:T(8,128)S(1)}, f32[136,1024]{1,0:T(8,128)S(1)}, u32[]{:S(2)}, u32[]{:S(2)}) collective-permute-start(f32[136,1024]{1,0:T(8,128)S(1)} %partners_far.1), channel_id=1, source_target_pairs={{0,1},{1,0},{2,3},{3,2},{4,5},{5,4},{6,7},{7,6},{8,9},{9,8},{10,11... | collective-permute-start | bytes 1671176 | tf_op jit(solution)/shard_map/ppermute | solution.py:275
  93.2 101.0 %collective-permute-start.8 = (f32[128,1024]{1,0:T(8,128)S(1)}, f32[128,1024]{1,0:T(8,128)S(1)}, u32[]{:S(2)}, u32[]{:S(2)}) collective-permute-start(f32[128,1024]{1,0:T(8,128)S(1)} %get-tuple-element.10.own), channel_id=1, source_target_pairs={{0,1},{1,0},{2,3},{3,2},{4,5},{5,4},{6,7},{7,6},{8,9},{9,8},{10,11... | collective-permute-start | bytes 1572872 | tf_op jit(solution)/shard_map/ppermute | solution.py:275

commit v3 on v2

--- a/solution.py
+++ b/solution.py
@@ -193,28 +193,25 @@
     )(core, here, there, rows_t, row_norms, own_sums, *near)
 
 
-def field_kernel(scale, sums, far_sums, field, upper):
+def field_kernel(scale, sums, far_sums, field, gram):
     sub = field.shape[0]
-    mid, low = sub // 2, sub // 4
     degree = jnp.sum(sums[sub:, :] + far_sums[sub:, :], axis=0, keepdims=True)
     field[...] = (sums[:sub, :] + far_sums[:sub, :]) / degree
-    gram = lax.dot_general(
+    terms = lax.dot_general(
         field[...],
         field[...],
         NT,
         precision=lax.Precision.HIGHEST,
         preferred_element_type=jnp.float32,
     )
-    gram = gram * scale
-    upper[:mid, :] = gram[:mid, :]
-    upper[mid:, :] = jnp.concatenate([gram[mid : mid + low, mid:], gram[mid + low :, mid:]], axis=1)
+    gram[...] = (terms * scale).reshape(gram.shape)
 
 
 def make_field(particles, sums, far_sums):
     sub, half = sums.shape[0] - 8, sums.shape[1]
     outs = [
         jax.ShapeDtypeStruct((sub, half), jnp.float32),
-        jax.ShapeDtypeStruct((3 * sub // 4, sub), jnp.float32),
+        jax.ShapeDtypeStruct((sub // 8, 8, sub), jnp.float32),
     ]
     return pl.pallas_call(
         functools.partial(field_kernel, 1.0 / particles),
@@ -227,10 +224,7 @@
     )(sums, far_sums)
 
 
-def join_kernel(core_ref, own, other, upper, out, gram):
-    sub = gram.shape[0]
-    mid, low = sub // 2, sub // 4
-
+def join_kernel(core_ref, own, other, out):
     @pl.when(pl.program_id(0) == core_ref[0])
     def _():
         out[...] = own[...]
@@ -239,36 +233,37 @@
     def _():
         out[...] = other[...]
 
-    @pl.when(pl.program_id(0) == 0)
-    def _():
-        gram[:mid, :] = upper[:mid, :]
-        last = jnp.concatenate([upper[mid:, :mid], upper[mid:, mid:]], axis=0)
-        gram[mid:, :] = jnp.concatenate([upper[:mid, mid:].T, last], axis=1)
-
-
-def join(core, own, other, upper):
+
+def join(core, own, other):
     sub, half = own.shape
-    outs = [
-        jax.ShapeDtypeStruct((sub, 2 * half), jnp.float32),
-        jax.ShapeDtypeStruct((sub, sub), jnp.float32),
-    ]
-    whole = lambda i, core: (0, 0)
     return pl.pallas_call(
         join_kernel,
         grid_spec=pltpu.PrefetchScalarGridSpec(
             num_scalar_prefetch=1,
             grid=(2,),
-            in_specs=[pl.BlockSpec(x.shape, whole) for x in (own, other, upper)],
-            out_specs=[
-                pl.BlockSpec((sub, half), lambda i, core: (0, i)),
-                pl.BlockSpec((sub, sub), whole),
-            ],
-        ),
-        out_shape=outs,
+            in_specs=[pl.BlockSpec((sub, half), lambda i, core: (0, 0))] * 2,
+            out_specs=pl.BlockSpec((sub, half), lambda i, core: (0, i)),
+        ),
+        out_shape=jax.ShapeDtypeStruct((sub, 2 * half), jnp.float32),
         compiler_params=PARAMS,
         cost_estimate=pl.CostEstimate(flops=0, bytes_accessed=2 * 2**20, transcendentals=0),
         name="join",
-    )(core, own, other, upper)
+    )(core, own, other)
+
+
+def exchange(tiles, groups):
+    return lax.all_to_all(tiles, "blk", 0, 0, axis_index_groups=groups, tiled=True)
+
+
+def sum_over_all(tiles):
+    count = tiles.shape[0]
+    blocks = lax.axis_size("blk")
+    near_z = [list(range(i, i + count)) for i in range(0, blocks, count)]
+    planes = [list(range(i, blocks, count)) for i in range(count)]
+    part = jnp.sum(exchange(tiles, planes), axis=0)
+    part = part + swap(part)
+    part = jnp.sum(exchange(jnp.broadcast_to(part, tiles.shape), near_z), axis=0)
+    return exchange(jnp.broadcast_to(part, tiles.shape), planes)
 
 
 def swap(x):
@@ -299,9 +294,10 @@
     far = apply_partners("far", core, here, there, rows_t, row_norms, own_sums, near)
     far_sums = swap(far)
     sums = apply_partners("near", core, here, there, rows_t, row_norms, own_sums, near)
-    field, upper = make_field(float(lax.axis_size("blk") * block), sums, far_sums)
+    field, tiles = make_field(float(lax.axis_size("blk") * block), sums, far_sums)
     other = swap(field)
-    return join(core, field, other, lax.psum(upper, ("blk", "pair")))
+    sub = field.shape[0]
+    return (join(core, field, other), sum_over_all(tiles).reshape(sub, sub))
 
 
 def solution(mesh):

time: 196 us -> 136 us (0.69)
  blocking collectives: 99.1 us -> 32.7 us
  starting transfers between devices: 53.5 us -> 57.1 us
    psum x1 -> x0, blocking collectives: 99.1 us -> none  [per_device(): return join(core, field, other, lax.psum(upper, ('blk', 'pair')))]
    all_to_all x0 -> x3, blocking collectives: none -> 32.7 us  [exchange(): lax.all_to_all(tiles, 'blk', 0, 0, axis_index_groups=groups, tiled=True)]
    ppermute x3 -> x4, starting transfers between devices: 12.1 us -> 15.7 us  [swap(): return lax.ppermute(x, 'pair', [(0, 1), (1, 0)])]
  transfers between devices with their start and end apart: 9 -> 10, of which waited for: 3 -> 4; matrix products, arithmetic and copies ran while one was open for 0% -> 0% of each run, Pallas kernels for 5% -> 7%
where the time goes in v3:
time: 136 us; the launch traced here: 134 us
  starting transfers between devices  57.1 us (42%)
  blocking collectives  32.7 us (24%)
  waiting for transfers between devices  22.4 us (16%)
  Pallas kernels  16.5 us (12%)
  local copies, waits for them, and re-layouts  2.91 us (2%)
  between operations  2.11 us (2%)
    ppermute x6, starting transfers between devices, shift(): lax.ppermute(x, 'blk', [(i, (i + by) % length) for i in range(length)])  41.4 us
    all_to_all x3, blocking collectives, exchange(): lax.all_to_all(tiles, 'blk', 0, 0, axis_index_groups=groups, tiled=True)  32.7 us
    ppermute x6, waiting for transfers between devices, shift(): lax.ppermute(x, 'blk', [(i, (i + by) % length) for i in range(length)])  21.6 us
    ppermute x4, starting transfers between devices, swap(): return lax.ppermute(x, 'pair', [(0, 1), (1, 0)])  15.7 us
    pallas_call x2, Pallas kernels, apply_partners(): pl.pallas_call(partner_kernel, grid_spec=pltpu.PrefetchScalarGridSpec(num...  9.99 us
    pallas_call x1, Pallas kernels, apply_self(): pl.pallas_call(self_kernel, grid_spec=pltpu.PrefetchScalarGridSpec(num_sc...  4.76 us
    unnamed x5, local copies, waits for them, and re-layouts  2.89 us
  transfers between devices with their start and end apart: 10, of which 4 were waited for; matrix products, arithmetic and copies ran while one was open for 0% of the time, Pallas kernels for 7%

profile of v3, /device:TPU:1, one launch (start us, length us, event | category | flops | bytes accessed | tf_op | source)
XLA Modules:
  0.0 133.9 jit_solution(13224119543292573878)
XLA Ops:
  0.6 1.2 copy-done
  1.9 1.0 copy-done.1
  3.0 16.6 %collective-permute-start.4 = (bf16[2048,128]{1,0:T(8,128)(2,1)S(1)}, bf16[2048,128]{1,0:T(8,128)(2,1)S(1)}, u32[]{:S(2)}, u32[]{:S(2)}) collective-permute-start(bf16[2048,128]{1,0:T(8,128)(2,1)S(1)} %pack.1.packed), channel_id=1, source_target_pairs={{0,510},{2,0},{4,2},{6,4},{8,6},{10,8},{12,10},{14,12},{16,14},{18... | collective-permute-start | bytes 1572872 | tf_op jit(solution)/shard_map/ppermute | solution.py:275
  19.6 1.9 %collective-permute-start.1 = (bf16[2048,128]{1,0:T(8,128)(2,1)S(1)}, bf16[2048,128]{1,0:T(8,128)(2,1)S(1)}, u32[]{:S(2)}, u32[]{:S(2)}) collective-permute-start(bf16[2048,128]{1,0:T(8,128)(2,1)S(1)} %pack.1.packed), channel_id=1, source_target_pairs={{0,2},{2,4},{4,6},{6,8},{8,10},{10,12},{12,14},{14,16},{16,18},{18... | collective-permute-start | bytes 1572872 | tf_op jit(solution)/shard_map/ppermute | solution.py:275
  21.5 8.6 %collective-permute-done.4.refs_3_ = bf16[2048,128]{1,0:T(8,128)(2,1)S(1)} collective-permute-done((bf16[2048,128]{1,0:T(8,128)(2,1)S(1)}, bf16[2048,128]{1,0:T(8,128)(2,1)S(1)}, u32[]{:S(2)}, u32[]{:S(2)}) %collective-permute-start.4) | collective-permute-done | bytes 524320 | tf_op jit(solution)/shard_map/ppermute | solution.py:275
  30.2 9.5 %collective-permute-start.5 = (bf16[2048,128]{1,0:T(8,128)(2,1)S(1)}, bf16[2048,128]{1,0:T(8,128)(2,1)S(1)}, u32[]{:S(2)}, u32[]{:S(2)}) collective-permute-start(bf16[2048,128]{1,0:T(8,128)(2,1)S(1)} %collective-permute-done.4.refs_3_), channel_id=1, source_target_pairs={{0,510},{2,0},{4,2},{6,4},{8,6},{10,8},{12,10},{14,12},{16,14},{18... | collective-permute-start | bytes 1572872 | tf_op jit(solution)/shard_map/ppermute | solution.py:275
  39.7 1.9 %collective-permute-start.2 = (bf16[2048,128]{1,0:T(8,128)(2,1)S(1)}, bf16[2048,128]{1,0:T(8,128)(2,1)S(1)}, u32[]{:S(2)}, u32[]{:S(2)}) collective-permute-start(bf16[2048,128]{1,0:T(8,128)(2,1)S(1)} %collective-permute-done.1.refs_2_), channel_id=1, source_target_pairs={{0,2},{2,4},{4,6},{6,8},{8,10},{10,12},{12,14},{14,16},{16,18},{18... | collective-permute-start | bytes 1572872 | tf_op jit(solution)/shard_map/ppermute | solution.py:275
  41.7 7.7 %collective-permute-done.5.refs_4_ = bf16[2048,128]{1,0:T(8,128)(2,1)S(1)} collective-permute-done((bf16[2048,128]{1,0:T(8,128)(2,1)S(1)}, bf16[2048,128]{1,0:T(8,128)(2,1)S(1)}, u32[]{:S(2)}, u32[]{:S(2)}) %collective-permute-start.5) | collective-permute-done | bytes 524320 | tf_op jit(solution)/shard_map/ppermute | solution.py:275
  49.4 9.5 %collective-permute-start.6 = (bf16[2048,128]{1,0:T(8,128)(2,1)S(1)}, bf16[2048,128]{1,0:T(8,128)(2,1)S(1)}, u32[]{:S(2)}, u32[]{:S(2)}) collective-permute-start(bf16[2048,128]{1,0:T(8,128)(2,1)S(1)} %collective-permute-done.5.refs_4_), channel_id=1, source_target_pairs={{0,510},{2,0},{4,2},{6,4},{8,6},{10,8},{12,10},{14,12},{16,14},{18... | collective-permute-start | bytes 1572872 | tf_op jit(solution)/shard_map/ppermute | solution.py:275
  58.9 1.9 %collective-permute-start.3 = (bf16[2048,128]{1,0:T(8,128)(2,1)S(1)}, bf16[2048,128]{1,0:T(8,128)(2,1)S(1)}, u32[]{:S(2)}, u32[]{:S(2)}) collective-permute-start(bf16[2048,128]{1,0:T(8,128)(2,1)S(1)} %collective-permute-done.2.refs_1_), channel_id=1, source_target_pairs={{0,2},{2,4},{4,6},{6,8},{8,10},{10,12},{12,14},{14,16},{16,18},{18... | collective-permute-start | bytes 1572872 | tf_op jit(solution)/shard_map/ppermute | solution.py:275
  62.2 4.6 %collective-permute-start = (s32[1,2]{1,0:T(1,128)S(1)}, s32[1,2]{1,0:T(1,128)S(1)}, u32[]{:S(2)}, u32[]{:S(2)}) collective-permute-start(s32[1,2]{1,0:T(1,128)S(1)} %pad_add_fusion.here), channel_id=1, source_target_pairs={{0,1},{1,0},{2,3},{3,2},{4,5},{5,4},{6,7},{7,6},{8,9},{9,8},{10,11... | collective-permute-start | bytes 32 | tf_op jit(solution)/shard_map/ppermute | solution.py:270
  66.9 4.8 %own_block.1 = (f32[136,2048]{1,0:T(8,128)S(1)}, bf16[128,2048]{1,0:T(8,128)(2,1)S(1)}, f32[1,2048]{1,0:T(1,128)S(1)}) custom-call(s32[1]{0:T(128)} %bitcast.core_ref, bf16[2048,128]{1,0:T(8,128)(2,1)S(1)} %copy-done.1, bf16[2048,128]{1,0:T(8,128)(2,1)S(1)} %pack.1.packed), custom_call_target="tpu_custom_call" | custom-call | flops 1073741824 | bytes 4194304 | tf_op jit(solution)/shard_map/own_block/pallas_call | solution.py:114
  71.7 5.2 %collective-permute-done.3.refs_0_ = bf16[2048,128]{1,0:T(8,128)(2,1)S(1)} collective-permute-done((bf16[2048,128]{1,0:T(8,128)(2,1)S(1)}, bf16[2048,128]{1,0:T(8,128)(2,1)S(1)}, u32[]{:S(2)}, u32[]{:S(2)}) %collective-permute-start.3) | collective-permute-done | bytes 524320 | tf_op jit(solution)/shard_map/ppermute | solution.py:275
  76.9 5.0 %partners_far.1 = f32[136,1024]{1,0:T(8,128)S(1)} custom-call(s32[1]{0:T(128)} %bitcast.core_ref, s32[1,2]{1,0:T(1,128)S(1)} %pad_add_fusion.here, s32[1,2]{1,0:T(1,128)S(1)} %collective-permute-done.there, bf16[128,2048]{1,0:T(8,128)(2,1)S(1)} %get-tuple-element.7.rows_t, f32[1,2048]{1,0:T(1,128)S(1)} %get-tuple-element.8.row_norms, ...), custom_call_target="tpu_custom_call" | custom-call | flops 1073741824 | bytes 3145728 | tf_op jit(solution)/shard_map/partners_far/pallas_call | solution.py:168
  81.9 5.6 %collective-permute-start.7 = (f32[136,1024]{1,0:T(8,128)S(1)}, f32[136,1024]{1,0:T(8,128)S(1)}, u32[]{:S(2)}, u32[]{:S(2)}) collective-permute-start(f32[136,1024]{1,0:T(8,128)S(1)} %partners_far.1), channel_id=1, source_target_pairs={{0,1},{1,0},{2,3},{3,2},{4,5},{5,4},{6,7},{7,6},{8,9},{9,8},{10,11... | collective-permute-start | bytes 1671176 | tf_op jit(solution)/shard_map/ppermute | solution.py:270
  87.5 5.0 %partners_near.1.sums = f32[136,1024]{1,0:T(8,128)S(1)} custom-call(s32[1]{0:T(128)} %bitcast.core_ref, s32[1,2]{1,0:T(1,128)S(1)} %pad_add_fusion.here, s32[1,2]{1,0:T(1,128)S(1)} %collective-permute-done.there, bf16[128,2048]{1,0:T(8,128)(2,1)S(1)} %get-tuple-element.7.rows_t, f32[1,2048]{1,0:T(1,128)S(1)} %get-tuple-element.8.row_norms, ...), custom_call_target="tpu_custom_call" | custom-call | flops 1073741824 | bytes 3145728 | tf_op jit(solution)/shard_map/partners_near/pallas_call | solution.py:168
  92.5 0.6 field.1
  93.1 1.9 %collective-permute-start.8 = (f32[128,1024]{1,0:T(8,128)S(1)}, f32[128,1024]{1,0:T(8,128)S(1)}, u32[]{:S(2)}, u32[]{:S(2)}) collective-permute-start(f32[128,1024]{1,0:T(8,128)S(1)} %get-tuple-element.10.own), channel_id=1, source_target_pairs={{0,1},{1,0},{2,3},{3,2},{4,5},{5,4},{6,7},{7,6},{8,9},{9,8},{10,11... | collective-permute-start | bytes 1572872 | tf_op jit(solution)/shard_map/ppermute | solution.py:270
  95.1 9.1 %all_to_all.15 = f32[16,8,128]{2,1,0:T(8,128)S(1)} all-to-all(f32[16,8,128]{2,1,0:T(8,128)S(1)} %get-tuple-element.11), channel_id=1, replica_groups={{0,32,64,96,128,160,192,224,256,288,320,352,384,416,448,480},{2,34,66,9..., dimensions={0} | all-to-all | bytes 131072 | tf_op jit(solution)/shard_map/all_to_all | solution.py:255
  104.2 3.6 %collective-permute-start.9 = (f32[8,128]{1,0:T(8,128)S(1)}, f32[8,128]{1,0:T(8,128)S(1)}, u32[]{:S(2)}, u32[]{:S(2)}) collective-permute-start(f32[8,128]{1,0:T(8,128)S(1)} %reduce_sum.18), channel_id=1, source_target_pairs={{0,1},{1,0},{2,3},{3,2},{4,5},{5,4},{6,7},{7,6},{8,9},{9,8},{10,11... | collective-permute-start | bytes 12296 | tf_op jit(solution)/shard_map/ppermute | solution.py:270
  107.7 0.8 collective-permute-done.9
  108.5 14.3 %all_to_all.16 = f32[16,8,128]{2,1,0:T(8,128)S(1)} all-to-all(f32[16,8,128]{2,1,0:T(8,128)S(1)} %broadcast_in_dim.6), channel_id=1, replica_groups={{0,2,4,6,8,10,12,14,16,18,20,22,24,26,28,30},{32,34,36,38,40,42,44,46,4..., dimensions={0} | all-to-all | bytes 131072 | tf_op jit(solution)/shard_map/all_to_all | solution.py:255
  122.8 9.4 %all_to_all.17 = f32[16,8,128]{2,1,0:T(8,128)S(1)} all-to-all(f32[16,8,128]{2,1,0:T(8,128)S(1)} %broadcast_in_dim.7), channel_id=1, replica_groups={{0,32,64,96,128,160,192,224,256,288,320,352,384,416,448,480},{2,34,66,9..., dimensions={0} | all-to-all | bytes 131072 | tf_op jit(solution)/shard_map/all_to_all | solution.py:255
  132.2 1.0 join.1
  (16 shorter events, 0.9 us)
Async XLA Ops:
  0.6 1.2 copy-start
  1.9 1.0 copy-start.1
  3.0 27.2 %collective-permute-start.4 = (bf16[2048,128]{1,0:T(8,128)(2,1)S(1)}, bf16[2048,128]{1,0:T(8,128)(2,1)S(1)}, u32[]{:S(2)}, u32[]{:S(2)}) collective-permute-start(bf16[2048,128]{1,0:T(8,128)(2,1)S(1)} %pack.1.packed), channel_id=1, source_target_pairs={{0,510},{2,0},{4,2},{6,4},{8,6},{10,8},{12,10},{14,12},{16,14},{18... | collective-permute-start | bytes 1572872 | tf_op jit(solution)/shard_map/ppermute | solution.py:275
  19.6 20.1 %collective-permute-start.1 = (bf16[2048,128]{1,0:T(8,128)(2,1)S(1)}, bf16[2048,128]{1,0:T(8,128)(2,1)S(1)}, u32[]{:S(2)}, u32[]{:S(2)}) collective-permute-start(bf16[2048,128]{1,0:T(8,128)(2,1)S(1)} %pack.1.packed), channel_id=1, source_target_pairs={{0,2},{2,4},{4,6},{6,8},{8,10},{10,12},{12,14},{14,16},{16,18},{18... | collective-permute-start | bytes 1572872 | tf_op jit(solution)/shard_map/ppermute | solution.py:275
  30.2 19.2 %collective-permute-start.5 = (bf16[2048,128]{1,0:T(8,128)(2,1)S(1)}, bf16[2048,128]{1,0:T(8,128)(2,1)S(1)}, u32[]{:S(2)}, u32[]{:S(2)}) collective-permute-start(bf16[2048,128]{1,0:T(8,128)(2,1)S(1)} %collective-permute-done.4.refs_3_), channel_id=1, source_target_pairs={{0,510},{2,0},{4,2},{6,4},{8,6},{10,8},{12,10},{14,12},{16,14},{18... | collective-permute-start | bytes 1572872 | tf_op jit(solution)/shard_map/ppermute | solution.py:275
  39.7 19.2 %collective-permute-start.2 = (bf16[2048,128]{1,0:T(8,128)(2,1)S(1)}, bf16[2048,128]{1,0:T(8,128)(2,1)S(1)}, u32[]{:S(2)}, u32[]{:S(2)}) collective-permute-start(bf16[2048,128]{1,0:T(8,128)(2,1)S(1)} %collective-permute-done.1.refs_2_), channel_id=1, source_target_pairs={{0,2},{2,4},{4,6},{6,8},{8,10},{10,12},{12,14},{14,16},{16,18},{18... | collective-permute-start | bytes 1572872 | tf_op jit(solution)/shard_map/ppermute | solution.py:275
  49.4 22.3 %collective-permute-start.6 = (bf16[2048,128]{1,0:T(8,128)(2,1)S(1)}, bf16[2048,128]{1,0:T(8,128)(2,1)S(1)}, u32[]{:S(2)}, u32[]{:S(2)}) collective-permute-start(bf16[2048,128]{1,0:T(8,128)(2,1)S(1)} %collective-permute-done.5.refs_4_), channel_id=1, source_target_pairs={{0,510},{2,0},{4,2},{6,4},{8,6},{10,8},{12,10},{14,12},{16,14},{18... | collective-permute-start | bytes 1572872 | tf_op jit(solution)/shard_map/ppermute | solution.py:275
  58.9 18.0 %collective-permute-start.3 = (bf16[2048,128]{1,0:T(8,128)(2,1)S(1)}, bf16[2048,128]{1,0:T(8,128)(2,1)S(1)}, u32[]{:S(2)}, u32[]{:S(2)}) collective-permute-start(bf16[2048,128]{1,0:T(8,128)(2,1)S(1)} %collective-permute-done.2.refs_1_), channel_id=1, source_target_pairs={{0,2},{2,4},{4,6},{6,8},{8,10},{10,12},{12,14},{14,16},{16,18},{18... | collective-permute-start | bytes 1572872 | tf_op jit(solution)/shard_map/ppermute | solution.py:275
  62.2 9.4 %collective-permute-start = (s32[1,2]{1,0:T(1,128)S(1)}, s32[1,2]{1,0:T(1,128)S(1)}, u32[]{:S(2)}, u32[]{:S(2)}) collective-permute-start(s32[1,2]{1,0:T(1,128)S(1)} %pad_add_fusion.here), channel_id=1, source_target_pairs={{0,1},{1,0},{2,3},{3,2},{4,5},{5,4},{6,7},{7,6},{8,9},{9,8},{10,11... | collective-permute-start | bytes 32 | tf_op jit(solution)/shard_map/ppermute | solution.py:270
  81.9 10.6 %collective-permute-start.7 = (f32[136,1024]{1,0:T(8,128)S(1)}, f32[136,1024]{1,0:T(8,128)S(1)}, u32[]{:S(2)}, u32[]{:S(2)}) collective-permute-start(f32[136,1024]{1,0:T(8,128)S(1)} %partners_far.1), channel_id=1, source_target_pairs={{0,1},{1,0},{2,3},{3,2},{4,5},{5,4},{6,7},{7,6},{8,9},{9,8},{10,11... | collective-permute-start | bytes 1671176 | tf_op jit(solution)/shard_map/ppermute | solution.py:270
  93.1 39.1 %collective-permute-start.8 = (f32[128,1024]{1,0:T(8,128)S(1)}, f32[128,1024]{1,0:T(8,128)S(1)}, u32[]{:S(2)}, u32[]{:S(2)}) collective-permute-start(f32[128,1024]{1,0:T(8,128)S(1)} %get-tuple-element.10.own), channel_id=1, source_target_pairs={{0,1},{1,0},{2,3},{3,2},{4,5},{5,4},{6,7},{7,6},{8,9},{9,8},{10,11... | collective-permute-start | bytes 1572872 | tf_op jit(solution)/shard_map/ppermute | solution.py:270
  104.2 4.4 %collective-permute-start.9 = (f32[8,128]{1,0:T(8,128)S(1)}, f32[8,128]{1,0:T(8,128)S(1)}, u32[]{:S(2)}, u32[]{:S(2)}) collective-permute-start(f32[8,128]{1,0:T(8,128)S(1)} %reduce_sum.18), channel_id=1, source_target_pairs={{0,1},{1,0},{2,3},{3,2},{4,5},{5,4},{6,7},{7,6},{8,9},{9,8},{10,11... | collective-permute-start | bytes 12296 | tf_op jit(solution)/shard_map/ppermute | solution.py:270

commit v4 on v3

--- a/solution.py
+++ b/solution.py
@@ -8,45 +8,40 @@
 from jax.sharding import PartitionSpec as P
 
 REACH = 3
+SIDE = 4
+LENGTH = 16
 TILE = 256
 FAR = 1e30
 NT = (((1,), (1,)), ((), ()))
 PARAMS = pltpu.CompilerParams(vmem_limit_bytes=32 * 2**20)
 
 
-def pack_kernel(core_ref, feats_ref, field_ref, packed_ref, field_part, sems):
+def pack_kernel(core_ref, feats_ref, field_ref, give, keep):
     half, feat = feats_ref.shape[0] // 2, feats_ref.shape[1]
-    start = pl.multiple_of(core_ref[0] * half, half)
-    feats_copy = pltpu.make_async_copy(
-        feats_ref.at[pl.ds(start, half), :], packed_ref.at[pl.ds(0, half), :], sems.at[0]
-    )
-    field_copy = pltpu.make_async_copy(field_ref.at[:, pl.ds(start, half)], field_part, sems.at[1])
-    feats_copy.start()
-    field_copy.start()
-    field_copy.wait()
-    for at in range(0, half, feat):
-        packed_ref[half + at : half + at + feat, :] = field_part[:, at : at + feat].astype(
-            jnp.bfloat16
-        )
-    feats_copy.wait()
+    for core in range(2):
+
+        @pl.when(core_ref[0] == core)
+        def _():
+            for packed, start in ((give, (1 - core) * half), (keep, core * half)):
+                packed[:half, :] = feats_ref[start : start + half, :]
+                for at in range(0, half, feat):
+                    packed[half + at : half + at + feat, :] = field_ref[
+                        :, start + at : start + at + feat
+                    ].astype(jnp.bfloat16)
 
 
 def pack(core, features, subspace):
-    block, feat = features.shape
-    sub = subspace.shape[0]
+    out = jax.ShapeDtypeStruct(features.shape, jnp.bfloat16)
+    whole = lambda i, core: (0, 0)
     return pl.pallas_call(
         pack_kernel,
         grid_spec=pltpu.PrefetchScalarGridSpec(
             num_scalar_prefetch=1,
             grid=(1,),
-            in_specs=[pl.BlockSpec(memory_space=pltpu.HBM)] * 2,
-            out_specs=pl.BlockSpec((block, feat), lambda i, core: (0, 0)),
-            scratch_shapes=[
-                pltpu.VMEM((sub, block // 2), jnp.float32),
-                pltpu.SemaphoreType.DMA((2,)),
-            ],
-        ),
-        out_shape=jax.ShapeDtypeStruct((block, feat), jnp.bfloat16),
+            in_specs=[pl.BlockSpec(x.shape, whole) for x in (features, subspace)],
+            out_specs=[pl.BlockSpec(out.shape, whole)] * 2,
+        ),
+        out_shape=[out, out],
         compiler_params=PARAMS,
         cost_estimate=pl.CostEstimate(flops=0, bytes_accessed=2 * 2**20, transcendentals=0),
         name="pack",
@@ -137,9 +132,12 @@
     half = held.shape[1] // 2
     picks = (here, there)
     for turn in range(2):
+        distance = picks[turn][0, 0]
+        same_way = (distance < 0) == (core_ref[0] == 0)
+        chosen = jnp.abs(distance) - 1 + jnp.where(same_way, 0, REACH)
         for slot in range(2 * REACH):
 
-            @pl.when(picks[turn][0, 0] == slot)
+            @pl.when(chosen == slot)
             def _():
                 pltpu.make_async_copy(near[slot], held.at[turn], sems.at[turn]).start()
 
@@ -147,7 +145,7 @@
     for turn in range(2):
         pltpu.make_async_copy(near[0], held.at[turn], sems.at[turn]).wait()
 
-        @pl.loop(0, half // TILE)
+        @pl.loop(0, half // TILE, unroll=True)
         def _(step):
             at = pl.multiple_of(step * TILE, TILE)
             part = held[turn, pl.ds(at, TILE), :]
@@ -204,14 +202,14 @@
         precision=lax.Precision.HIGHEST,
         preferred_element_type=jnp.float32,
     )
-    gram[...] = (terms * scale).reshape(gram.shape)
+    gram[...] = terms * scale
 
 
 def make_field(particles, sums, far_sums):
     sub, half = sums.shape[0] - 8, sums.shape[1]
     outs = [
         jax.ShapeDtypeStruct((sub, half), jnp.float32),
-        jax.ShapeDtypeStruct((sub // 8, 8, sub), jnp.float32),
+        jax.ShapeDtypeStruct((sub, sub), jnp.float32),
     ]
     return pl.pallas_call(
         functools.partial(field_kernel, 1.0 / particles),
@@ -251,53 +249,66 @@
     )(core, own, other)
 
 
-def exchange(tiles, groups):
-    return lax.all_to_all(tiles, "blk", 0, 0, axis_index_groups=groups, tiled=True)
-
-
-def sum_over_all(tiles):
-    count = tiles.shape[0]
+def exchange(pieces, stride):
+    count = pieces.shape[0]
     blocks = lax.axis_size("blk")
-    near_z = [list(range(i, i + count)) for i in range(0, blocks, count)]
-    planes = [list(range(i, blocks, count)) for i in range(count)]
-    part = jnp.sum(exchange(tiles, planes), axis=0)
+    groups = [
+        list(range(start, start + count * stride, stride))
+        for start in range(blocks)
+        if start // stride % count == 0
+    ]
+    return lax.all_to_all(pieces, "blk", 0, 0, axis_index_groups=groups, tiled=True)
+
+
+def repeat(piece):
+    return jnp.broadcast_to(piece, (SIDE, *piece.shape))
+
+
+def sum_over_all(gram):
+    size = gram.shape[0]
+    part = gram.reshape(SIDE, size // SIDE, size)
+    part = jnp.sum(exchange(part, LENGTH), axis=0)
+    part = part.reshape(SIDE, size // SIDE // SIDE, size)
+    part = jnp.sum(exchange(part, LENGTH * SIDE), axis=0)
     part = part + swap(part)
-    part = jnp.sum(exchange(jnp.broadcast_to(part, tiles.shape), near_z), axis=0)
-    return exchange(jnp.broadcast_to(part, tiles.shape), planes)
+    part = jnp.sum(exchange(repeat(part), 1), axis=0)
+    part = jnp.sum(exchange(repeat(part), SIDE), axis=0)
+    part = exchange(repeat(part), LENGTH * SIDE).reshape(size // SIDE, size)
+    return exchange(repeat(part), LENGTH).reshape(size, size)
 
 
 def swap(x):
     return lax.ppermute(x, "pair", [(0, 1), (1, 0)])
 
 
-def shift(x, by):
-    length = lax.axis_size("blk")
-    return lax.ppermute(x, "blk", [(i, (i + by) % length) for i in range(length)])
-
-
-def slot_of(distance):
-    return distance + REACH - (distance > 0).astype(jnp.int32)
+def relay(x):
+    blocks = lax.axis_size("blk")
+    pairs = []
+    for i in range(blocks):
+        pairs.append((2 * i, (i + 1) % blocks * 2))
+        pairs.append((2 * i + 1, (i - 1) % blocks * 2 + 1))
+    return lax.ppermute(x, ("blk", "pair"), pairs)
 
 
 def per_device(features, subspace, offsets, counts):
     block = features.shape[0]
     core = lax.axis_index("pair").astype(jnp.int32).reshape(1)
-    here = jnp.concatenate([slot_of(offsets), counts], axis=1)
+    here = jnp.concatenate([offsets, counts], axis=1)
     there = swap(here)
-    packed = pack(core, features, subspace)
-    up, down = [packed], [packed]
+    give, keep = pack(core, features, subspace)
+    own_sums, rows_t, row_norms = apply_self(core, features, keep)
+    kept, swapped = [], []
     for _ in range(REACH):
-        up.append(shift(up[-1], 1))
-        down.append(shift(down[-1], -1))
-    near = [up[3], up[2], up[1], down[1], down[2], down[3]]
-    own_sums, rows_t, row_norms = apply_self(core, features, packed)
+        give, keep = relay(give), relay(keep)
+        kept.append(keep)
+        swapped.append(swap(give))
+    near = kept + swapped
     far = apply_partners("far", core, here, there, rows_t, row_norms, own_sums, near)
     far_sums = swap(far)
     sums = apply_partners("near", core, here, there, rows_t, row_norms, own_sums, near)
-    field, tiles = make_field(float(lax.axis_size("blk") * block), sums, far_sums)
+    field, gram = make_field(float(lax.axis_size("blk") * block), sums, far_sums)
     other = swap(field)
-    sub = field.shape[0]
-    return (join(core, field, other), sum_over_all(tiles).reshape(sub, sub))
+    return (join(core, field, other), sum_over_all(gram))
 
 
 def solution(mesh):

time: 136 us -> 144 us (1.059)
  the two profiles are of different devices: /device:TPU:1 before, /device:TPU:2 now
where the time goes in v4:
time: 144 us
  blocking collectives  67.2 us (47%)
  starting transfers between devices  31 us (22%)
  waiting for transfers between devices  25.5 us (18%)
  Pallas kernels  14.6 us (10%)
  local copies, waits for them, and re-layouts  2.91 us (2%)
  between operations  2.15 us (1%)
    all_to_all x6, blocking collectives, exchange(): lax.all_to_all(pieces, 'blk', 0, 0, axis_index_groups=groups, tiled=True)  67.2 us
    ppermute x6, waiting for transfers between devices, relay(): return lax.ppermute(x, ('blk', 'pair'), pairs)  24.3 us
    ppermute x7, starting transfers between devices, swap(): return lax.ppermute(x, 'pair', [(0, 1), (1, 0)])  15.7 us
    ppermute x6, starting transfers between devices, relay(): return lax.ppermute(x, ('blk', 'pair'), pairs)  15.3 us
    pallas_call x2, Pallas kernels, apply_partners(): pl.pallas_call(partner_kernel, grid_spec=pltpu.PrefetchScalarGridSpec(num...  8.1 us
    pallas_call x1, Pallas kernels, apply_self(): pl.pallas_call(self_kernel, grid_spec=pltpu.PrefetchScalarGridSpec(num_sc...  4.76 us
    unnamed x5, local copies, waits for them, and re-layouts  2.89 us
  transfers between devices with their start and end apart: 13, of which 5 were waited for; matrix products, arithmetic and copies ran while one was open for 0% of the time, Pallas kernels for 6%

profile of v4, /device:TPU:2, one launch (start us, length us, event | category | flops | bytes accessed | tf_op | source)
XLA Modules:
  0.0 143.5 jit_solution(12082991594087392051)
XLA Ops:
  3.0 3.8 %collective-permute-start.4 = (bf16[2048,128]{1,0:T(8,128)(2,1)S(1)}, bf16[2048,128]{1,0:T(8,128)(2,1)S(1)}, u32[]{:S(2)}, u32[]{:S(2)}) collective-permute-start(bf16[2048,128]{1,0:T(8,128)(2,1)S(1)} %get-tuple-element.13), channel_id=1, source_target_pairs={{0,2},{1,511},{2,4},{3,1},{4,6},{5,3},{6,8},{7,5},{8,10},{9,7},{10... | collective-permute-start | bytes 1572872 | tf_op jit(solution)/shard_map/ppermute | solution.py:290
  6.8 3.8 %collective-permute-start.1 = (bf16[2048,128]{1,0:T(8,128)(2,1)S(1)}, bf16[2048,128]{1,0:T(8,128)(2,1)S(1)}, u32[]{:S(2)}, u32[]{:S(2)}) collective-permute-start(bf16[2048,128]{1,0:T(8,128)(2,1)S(1)} %get-tuple-element.9.packed), channel_id=1, source_target_pairs={{0,2},{1,511},{2,4},{3,1},{4,6},{5,3},{6,8},{7,5},{8,10},{9,7},{10... | collective-permute-start | bytes 1572872 | tf_op jit(solution)/shard_map/ppermute | solution.py:290
  10.7 10.9 %collective-permute-done.4 = bf16[2048,128]{1,0:T(8,128)(2,1)S(1)} collective-permute-done((bf16[2048,128]{1,0:T(8,128)(2,1)S(1)}, bf16[2048,128]{1,0:T(8,128)(2,1)S(1)}, u32[]{:S(2)}, u32[]{:S(2)}) %collective-permute-start.4) | collective-permute-done | bytes 524320 | tf_op jit(solution)/shard_map/ppermute | solution.py:290
  21.5 1.9 %collective-permute-start.6 = (bf16[2048,128]{1,0:T(8,128)(2,1)S(1)}, bf16[2048,128]{1,0:T(8,128)(2,1)S(1)}, u32[]{:S(2)}, u32[]{:S(2)}) collective-permute-start(bf16[2048,128]{1,0:T(8,128)(2,1)S(1)} %collective-permute-done.4), channel_id=1, source_target_pairs={{0,2},{1,511},{2,4},{3,1},{4,6},{5,3},{6,8},{7,5},{8,10},{9,7},{10... | collective-permute-start | bytes 1572872 | tf_op jit(solution)/shard_map/ppermute | solution.py:290
  23.4 3.7 %collective-permute-done.1.refs_0_ = bf16[2048,128]{1,0:T(8,128)(2,1)S(1)} collective-permute-done((bf16[2048,128]{1,0:T(8,128)(2,1)S(1)}, bf16[2048,128]{1,0:T(8,128)(2,1)S(1)}, u32[]{:S(2)}, u32[]{:S(2)}) %collective-permute-start.1) | collective-permute-done | bytes 524320 | tf_op jit(solution)/shard_map/ppermute | solution.py:290
  27.1 1.9 %collective-permute-start.2 = (bf16[2048,128]{1,0:T(8,128)(2,1)S(1)}, bf16[2048,128]{1,0:T(8,128)(2,1)S(1)}, u32[]{:S(2)}, u32[]{:S(2)}) collective-permute-start(bf16[2048,128]{1,0:T(8,128)(2,1)S(1)} %collective-permute-done.1.refs_0_), channel_id=1, source_target_pairs={{0,2},{1,511},{2,4},{3,1},{4,6},{5,3},{6,8},{7,5},{8,10},{9,7},{10... | collective-permute-start | bytes 1572872 | tf_op jit(solution)/shard_map/ppermute | solution.py:290
  29.1 5.6 %collective-permute-done.6 = bf16[2048,128]{1,0:T(8,128)(2,1)S(1)} collective-permute-done((bf16[2048,128]{1,0:T(8,128)(2,1)S(1)}, bf16[2048,128]{1,0:T(8,128)(2,1)S(1)}, u32[]{:S(2)}, u32[]{:S(2)}) %collective-permute-start.6) | collective-permute-done | bytes 524320 | tf_op jit(solution)/shard_map/ppermute | solution.py:290
  34.7 1.9 %collective-permute-start.8 = (bf16[2048,128]{1,0:T(8,128)(2,1)S(1)}, bf16[2048,128]{1,0:T(8,128)(2,1)S(1)}, u32[]{:S(2)}, u32[]{:S(2)}) collective-permute-start(bf16[2048,128]{1,0:T(8,128)(2,1)S(1)} %collective-permute-done.6), channel_id=1, source_target_pairs={{0,2},{1,511},{2,4},{3,1},{4,6},{5,3},{6,8},{7,5},{8,10},{9,7},{10... | collective-permute-start | bytes 1572872 | tf_op jit(solution)/shard_map/ppermute | solution.py:290
  36.6 3.3 %collective-permute-start.5 = (bf16[2048,128]{1,0:T(8,128)(2,1)S(1)}, bf16[2048,128]{1,0:T(8,128)(2,1)S(1)}, u32[]{:S(2)}, u32[]{:S(2)}) collective-permute-start(bf16[2048,128]{1,0:T(8,128)(2,1)S(1)} %collective-permute-done.4), channel_id=1, source_target_pairs={{0,1},{1,0},{2,3},{3,2},{4,5},{5,4},{6,7},{7,6},{8,9},{9,8},{10,11... | collective-permute-start | bytes 1572872 | tf_op jit(solution)/shard_map/ppermute | solution.py:281
  39.9 1.9 %collective-permute-start.7 = (bf16[2048,128]{1,0:T(8,128)(2,1)S(1)}, bf16[2048,128]{1,0:T(8,128)(2,1)S(1)}, u32[]{:S(2)}, u32[]{:S(2)}) collective-permute-start(bf16[2048,128]{1,0:T(8,128)(2,1)S(1)} %collective-permute-done.6), channel_id=1, source_target_pairs={{0,1},{1,0},{2,3},{3,2},{4,5},{5,4},{6,7},{7,6},{8,9},{9,8},{10,11... | collective-permute-start | bytes 1572872 | tf_op jit(solution)/shard_map/ppermute | solution.py:281
  41.8 1.9 %collective-permute-start.3 = (bf16[2048,128]{1,0:T(8,128)(2,1)S(1)}, bf16[2048,128]{1,0:T(8,128)(2,1)S(1)}, u32[]{:S(2)}, u32[]{:S(2)}) collective-permute-start(bf16[2048,128]{1,0:T(8,128)(2,1)S(1)} %collective-permute-done.2.refs_1_), channel_id=1, source_target_pairs={{0,2},{1,511},{2,4},{3,1},{4,6},{5,3},{6,8},{7,5},{8,10},{9,7},{10... | collective-permute-start | bytes 1572872 | tf_op jit(solution)/shard_map/ppermute | solution.py:290
  43.8 4.1 %collective-permute-done.8 = bf16[2048,128]{1,0:T(8,128)(2,1)S(1)} collective-permute-done((bf16[2048,128]{1,0:T(8,128)(2,1)S(1)}, bf16[2048,128]{1,0:T(8,128)(2,1)S(1)}, u32[]{:S(2)}, u32[]{:S(2)}) %collective-permute-start.8) | collective-permute-done | bytes 524320 | tf_op jit(solution)/shard_map/ppermute | solution.py:290
  51.2 2.4 %collective-permute-start = (s32[1,2]{1,0:T(1,128)S(1)}, s32[1,2]{1,0:T(1,128)S(1)}, u32[]{:S(2)}, u32[]{:S(2)}) collective-permute-start(s32[1,2]{1,0:T(1,128)S(1)} %pad_add_fusion.here), channel_id=1, source_target_pairs={{0,1},{1,0},{2,3},{3,2},{4,5},{5,4},{6,7},{7,6},{8,9},{9,8},{10,11... | collective-permute-start | bytes 32 | tf_op jit(solution)/shard_map/ppermute | solution.py:281
  53.6 4.8 %own_block.1 = (f32[136,2048]{1,0:T(8,128)S(1)}, bf16[128,2048]{1,0:T(8,128)(2,1)S(1)}, f32[1,2048]{1,0:T(1,128)S(1)}) custom-call(s32[1]{0:T(128)} %bitcast.core_ref, bf16[2048,128]{1,0:T(8,128)(2,1)S(1)} %copy-done.1, bf16[2048,128]{1,0:T(8,128)(2,1)S(1)} %get-tuple-element.9.packed), custom_call_target="tpu_custom_call" | custom-call | flops 1073741824 | bytes 4194304 | tf_op jit(solution)/shard_map/own_block/pallas_call | solution.py:109
  58.4 4.1 %partners_far.1 = f32[136,1024]{1,0:T(8,128)S(1)} custom-call(s32[1]{0:T(128)} %bitcast.core_ref, s32[1,2]{1,0:T(1,128)S(1)} %pad_add_fusion.here, s32[1,2]{1,0:T(1,128)S(1)} %collective-permute-done.there, bf16[128,2048]{1,0:T(8,128)(2,1)S(1)} %get-tuple-element.10.rows_t, f32[1,2048]{1,0:T(1,128)S(1)} %get-tuple-element.11.row_norms, ...), custom_call_target="tpu_custom_call" | custom-call | flops 1073741824 | bytes 3145728 | tf_op jit(solution)/shard_map/partners_far/pallas_call | solution.py:166
  62.5 1.9 %collective-permute-start.10 = (f32[136,1024]{1,0:T(8,128)S(1)}, f32[136,1024]{1,0:T(8,128)S(1)}, u32[]{:S(2)}, u32[]{:S(2)}) collective-permute-start(f32[136,1024]{1,0:T(8,128)S(1)} %partners_far.1), channel_id=1, source_target_pairs={{0,1},{1,0},{2,3},{3,2},{4,5},{5,4},{6,7},{7,6},{8,9},{9,8},{10,11... | collective-permute-start | bytes 1671176 | tf_op jit(solution)/shard_map/ppermute | solution.py:281
  64.4 4.0 %partners_near.1.sums = f32[136,1024]{1,0:T(8,128)S(1)} custom-call(s32[1]{0:T(128)} %bitcast.core_ref, s32[1,2]{1,0:T(1,128)S(1)} %pad_add_fusion.here, s32[1,2]{1,0:T(1,128)S(1)} %collective-permute-done.there, bf16[128,2048]{1,0:T(8,128)(2,1)S(1)} %get-tuple-element.10.rows_t, f32[1,2048]{1,0:T(1,128)S(1)} %get-tuple-element.11.row_norms, ...), custom_call_target="tpu_custom_call" | custom-call | flops 1073741824 | bytes 3145728 | tf_op jit(solution)/shard_map/partners_near/pallas_call | solution.py:166
  69.1 2.4 %collective-permute-start.11 = (f32[128,1024]{1,0:T(8,128)S(1)}, f32[128,1024]{1,0:T(8,128)S(1)}, u32[]{:S(2)}, u32[]{:S(2)}) collective-permute-start(f32[128,1024]{1,0:T(8,128)S(1)} %get-tuple-element.14.own), channel_id=1, source_target_pairs={{0,1},{1,0},{2,3},{3,2},{4,5},{5,4},{6,7},{7,6},{8,9},{9,8},{10,11... | collective-permute-start | bytes 1572872 | tf_op jit(solution)/shard_map/ppermute | solution.py:281
  71.5 18.4 %all_to_all.30 = f32[4,32,128]{2,1,0:T(8,128)S(1)} all-to-all(f32[4,32,128]{2,1,0:T(8,128)S(1)} %bitcast.5), channel_id=1, replica_groups={{0,32,64,96},{2,34,66,98},{4,36,68,100},{6,38,70,102},{8,40,72,104},{10..., dimensions={0} | all-to-all | bytes 131072 | tf_op jit(solution)/shard_map/all_to_all | solution.py:260
  89.9 7.7 %all_to_all.31 = f32[4,8,128]{2,1,0:T(8,128)S(1)} all-to-all(f32[4,8,128]{2,1,0:T(8,128)S(1)} %bitcast.7), channel_id=1, replica_groups={{0,128,256,384},{2,130,258,386},{4,132,260,388},{6,134,262,390},{8,136,..., dimensions={0} | all-to-all | bytes 32768 | tf_op jit(solution)/shard_map/all_to_all | solution.py:260
  100.7 8.0 %all_to_all.32 = f32[4,8,128]{2,1,0:T(8,128)S(1)} all-to-all(f32[4,8,128]{2,1,0:T(8,128)S(1)} %broadcast_in_dim.12), channel_id=1, replica_groups={{0,2,4,6},{8,10,12,14},{16,18,20,22},{24,26,28,30},{32,34,36,38},{40,42..., dimensions={0} | all-to-all | bytes 32768 | tf_op jit(solution)/shard_map/all_to_all | solution.py:260
  108.6 17.5 %all_to_all.33 = f32[4,8,128]{2,1,0:T(8,128)S(1)} all-to-all(f32[4,8,128]{2,1,0:T(8,128)S(1)} %broadcast_in_dim.13), channel_id=1, replica_groups={{0,8,16,24},{2,10,18,26},{4,12,20,28},{6,14,22,30},{32,40,48,56},{34,42..., dimensions={0} | all-to-all | bytes 32768 | tf_op jit(solution)/shard_map/all_to_all | solution.py:260
  126.2 7.7 %all_to_all.34 = f32[4,8,128]{2,1,0:T(8,128)S(1)} all-to-all(f32[4,8,128]{2,1,0:T(8,128)S(1)} %broadcast_in_dim.14), channel_id=1, replica_groups={{0,128,256,384},{2,130,258,386},{4,132,260,388},{6,134,262,390},{8,136,..., dimensions={0} | all-to-all | bytes 32768 | tf_op jit(solution)/shard_map/all_to_all | solution.py:260
  133.9 8.0 %all_to_all.35 = f32[4,32,128]{2,1,0:T(8,128)S(1)} all-to-all(f32[4,32,128]{2,1,0:T(8,128)S(1)} %broadcast_in_dim.15), channel_id=1, replica_groups={{0,32,64,96},{2,34,66,98},{4,36,68,100},{6,38,70,102},{8,40,72,104},{10..., dimensions={0} | all-to-all | bytes 131072 | tf_op jit(solution)/shard_map/all_to_all | solution.py:260
  (29 shorter events, 9.7 us)
Async XLA Ops:
  0.6 1.2 copy-start
  1.9 1.0 copy-start.1
  3.0 18.5 %collective-permute-start.4 = (bf16[2048,128]{1,0:T(8,128)(2,1)S(1)}, bf16[2048,128]{1,0:T(8,128)(2,1)S(1)}, u32[]{:S(2)}, u32[]{:S(2)}) collective-permute-start(bf16[2048,128]{1,0:T(8,128)(2,1)S(1)} %get-tuple-element.13), channel_id=1, source_target_pairs={{0,2},{1,511},{2,4},{3,1},{4,6},{5,3},{6,8},{7,5},{8,10},{9,7},{10... | collective-permute-start | bytes 1572872 | tf_op jit(solution)/shard_map/ppermute | solution.py:290
  6.8 20.3 %collective-permute-start.1 = (bf16[2048,128]{1,0:T(8,128)(2,1)S(1)}, bf16[2048,128]{1,0:T(8,128)(2,1)S(1)}, u32[]{:S(2)}, u32[]{:S(2)}) collective-permute-start(bf16[2048,128]{1,0:T(8,128)(2,1)S(1)} %get-tuple-element.9.packed), channel_id=1, source_target_pairs={{0,2},{1,511},{2,4},{3,1},{4,6},{5,3},{6,8},{7,5},{8,10},{9,7},{10... | collective-permute-start | bytes 1572872 | tf_op jit(solution)/shard_map/ppermute | solution.py:290
  21.5 13.2 %collective-permute-start.6 = (bf16[2048,128]{1,0:T(8,128)(2,1)S(1)}, bf16[2048,128]{1,0:T(8,128)(2,1)S(1)}, u32[]{:S(2)}, u32[]{:S(2)}) collective-permute-start(bf16[2048,128]{1,0:T(8,128)(2,1)S(1)} %collective-permute-done.4), channel_id=1, source_target_pairs={{0,2},{1,511},{2,4},{3,1},{4,6},{5,3},{6,8},{7,5},{8,10},{9,7},{10... | collective-permute-start | bytes 1572872 | tf_op jit(solution)/shard_map/ppermute | solution.py:290
  27.1 14.7 %collective-permute-start.2 = (bf16[2048,128]{1,0:T(8,128)(2,1)S(1)}, bf16[2048,128]{1,0:T(8,128)(2,1)S(1)}, u32[]{:S(2)}, u32[]{:S(2)}) collective-permute-start(bf16[2048,128]{1,0:T(8,128)(2,1)S(1)} %collective-permute-done.1.refs_0_), channel_id=1, source_target_pairs={{0,2},{1,511},{2,4},{3,1},{4,6},{5,3},{6,8},{7,5},{8,10},{9,7},{10... | collective-permute-start | bytes 1572872 | tf_op jit(solution)/shard_map/ppermute | solution.py:290
  34.7 13.2 %collective-permute-start.8 = (bf16[2048,128]{1,0:T(8,128)(2,1)S(1)}, bf16[2048,128]{1,0:T(8,128)(2,1)S(1)}, u32[]{:S(2)}, u32[]{:S(2)}) collective-permute-start(bf16[2048,128]{1,0:T(8,128)(2,1)S(1)} %collective-permute-done.6), channel_id=1, source_target_pairs={{0,2},{1,511},{2,4},{3,1},{4,6},{5,3},{6,8},{7,5},{8,10},{9,7},{10... | collective-permute-start | bytes 1572872 | tf_op jit(solution)/shard_map/ppermute | solution.py:290
  36.6 21.7 %collective-permute-start.5 = (bf16[2048,128]{1,0:T(8,128)(2,1)S(1)}, bf16[2048,128]{1,0:T(8,128)(2,1)S(1)}, u32[]{:S(2)}, u32[]{:S(2)}) collective-permute-start(bf16[2048,128]{1,0:T(8,128)(2,1)S(1)} %collective-permute-done.4), channel_id=1, source_target_pairs={{0,1},{1,0},{2,3},{3,2},{4,5},{5,4},{6,7},{7,6},{8,9},{9,8},{10,11... | collective-permute-start | bytes 1572872 | tf_op jit(solution)/shard_map/ppermute | solution.py:281
  39.9 18.5 %collective-permute-start.7 = (bf16[2048,128]{1,0:T(8,128)(2,1)S(1)}, bf16[2048,128]{1,0:T(8,128)(2,1)S(1)}, u32[]{:S(2)}, u32[]{:S(2)}) collective-permute-start(bf16[2048,128]{1,0:T(8,128)(2,1)S(1)} %collective-permute-done.6), channel_id=1, source_target_pairs={{0,1},{1,0},{2,3},{3,2},{4,5},{5,4},{6,7},{7,6},{8,9},{9,8},{10,11... | collective-permute-start | bytes 1572872 | tf_op jit(solution)/shard_map/ppermute | solution.py:281
  41.8 16.5 %collective-permute-start.3 = (bf16[2048,128]{1,0:T(8,128)(2,1)S(1)}, bf16[2048,128]{1,0:T(8,128)(2,1)S(1)}, u32[]{:S(2)}, u32[]{:S(2)}) collective-permute-start(bf16[2048,128]{1,0:T(8,128)(2,1)S(1)} %collective-permute-done.2.refs_1_), channel_id=1, source_target_pairs={{0,2},{1,511},{2,4},{3,1},{4,6},{5,3},{6,8},{7,5},{8,10},{9,7},{10... | collective-permute-start | bytes 1572872 | tf_op jit(solution)/shard_map/ppermute | solution.py:290
  47.9 10.5 %collective-permute-start.9 = (bf16[2048,128]{1,0:T(8,128)(2,1)S(1)}, bf16[2048,128]{1,0:T(8,128)(2,1)S(1)}, u32[]{:S(2)}, u32[]{:S(2)}) collective-permute-start(bf16[2048,128]{1,0:T(8,128)(2,1)S(1)} %collective-permute-done.8), channel_id=1, source_target_pairs={{0,1},{1,0},{2,3},{3,2},{4,5},{5,4},{6,7},{7,6},{8,9},{9,8},{10,11... | collective-permute-start | bytes 1572872 | tf_op jit(solution)/shard_map/ppermute | solution.py:281
  51.2 7.2 %collective-permute-start = (s32[1,2]{1,0:T(1,128)S(1)}, s32[1,2]{1,0:T(1,128)S(1)}, u32[]{:S(2)}, u32[]{:S(2)}) collective-permute-start(s32[1,2]{1,0:T(1,128)S(1)} %pad_add_fusion.here), channel_id=1, source_target_pairs={{0,1},{1,0},{2,3},{3,2},{4,5},{5,4},{6,7},{7,6},{8,9},{9,8},{10,11... | collective-permute-start | bytes 32 | tf_op jit(solution)/shard_map/ppermute | solution.py:281
  62.5 6.0 %collective-permute-start.10 = (f32[136,1024]{1,0:T(8,128)S(1)}, f32[136,1024]{1,0:T(8,128)S(1)}, u32[]{:S(2)}, u32[]{:S(2)}) collective-permute-start(f32[136,1024]{1,0:T(8,128)S(1)} %partners_far.1), channel_id=1, source_target_pairs={{0,1},{1,0},{2,3},{3,2},{4,5},{5,4},{6,7},{7,6},{8,9},{9,8},{10,11... | collective-permute-start | bytes 1671176 | tf_op jit(solution)/shard_map/ppermute | solution.py:281
  69.1 72.8 %collective-permute-start.11 = (f32[128,1024]{1,0:T(8,128)S(1)}, f32[128,1024]{1,0:T(8,128)S(1)}, u32[]{:S(2)}, u32[]{:S(2)}) collective-permute-start(f32[128,1024]{1,0:T(8,128)S(1)} %get-tuple-element.14.own), channel_id=1, source_target_pairs={{0,1},{1,0},{2,3},{3,2},{4,5},{5,4},{6,7},{7,6},{8,9},{9,8},{10,11... | collective-permute-start | bytes 1572872 | tf_op jit(solution)/shard_map/ppermute | solution.py:281
  97.6 3.0 %collective-permute-start.12 = (f32[8,128]{1,0:T(8,128)S(1)}, f32[8,128]{1,0:T(8,128)S(1)}, u32[]{:S(2)}, u32[]{:S(2)}) collective-permute-start(f32[8,128]{1,0:T(8,128)S(1)} %reduce_sum.37), channel_id=1, source_target_pairs={{0,1},{1,0},{2,3},{3,2},{4,5},{5,4},{6,7},{7,6},{8,9},{9,8},{10,11... | collective-permute-start | bytes 12296 | tf_op jit(solution)/shard_map/ppermute | solution.py:281

commit v5 on v4

--- a/solution.py
+++ b/solution.py
@@ -8,8 +8,6 @@
 from jax.sharding import PartitionSpec as P
 
 REACH = 3
-SIDE = 4
-LENGTH = 16
 TILE = 256
 FAR = 1e30
 NT = (((1,), (1,)), ((), ()))
@@ -202,14 +200,14 @@
         precision=lax.Precision.HIGHEST,
         preferred_element_type=jnp.float32,
     )
-    gram[...] = terms * scale
+    gram[...] = (terms * scale).reshape(gram.shape)
 
 
 def make_field(particles, sums, far_sums):
     sub, half = sums.shape[0] - 8, sums.shape[1]
     outs = [
         jax.ShapeDtypeStruct((sub, half), jnp.float32),
-        jax.ShapeDtypeStruct((sub, sub), jnp.float32),
+        jax.ShapeDtypeStruct((sub // 8, 8, sub), jnp.float32),
     ]
     return pl.pallas_call(
         functools.partial(field_kernel, 1.0 / particles),
@@ -222,7 +220,7 @@
     )(sums, far_sums)
 
 
-def join_kernel(core_ref, own, other, out):
+def join_kernel(core_ref, own, other, tiles, out, gram):
     @pl.when(pl.program_id(0) == core_ref[0])
     def _():
         out[...] = own[...]
@@ -231,50 +229,49 @@
     def _():
         out[...] = other[...]
 
-
-def join(core, own, other):
+    @pl.when(pl.program_id(0) == 0)
+    def _():
+        gram[...] = tiles[...].reshape(gram.shape)
+
+
+def join(core, own, other, tiles):
     sub, half = own.shape
+    outs = [
+        jax.ShapeDtypeStruct((sub, 2 * half), jnp.float32),
+        jax.ShapeDtypeStruct((sub, sub), jnp.float32),
+    ]
     return pl.pallas_call(
         join_kernel,
         grid_spec=pltpu.PrefetchScalarGridSpec(
             num_scalar_prefetch=1,
             grid=(2,),
-            in_specs=[pl.BlockSpec((sub, half), lambda i, core: (0, 0))] * 2,
-            out_specs=pl.BlockSpec((sub, half), lambda i, core: (0, i)),
-        ),
-        out_shape=jax.ShapeDtypeStruct((sub, 2 * half), jnp.float32),
+            in_specs=[pl.BlockSpec((sub, half), lambda i, core: (0, 0))] * 2
+            + [pl.BlockSpec(tiles.shape, lambda i, core: (0, 0, 0))],
+            out_specs=[
+                pl.BlockSpec((sub, half), lambda i, core: (0, i)),
+                pl.BlockSpec((sub, sub), lambda i, core: (0, 0)),
+            ],
+        ),
+        out_shape=outs,
         compiler_params=PARAMS,
         cost_estimate=pl.CostEstimate(flops=0, bytes_accessed=2 * 2**20, transcendentals=0),
         name="join",
-    )(core, own, other)
-
-
-def exchange(pieces, stride):
-    count = pieces.shape[0]
+    )(core, own, other, tiles)
+
+
+def exchange(tiles, groups):
+    return lax.all_to_all(tiles, "blk", 0, 0, axis_index_groups=groups, tiled=True)
+
+
+def sum_over_all(tiles):
+    count = tiles.shape[0]
     blocks = lax.axis_size("blk")
-    groups = [
-        list(range(start, start + count * stride, stride))
-        for start in range(blocks)
-        if start // stride % count == 0
-    ]
-    return lax.all_to_all(pieces, "blk", 0, 0, axis_index_groups=groups, tiled=True)
-
-
-def repeat(piece):
-    return jnp.broadcast_to(piece, (SIDE, *piece.shape))
-
-
-def sum_over_all(gram):
-    size = gram.shape[0]
-    part = gram.reshape(SIDE, size // SIDE, size)
-    part = jnp.sum(exchange(part, LENGTH), axis=0)
-    part = part.reshape(SIDE, size // SIDE // SIDE, size)
-    part = jnp.sum(exchange(part, LENGTH * SIDE), axis=0)
+    near_z = [list(range(i, i + count)) for i in range(0, blocks, count)]
+    planes = [list(range(i, blocks, count)) for i in range(count)]
+    part = jnp.sum(exchange(tiles, planes), axis=0)
     part = part + swap(part)
-    part = jnp.sum(exchange(repeat(part), 1), axis=0)
-    part = jnp.sum(exchange(repeat(part), SIDE), axis=0)
-    part = exchange(repeat(part), LENGTH * SIDE).reshape(size // SIDE, size)
-    return exchange(repeat(part), LENGTH).reshape(size, size)
+    part = jnp.sum(exchange(jnp.broadcast_to(part, tiles.shape), near_z), axis=0)
+    return exchange(jnp.broadcast_to(part, tiles.shape), planes)
 
 
 def swap(x):
@@ -298,8 +295,12 @@
     give, keep = pack(core, features, subspace)
     own_sums, rows_t, row_norms = apply_self(core, features, keep)
     kept, swapped = [], []
-    for _ in range(REACH):
+    for step in range(REACH):
         give, keep = relay(give), relay(keep)
+        if step == 0:
+            give, there, own_sums, rows_t, row_norms = lax.optimization_barrier(
+                (give, there, own_sums, rows_t, row_norms)
+            )
         kept.append(keep)
         swapped.append(swap(give))
     near = kept + swapped
@@ -308,7 +309,7 @@
     sums = apply_partners("near", core, here, there, rows_t, row_norms, own_sums, near)
     field, gram = make_field(float(lax.axis_size("blk") * block), sums, far_sums)
     other = swap(field)
-    return (join(core, field, other), sum_over_all(gram))
+    return tuple(join(core, field, other, sum_over_all(gram)))
 
 
 def solution(mesh):

time: 144 us -> 125 us (0.87)
  the two profiles are of different devices: /device:TPU:2 before, /device:TPU:1 now
where the time goes in v5:
time: 125 us; the launch traced here: 124 us
  starting transfers between devices  68.3 us (55%)
  blocking collectives  32.7 us (26%)
  Pallas kernels  14.6 us (12%)
  waiting for transfers between devices  3.55 us (3%)
  local copies, waits for them, and re-layouts  2.28 us (2%)
  between operations  2.14 us (2%)
    ppermute x6, starting transfers between devices, relay(): return lax.ppermute(x, ('blk', 'pair'), pairs)  45.8 us
    all_to_all x3, blocking collectives, exchange(): lax.all_to_all(tiles, 'blk', 0, 0, axis_index_groups=groups, tiled=True)  32.7 us
    ppermute x7, starting transfers between devices, swap(): return lax.ppermute(x, 'pair', [(0, 1), (1, 0)])  22.4 us
    pallas_call x2, Pallas kernels, apply_partners(): pl.pallas_call(partner_kernel, grid_spec=pltpu.PrefetchScalarGridSpec(num...  8.1 us
    pallas_call x1, Pallas kernels, apply_self(): pl.pallas_call(self_kernel, grid_spec=pltpu.PrefetchScalarGridSpec(num_sc...  4.76 us
    ppermute x6, waiting for transfers between devices, relay(): return lax.ppermute(x, ('blk', 'pair'), pairs)  2.73 us
  transfers between devices with their start and end apart: 13, of which 3 were waited for; matrix products, arithmetic and copies ran while one was open for 0% of the time, Pallas kernels for 7%

profile of v5, /device:TPU:1, one launch (start us, length us, event | category | flops | bytes accessed | tf_op | source)
XLA Modules:
  0.0 123.7 jit_solution(3692075935376361069)
XLA Ops:
  0.6 1.2 copy-done
  1.9 1.0 copy-done.1
  3.0 16.6 %collective-permute-start = (bf16[2048,128]{1,0:T(8,128)(2,1)S(1)}, bf16[2048,128]{1,0:T(8,128)(2,1)S(1)}, u32[]{:S(2)}, u32[]{:S(2)}) collective-permute-start(bf16[2048,128]{1,0:T(8,128)(2,1)S(1)} %get-tuple-element.14), channel_id=1, source_target_pairs={{0,2},{1,511},{2,4},{3,1},{4,6},{5,3},{6,8},{7,5},{8,10},{9,7},{10... | collective-permute-start | bytes 1572872 | tf_op jit(solution)/shard_map/ppermute | solution.py:287
  21.0 1.9 %collective-permute-start.1 = (s32[1,2]{1,0:T(1,128)S(1)}, s32[1,2]{1,0:T(1,128)S(1)}, u32[]{:S(2)}, u32[]{:S(2)}) collective-permute-start(s32[1,2]{1,0:T(1,128)S(1)} %pad_add_fusion.here), channel_id=1, source_target_pairs={{0,1},{1,0},{2,3},{3,2},{4,5},{5,4},{6,7},{7,6},{8,9},{9,8},{10,11... | collective-permute-start | bytes 32 | tf_op jit(solution)/shard_map/ppermute | solution.py:278
  22.9 2.6 %collective-permute-start.2 = (bf16[2048,128]{1,0:T(8,128)(2,1)S(1)}, bf16[2048,128]{1,0:T(8,128)(2,1)S(1)}, u32[]{:S(2)}, u32[]{:S(2)}) collective-permute-start(bf16[2048,128]{1,0:T(8,128)(2,1)S(1)} %get-tuple-element.15.packed), channel_id=1, source_target_pairs={{0,2},{1,511},{2,4},{3,1},{4,6},{5,3},{6,8},{7,5},{8,10},{9,7},{10... | collective-permute-start | bytes 1572872 | tf_op jit(solution)/shard_map/ppermute | solution.py:287
  25.5 4.8 %own_block.1 = (f32[136,2048]{1,0:T(8,128)S(1)}, bf16[128,2048]{1,0:T(8,128)(2,1)S(1)}, f32[1,2048]{1,0:T(1,128)S(1)}) custom-call(s32[1]{0:T(128)} %bitcast.core_ref, bf16[2048,128]{1,0:T(8,128)(2,1)S(1)} %copy-done.1, bf16[2048,128]{1,0:T(8,128)(2,1)S(1)} %get-tuple-element.15.packed), custom_call_target="tpu_custom_call" | custom-call | flops 1073741824 | bytes 4194304 | tf_op jit(solution)/shard_map/own_block/pallas_call | solution.py:107
  30.3 4.6 %collective-permute-start.6 = (bf16[2048,128]{1,0:T(8,128)(2,1)S(1)}, bf16[2048,128]{1,0:T(8,128)(2,1)S(1)}, u32[]{:S(2)}, u32[]{:S(2)}) collective-permute-start(bf16[2048,128]{1,0:T(8,128)(2,1)S(1)} %collective-permute-done), channel_id=1, source_target_pairs={{0,2},{1,511},{2,4},{3,1},{4,6},{5,3},{6,8},{7,5},{8,10},{9,7},{10... | collective-permute-start | bytes 1572872 | tf_op jit(solution)/shard_map/ppermute | solution.py:287
  35.0 5.9 %collective-permute-start.3 = (bf16[2048,128]{1,0:T(8,128)(2,1)S(1)}, bf16[2048,128]{1,0:T(8,128)(2,1)S(1)}, u32[]{:S(2)}, u32[]{:S(2)}) collective-permute-start(bf16[2048,128]{1,0:T(8,128)(2,1)S(1)} %collective-permute-done.2.refs_0_), channel_id=1, source_target_pairs={{0,2},{1,511},{2,4},{3,1},{4,6},{5,3},{6,8},{7,5},{8,10},{9,7},{10... | collective-permute-start | bytes 1572872 | tf_op jit(solution)/shard_map/ppermute | solution.py:287
  41.0 9.2 %collective-permute-start.8 = (bf16[2048,128]{1,0:T(8,128)(2,1)S(1)}, bf16[2048,128]{1,0:T(8,128)(2,1)S(1)}, u32[]{:S(2)}, u32[]{:S(2)}) collective-permute-start(bf16[2048,128]{1,0:T(8,128)(2,1)S(1)} %collective-permute-done.6), channel_id=1, source_target_pairs={{0,2},{1,511},{2,4},{3,1},{4,6},{5,3},{6,8},{7,5},{8,10},{9,7},{10... | collective-permute-start | bytes 1572872 | tf_op jit(solution)/shard_map/ppermute | solution.py:287
  50.3 1.9 %collective-permute-start.5 = (bf16[2048,128]{1,0:T(8,128)(2,1)S(1)}, bf16[2048,128]{1,0:T(8,128)(2,1)S(1)}, u32[]{:S(2)}, u32[]{:S(2)}) collective-permute-start(bf16[2048,128]{1,0:T(8,128)(2,1)S(1)} %collective-permute-done), channel_id=1, source_target_pairs={{0,1},{1,0},{2,3},{3,2},{4,5},{5,4},{6,7},{7,6},{8,9},{9,8},{10,11... | collective-permute-start | bytes 1572872 | tf_op jit(solution)/shard_map/ppermute | solution.py:278
  52.2 2.4 %collective-permute-start.7 = (bf16[2048,128]{1,0:T(8,128)(2,1)S(1)}, bf16[2048,128]{1,0:T(8,128)(2,1)S(1)}, u32[]{:S(2)}, u32[]{:S(2)}) collective-permute-start(bf16[2048,128]{1,0:T(8,128)(2,1)S(1)} %collective-permute-done.6), channel_id=1, source_target_pairs={{0,1},{1,0},{2,3},{3,2},{4,5},{5,4},{6,7},{7,6},{8,9},{9,8},{10,11... | collective-permute-start | bytes 1572872 | tf_op jit(solution)/shard_map/ppermute | solution.py:278
  54.6 6.8 %collective-permute-start.4 = (bf16[2048,128]{1,0:T(8,128)(2,1)S(1)}, bf16[2048,128]{1,0:T(8,128)(2,1)S(1)}, u32[]{:S(2)}, u32[]{:S(2)}) collective-permute-start(bf16[2048,128]{1,0:T(8,128)(2,1)S(1)} %collective-permute-done.3.refs_1_), channel_id=1, source_target_pairs={{0,2},{1,511},{2,4},{3,1},{4,6},{5,3},{6,8},{7,5},{8,10},{9,7},{10... | collective-permute-start | bytes 1572872 | tf_op jit(solution)/shard_map/ppermute | solution.py:287
  61.5 3.5 %collective-permute-start.9 = (bf16[2048,128]{1,0:T(8,128)(2,1)S(1)}, bf16[2048,128]{1,0:T(8,128)(2,1)S(1)}, u32[]{:S(2)}, u32[]{:S(2)}) collective-permute-start(bf16[2048,128]{1,0:T(8,128)(2,1)S(1)} %collective-permute-done.8), channel_id=1, source_target_pairs={{0,1},{1,0},{2,3},{3,2},{4,5},{5,4},{6,7},{7,6},{8,9},{9,8},{10,11... | collective-permute-start | bytes 1572872 | tf_op jit(solution)/shard_map/ppermute | solution.py:278
  65.0 2.5 %collective-permute-done.4.refs_2_ = bf16[2048,128]{1,0:T(8,128)(2,1)S(1)} collective-permute-done((bf16[2048,128]{1,0:T(8,128)(2,1)S(1)}, bf16[2048,128]{1,0:T(8,128)(2,1)S(1)}, u32[]{:S(2)}, u32[]{:S(2)}) %collective-permute-start.4) | collective-permute-done | bytes 524320 | tf_op jit(solution)/shard_map/ppermute | solution.py:287
  67.6 4.0 %partners_far.1 = f32[136,1024]{1,0:T(8,128)S(1)} custom-call(s32[1]{0:T(128)} %bitcast.core_ref, s32[1,2]{1,0:T(1,128)S(1)} %pad_add_fusion.here, s32[1,2]{1,0:T(1,128)S(1)} %collective-permute-done.1.there, bf16[128,2048]{1,0:T(8,128)(2,1)S(1)} %get-tuple-element.20.rows_t, f32[1,2048]{1,0:T(1,128)S(1)} %get-tuple-element.21.row_norms, ...), custom_call_target="tpu_custom_call" | custom-call | flops 1073741824 | bytes 3145728 | tf_op jit(solution)/shard_map/partners_far/pallas_call | solution.py:164
  71.6 7.2 %collective-permute-start.10 = (f32[136,1024]{1,0:T(8,128)S(1)}, f32[136,1024]{1,0:T(8,128)S(1)}, u32[]{:S(2)}, u32[]{:S(2)}) collective-permute-start(f32[136,1024]{1,0:T(8,128)S(1)} %partners_far.1), channel_id=1, source_target_pairs={{0,1},{1,0},{2,3},{3,2},{4,5},{5,4},{6,7},{7,6},{8,9},{9,8},{10,11... | collective-permute-start | bytes 1671176 | tf_op jit(solution)/shard_map/ppermute | solution.py:278
  78.9 4.1 %partners_near.1.sums = f32[136,1024]{1,0:T(8,128)S(1)} custom-call(s32[1]{0:T(128)} %bitcast.core_ref, s32[1,2]{1,0:T(1,128)S(1)} %pad_add_fusion.here, s32[1,2]{1,0:T(1,128)S(1)} %collective-permute-done.1.there, bf16[128,2048]{1,0:T(8,128)(2,1)S(1)} %get-tuple-element.20.rows_t, f32[1,2048]{1,0:T(1,128)S(1)} %get-tuple-element.21.row_norms, ...), custom_call_target="tpu_custom_call" | custom-call | flops 1073741824 | bytes 3145728 | tf_op jit(solution)/shard_map/partners_near/pallas_call | solution.py:164
  83.6 1.9 %collective-permute-start.11 = (f32[128,1024]{1,0:T(8,128)S(1)}, f32[128,1024]{1,0:T(8,128)S(1)}, u32[]{:S(2)}, u32[]{:S(2)}) collective-permute-start(f32[128,1024]{1,0:T(8,128)S(1)} %get-tuple-element.24.own), channel_id=1, source_target_pairs={{0,1},{1,0},{2,3},{3,2},{4,5},{5,4},{6,7},{7,6},{8,9},{9,8},{10,11... | collective-permute-start | bytes 1572872 | tf_op jit(solution)/shard_map/ppermute | solution.py:278
  85.5 9.1 %all_to_all.15 = f32[16,8,128]{2,1,0:T(8,128)S(1)} all-to-all(f32[16,8,128]{2,1,0:T(8,128)S(1)} %get-tuple-element.25), channel_id=1, replica_groups={{0,32,64,96,128,160,192,224,256,288,320,352,384,416,448,480},{2,34,66,9..., dimensions={0} | all-to-all | bytes 131072 | tf_op jit(solution)/shard_map/all_to_all | solution.py:263
  94.6 3.6 %collective-permute-start.12 = (f32[8,128]{1,0:T(8,128)S(1)}, f32[8,128]{1,0:T(8,128)S(1)}, u32[]{:S(2)}, u32[]{:S(2)}) collective-permute-start(f32[8,128]{1,0:T(8,128)S(1)} %reduce_sum.18), channel_id=1, source_target_pairs={{0,1},{1,0},{2,3},{3,2},{4,5},{5,4},{6,7},{7,6},{8,9},{9,8},{10,11... | collective-permute-start | bytes 12296 | tf_op jit(solution)/shard_map/ppermute | solution.py:278
  98.1 0.8 collective-permute-done.12
  99.0 14.2 %all_to_all.16 = f32[16,8,128]{2,1,0:T(8,128)S(1)} all-to-all(f32[16,8,128]{2,1,0:T(8,128)S(1)} %broadcast_in_dim.6), channel_id=1, replica_groups={{0,2,4,6,8,10,12,14,16,18,20,22,24,26,28,30},{32,34,36,38,40,42,44,46,4..., dimensions={0} | all-to-all | bytes 131072 | tf_op jit(solution)/shard_map/all_to_all | solution.py:263
  113.2 9.4 %all_to_all.17.tiles = f32[16,8,128]{2,1,0:T(8,128)S(1)} all-to-all(f32[16,8,128]{2,1,0:T(8,128)S(1)} %broadcast_in_dim.7), channel_id=1, replica_groups={{0,32,64,96,128,160,192,224,256,288,320,352,384,416,448,480},{2,34,66,9..., dimensions={0} | all-to-all | bytes 131072 | tf_op jit(solution)/shard_map/all_to_all | solution.py:263
  122.6 1.0 join.1
  (21 shorter events, 1.1 us)
Async XLA Ops:
  0.6 1.2 copy-start
  1.9 1.0 copy-start.1
  3.0 27.3 %collective-permute-start = (bf16[2048,128]{1,0:T(8,128)(2,1)S(1)}, bf16[2048,128]{1,0:T(8,128)(2,1)S(1)}, u32[]{:S(2)}, u32[]{:S(2)}) collective-permute-start(bf16[2048,128]{1,0:T(8,128)(2,1)S(1)} %get-tuple-element.14), channel_id=1, source_target_pairs={{0,2},{1,511},{2,4},{3,1},{4,6},{5,3},{6,8},{7,5},{8,10},{9,7},{10... | collective-permute-start | bytes 1572872 | tf_op jit(solution)/shard_map/ppermute | solution.py:287
  21.0 9.3 %collective-permute-start.1 = (s32[1,2]{1,0:T(1,128)S(1)}, s32[1,2]{1,0:T(1,128)S(1)}, u32[]{:S(2)}, u32[]{:S(2)}) collective-permute-start(s32[1,2]{1,0:T(1,128)S(1)} %pad_add_fusion.here), channel_id=1, source_target_pairs={{0,1},{1,0},{2,3},{3,2},{4,5},{5,4},{6,7},{7,6},{8,9},{9,8},{10,11... | collective-permute-start | bytes 32 | tf_op jit(solution)/shard_map/ppermute | solution.py:278
  22.9 12.1 %collective-permute-start.2 = (bf16[2048,128]{1,0:T(8,128)(2,1)S(1)}, bf16[2048,128]{1,0:T(8,128)(2,1)S(1)}, u32[]{:S(2)}, u32[]{:S(2)}) collective-permute-start(bf16[2048,128]{1,0:T(8,128)(2,1)S(1)} %get-tuple-element.15.packed), channel_id=1, source_target_pairs={{0,2},{1,511},{2,4},{3,1},{4,6},{5,3},{6,8},{7,5},{8,10},{9,7},{10... | collective-permute-start | bytes 1572872 | tf_op jit(solution)/shard_map/ppermute | solution.py:287
  30.3 10.7 %collective-permute-start.6 = (bf16[2048,128]{1,0:T(8,128)(2,1)S(1)}, bf16[2048,128]{1,0:T(8,128)(2,1)S(1)}, u32[]{:S(2)}, u32[]{:S(2)}) collective-permute-start(bf16[2048,128]{1,0:T(8,128)(2,1)S(1)} %collective-permute-done), channel_id=1, source_target_pairs={{0,2},{1,511},{2,4},{3,1},{4,6},{5,3},{6,8},{7,5},{8,10},{9,7},{10... | collective-permute-start | bytes 1572872 | tf_op jit(solution)/shard_map/ppermute | solution.py:287
  35.0 19.7 %collective-permute-start.3 = (bf16[2048,128]{1,0:T(8,128)(2,1)S(1)}, bf16[2048,128]{1,0:T(8,128)(2,1)S(1)}, u32[]{:S(2)}, u32[]{:S(2)}) collective-permute-start(bf16[2048,128]{1,0:T(8,128)(2,1)S(1)} %collective-permute-done.2.refs_0_), channel_id=1, source_target_pairs={{0,2},{1,511},{2,4},{3,1},{4,6},{5,3},{6,8},{7,5},{8,10},{9,7},{10... | collective-permute-start | bytes 1572872 | tf_op jit(solution)/shard_map/ppermute | solution.py:287
  41.0 20.4 %collective-permute-start.8 = (bf16[2048,128]{1,0:T(8,128)(2,1)S(1)}, bf16[2048,128]{1,0:T(8,128)(2,1)S(1)}, u32[]{:S(2)}, u32[]{:S(2)}) collective-permute-start(bf16[2048,128]{1,0:T(8,128)(2,1)S(1)} %collective-permute-done.6), channel_id=1, source_target_pairs={{0,2},{1,511},{2,4},{3,1},{4,6},{5,3},{6,8},{7,5},{8,10},{9,7},{10... | collective-permute-start | bytes 1572872 | tf_op jit(solution)/shard_map/ppermute | solution.py:287
  50.3 14.7 %collective-permute-start.5 = (bf16[2048,128]{1,0:T(8,128)(2,1)S(1)}, bf16[2048,128]{1,0:T(8,128)(2,1)S(1)}, u32[]{:S(2)}, u32[]{:S(2)}) collective-permute-start(bf16[2048,128]{1,0:T(8,128)(2,1)S(1)} %collective-permute-done), channel_id=1, source_target_pairs={{0,1},{1,0},{2,3},{3,2},{4,5},{5,4},{6,7},{7,6},{8,9},{9,8},{10,11... | collective-permute-start | bytes 1572872 | tf_op jit(solution)/shard_map/ppermute | solution.py:278
  52.2 15.4 %collective-permute-start.7 = (bf16[2048,128]{1,0:T(8,128)(2,1)S(1)}, bf16[2048,128]{1,0:T(8,128)(2,1)S(1)}, u32[]{:S(2)}, u32[]{:S(2)}) collective-permute-start(bf16[2048,128]{1,0:T(8,128)(2,1)S(1)} %collective-permute-done.6), channel_id=1, source_target_pairs={{0,1},{1,0},{2,3},{3,2},{4,5},{5,4},{6,7},{7,6},{8,9},{9,8},{10,11... | collective-permute-start | bytes 1572872 | tf_op jit(solution)/shard_map/ppermute | solution.py:278
  54.6 12.9 %collective-permute-start.4 = (bf16[2048,128]{1,0:T(8,128)(2,1)S(1)}, bf16[2048,128]{1,0:T(8,128)(2,1)S(1)}, u32[]{:S(2)}, u32[]{:S(2)}) collective-permute-start(bf16[2048,128]{1,0:T(8,128)(2,1)S(1)} %collective-permute-done.3.refs_1_), channel_id=1, source_target_pairs={{0,2},{1,511},{2,4},{3,1},{4,6},{5,3},{6,8},{7,5},{8,10},{9,7},{10... | collective-permute-start | bytes 1572872 | tf_op jit(solution)/shard_map/ppermute | solution.py:287
  61.5 6.1 %collective-permute-start.9 = (bf16[2048,128]{1,0:T(8,128)(2,1)S(1)}, bf16[2048,128]{1,0:T(8,128)(2,1)S(1)}, u32[]{:S(2)}, u32[]{:S(2)}) collective-permute-start(bf16[2048,128]{1,0:T(8,128)(2,1)S(1)} %collective-permute-done.8), channel_id=1, source_target_pairs={{0,1},{1,0},{2,3},{3,2},{4,5},{5,4},{6,7},{7,6},{8,9},{9,8},{10,11... | collective-permute-start | bytes 1572872 | tf_op jit(solution)/shard_map/ppermute | solution.py:278
  71.6 11.3 %collective-permute-start.10 = (f32[136,1024]{1,0:T(8,128)S(1)}, f32[136,1024]{1,0:T(8,128)S(1)}, u32[]{:S(2)}, u32[]{:S(2)}) collective-permute-start(f32[136,1024]{1,0:T(8,128)S(1)} %partners_far.1), channel_id=1, source_target_pairs={{0,1},{1,0},{2,3},{3,2},{4,5},{5,4},{6,7},{7,6},{8,9},{9,8},{10,11... | collective-permute-start | bytes 1671176 | tf_op jit(solution)/shard_map/ppermute | solution.py:278
  83.6 39.1 %collective-permute-start.11 = (f32[128,1024]{1,0:T(8,128)S(1)}, f32[128,1024]{1,0:T(8,128)S(1)}, u32[]{:S(2)}, u32[]{:S(2)}) collective-permute-start(f32[128,1024]{1,0:T(8,128)S(1)} %get-tuple-element.24.own), channel_id=1, source_target_pairs={{0,1},{1,0},{2,3},{3,2},{4,5},{5,4},{6,7},{7,6},{8,9},{9,8},{10,11... | collective-permute-start | bytes 1572872 | tf_op jit(solution)/shard_map/ppermute | solution.py:278
  94.6 4.4 %collective-permute-start.12 = (f32[8,128]{1,0:T(8,128)S(1)}, f32[8,128]{1,0:T(8,128)S(1)}, u32[]{:S(2)}, u32[]{:S(2)}) collective-permute-start(f32[8,128]{1,0:T(8,128)S(1)} %reduce_sum.18), channel_id=1, source_target_pairs={{0,1},{1,0},{2,3},{3,2},{4,5},{5,4},{6,7},{7,6},{8,9},{9,8},{10,11... | collective-permute-start | bytes 12296 | tf_op jit(solution)/shard_map/ppermute | solution.py:278

commit v6 on v5

--- a/solution.py
+++ b/solution.py
@@ -40,7 +40,7 @@
             out_specs=[pl.BlockSpec(out.shape, whole)] * 2,
         ),
         out_shape=[out, out],
-        compiler_params=PARAMS,
+        compiler_params=pltpu.CompilerParams(vmem_limit_bytes=62 * 2**20),
         cost_estimate=pl.CostEstimate(flops=0, bytes_accessed=2 * 2**20, transcendentals=0),
         name="pack",
     )(core, features, subspace)
@@ -282,8 +282,9 @@
     blocks = lax.axis_size("blk")
     pairs = []
     for i in range(blocks):
-        pairs.append((2 * i, (i + 1) % blocks * 2))
-        pairs.append((2 * i + 1, (i - 1) % blocks * 2 + 1))
+        if i + 1 < blocks:
+            pairs.append((2 * i, 2 * i + 2))
+            pairs.append((2 * i + 3, 2 * i + 1))
     return lax.ppermute(x, ("blk", "pair"), pairs)
 
 

time: 125 us -> 123 us (0.984)
  starting transfers between devices: 68.3 us -> 36.4 us
  blocking collectives: 32.7 us -> 50.4 us
  waiting for transfers between devices: 3.55 us -> 14 us
  Pallas kernels: 14.6 us -> 17 us
    ppermute x6, starting transfers between devices: 45.8 us -> 7.72 us  [relay(): return lax.ppermute(x, ('blk', 'pair'), pairs)]
    all_to_all x3, blocking collectives: 32.7 us -> 50.4 us  [exchange(): lax.all_to_all(tiles, 'blk', 0, 0, axis_index_groups=groups, tiled=True)]
    ppermute x6, waiting for transfers between devices: 2.73 us -> 13.2 us  [relay(): return lax.ppermute(x, ('blk', 'pair'), pairs)]
    ppermute x7, starting transfers between devices: 22.4 us -> 28.7 us  [swap(): return lax.ppermute(x, 'pair', [(0, 1), (1, 0)])]
    pallas_call x1, Pallas kernels: 0.09 us -> 2.51 us  [pack(): pl.pallas_call(pack_kernel, grid_spec=pltpu.PrefetchScalarGridSpec(num_sc...]
  transfers between devices with their start and end apart: 13 -> 13, of which waited for: 3 -> 5; matrix products, arithmetic and copies ran while one was open for 0% -> 0% of each run, Pallas kernels for 7% -> 7%
where the time goes in v6:
time: 123 us; the launch traced here: 121 us
  blocking collectives  50.4 us (41%)
  starting transfers between devices  36.4 us (30%)
  Pallas kernels  17 us (14%)
  waiting for transfers between devices  14 us (11%)
  between operations  2.13 us (2%)
    all_to_all x3, blocking collectives, exchange(): lax.all_to_all(tiles, 'blk', 0, 0, axis_index_groups=groups, tiled=True)  50.4 us
    ppermute x7, starting transfers between devices, swap(): return lax.ppermute(x, 'pair', [(0, 1), (1, 0)])  28.7 us
    ppermute x6, waiting for transfers between devices, relay(): return lax.ppermute(x, ('blk', 'pair'), pairs)  13.2 us
    pallas_call x2, Pallas kernels, apply_partners(): pl.pallas_call(partner_kernel, grid_spec=pltpu.PrefetchScalarGridSpec(num...  8.12 us
    ppermute x6, starting transfers between devices, relay(): return lax.ppermute(x, ('blk', 'pair'), pairs)  7.72 us
    pallas_call x1, Pallas kernels, apply_self(): pl.pallas_call(self_kernel, grid_spec=pltpu.PrefetchScalarGridSpec(num_sc...  4.76 us
    pallas_call x1, Pallas kernels, pack(): pl.pallas_call(pack_kernel, grid_spec=pltpu.PrefetchScalarGridSpec(num_sc...  2.51 us
  transfers between devices with their start and end apart: 13, of which 5 were waited for; matrix products, arithmetic and copies ran while one was open for 0% of the time, Pallas kernels for 7%

profile of v6, /device:TPU:1, one launch (start us, length us, event | category | flops | bytes accessed | tf_op | source)
XLA Modules:
  0.0 121.2 jit_solution(6252055698283373217)
XLA Ops:
  0.6 2.5 %pack.1 = (bf16[2048,128]{1,0:T(8,128)(2,1)}, bf16[2048,128]{1,0:T(8,128)(2,1)}) custom-call(s32[1]{0:T(128)} %bitcast.core_ref, bf16[2048,128]{1,0:T(8,128)(2,1)} %feats_ref.3, f32[128,2048]{1,0:T(8,128)} %field_ref.1), custom_call_target="tpu_custom_call" | custom-call | bytes 2097152 | tf_op jit(solution)/shard_map/pack/pallas_call | solution.py:34
  3.2 1.3 %collective-permute-start = (bf16[2048,128]{1,0:T(8,128)(2,1)}, bf16[2048,128]{1,0:T(8,128)(2,1)S(1)}, u32[]{:S(2)}, u32[]{:S(2)}) collective-permute-start(bf16[2048,128]{1,0:T(8,128)(2,1)} %get-tuple-element.14), channel_id=1, source_target_pairs={{0,2},{3,1},{2,4},{5,3},{4,6},{7,5},{6,8},{9,7},{8,10},{11,9},{10,... | collective-permute-start | bytes 1572872 | tf_op jit(solution)/shard_map/ppermute | solution.py:288
  5.8 8.8 %collective-permute-start.1 = (s32[1,2]{1,0:T(1,128)S(1)}, s32[1,2]{1,0:T(1,128)S(1)}, u32[]{:S(2)}, u32[]{:S(2)}) collective-permute-start(s32[1,2]{1,0:T(1,128)S(1)} %pad_add_fusion.here), channel_id=1, source_target_pairs={{0,1},{1,0},{2,3},{3,2},{4,5},{5,4},{6,7},{7,6},{8,9},{9,8},{10,11... | collective-permute-start | bytes 32 | tf_op jit(solution)/shard_map/ppermute | solution.py:278
  14.6 1.3 %collective-permute-start.2 = (bf16[2048,128]{1,0:T(8,128)(2,1)}, bf16[2048,128]{1,0:T(8,128)(2,1)S(1)}, u32[]{:S(2)}, u32[]{:S(2)}) collective-permute-start(bf16[2048,128]{1,0:T(8,128)(2,1)} %get-tuple-element.15.packed), channel_id=1, source_target_pairs={{0,2},{3,1},{2,4},{5,3},{4,6},{7,5},{6,8},{9,7},{8,10},{11,9},{10,... | collective-permute-start | bytes 1572872 | tf_op jit(solution)/shard_map/ppermute | solution.py:288
  17.0 4.8 %own_block.1 = (f32[136,2048]{1,0:T(8,128)S(1)}, bf16[128,2048]{1,0:T(8,128)(2,1)S(1)}, f32[1,2048]{1,0:T(1,128)S(1)}) custom-call(s32[1]{0:T(128)} %bitcast.core_ref, bf16[2048,128]{1,0:T(8,128)(2,1)S(1)} %copy-done, bf16[2048,128]{1,0:T(8,128)(2,1)S(1)} %copy-done.1), custom_call_target="tpu_custom_call" | custom-call | flops 1073741824 | bytes 4194304 | tf_op jit(solution)/shard_map/own_block/pallas_call | solution.py:107
  21.8 1.3 %collective-permute-start.6 = (bf16[2048,128]{1,0:T(8,128)(2,1)S(1)}, bf16[2048,128]{1,0:T(8,128)(2,1)S(1)}, u32[]{:S(2)}, u32[]{:S(2)}) collective-permute-start(bf16[2048,128]{1,0:T(8,128)(2,1)S(1)} %collective-permute-done), channel_id=1, source_target_pairs={{0,2},{3,1},{2,4},{5,3},{4,6},{7,5},{6,8},{9,7},{8,10},{11,9},{10,... | collective-permute-start | bytes 1572872 | tf_op jit(solution)/shard_map/ppermute | solution.py:288
  23.1 1.7 %collective-permute-done.2.refs_0_ = bf16[2048,128]{1,0:T(8,128)(2,1)S(1)} collective-permute-done((bf16[2048,128]{1,0:T(8,128)(2,1)}, bf16[2048,128]{1,0:T(8,128)(2,1)S(1)}, u32[]{:S(2)}, u32[]{:S(2)}) %collective-permute-start.2) | collective-permute-done | bytes 524320 | tf_op jit(solution)/shard_map/ppermute | solution.py:288
  24.8 1.3 %collective-permute-start.3 = (bf16[2048,128]{1,0:T(8,128)(2,1)S(1)}, bf16[2048,128]{1,0:T(8,128)(2,1)S(1)}, u32[]{:S(2)}, u32[]{:S(2)}) collective-permute-start(bf16[2048,128]{1,0:T(8,128)(2,1)S(1)} %collective-permute-done.2.refs_0_), channel_id=1, source_target_pairs={{0,2},{3,1},{2,4},{5,3},{4,6},{7,5},{6,8},{9,7},{8,10},{11,9},{10,... | collective-permute-start | bytes 1572872 | tf_op jit(solution)/shard_map/ppermute | solution.py:288
  26.1 6.3 %collective-permute-done.6 = bf16[2048,128]{1,0:T(8,128)(2,1)S(1)} collective-permute-done((bf16[2048,128]{1,0:T(8,128)(2,1)S(1)}, bf16[2048,128]{1,0:T(8,128)(2,1)S(1)}, u32[]{:S(2)}, u32[]{:S(2)}) %collective-permute-start.6) | collective-permute-done | bytes 524320 | tf_op jit(solution)/shard_map/ppermute | solution.py:288
  32.3 1.3 %collective-permute-start.8 = (bf16[2048,128]{1,0:T(8,128)(2,1)S(1)}, bf16[2048,128]{1,0:T(8,128)(2,1)S(1)}, u32[]{:S(2)}, u32[]{:S(2)}) collective-permute-start(bf16[2048,128]{1,0:T(8,128)(2,1)S(1)} %collective-permute-done.6), channel_id=1, source_target_pairs={{0,2},{3,1},{2,4},{5,3},{4,6},{7,5},{6,8},{9,7},{8,10},{11,9},{10,... | collective-permute-start | bytes 1572872 | tf_op jit(solution)/shard_map/ppermute | solution.py:288
  33.6 5.3 %collective-permute-start.5 = (bf16[2048,128]{1,0:T(8,128)(2,1)S(1)}, bf16[2048,128]{1,0:T(8,128)(2,1)S(1)}, u32[]{:S(2)}, u32[]{:S(2)}) collective-permute-start(bf16[2048,128]{1,0:T(8,128)(2,1)S(1)} %collective-permute-done), channel_id=1, source_target_pairs={{0,1},{1,0},{2,3},{3,2},{4,5},{5,4},{6,7},{7,6},{8,9},{9,8},{10,11... | collective-permute-start | bytes 1572872 | tf_op jit(solution)/shard_map/ppermute | solution.py:278
  38.9 1.9 %collective-permute-start.7 = (bf16[2048,128]{1,0:T(8,128)(2,1)S(1)}, bf16[2048,128]{1,0:T(8,128)(2,1)S(1)}, u32[]{:S(2)}, u32[]{:S(2)}) collective-permute-start(bf16[2048,128]{1,0:T(8,128)(2,1)S(1)} %collective-permute-done.6), channel_id=1, source_target_pairs={{0,1},{1,0},{2,3},{3,2},{4,5},{5,4},{6,7},{7,6},{8,9},{9,8},{10,11... | collective-permute-start | bytes 1572872 | tf_op jit(solution)/shard_map/ppermute | solution.py:278
  40.9 1.3 %collective-permute-start.4 = (bf16[2048,128]{1,0:T(8,128)(2,1)S(1)}, bf16[2048,128]{1,0:T(8,128)(2,1)S(1)}, u32[]{:S(2)}, u32[]{:S(2)}) collective-permute-start(bf16[2048,128]{1,0:T(8,128)(2,1)S(1)} %collective-permute-done.3.refs_1_), channel_id=1, source_target_pairs={{0,2},{3,1},{2,4},{5,3},{4,6},{7,5},{6,8},{9,7},{8,10},{11,9},{10,... | collective-permute-start | bytes 1572872 | tf_op jit(solution)/shard_map/ppermute | solution.py:288
  42.2 1.4 %collective-permute-done.8 = bf16[2048,128]{1,0:T(8,128)(2,1)S(1)} collective-permute-done((bf16[2048,128]{1,0:T(8,128)(2,1)S(1)}, bf16[2048,128]{1,0:T(8,128)(2,1)S(1)}, u32[]{:S(2)}, u32[]{:S(2)}) %collective-permute-start.8) | collective-permute-done | bytes 524320 | tf_op jit(solution)/shard_map/ppermute | solution.py:288
  43.6 4.1 %collective-permute-start.9 = (bf16[2048,128]{1,0:T(8,128)(2,1)S(1)}, bf16[2048,128]{1,0:T(8,128)(2,1)S(1)}, u32[]{:S(2)}, u32[]{:S(2)}) collective-permute-start(bf16[2048,128]{1,0:T(8,128)(2,1)S(1)} %collective-permute-done.8), channel_id=1, source_target_pairs={{0,1},{1,0},{2,3},{3,2},{4,5},{5,4},{6,7},{7,6},{8,9},{9,8},{10,11... | collective-permute-start | bytes 1572872 | tf_op jit(solution)/shard_map/ppermute | solution.py:278
  47.7 3.8 %collective-permute-done.4.refs_2_ = bf16[2048,128]{1,0:T(8,128)(2,1)S(1)} collective-permute-done((bf16[2048,128]{1,0:T(8,128)(2,1)S(1)}, bf16[2048,128]{1,0:T(8,128)(2,1)S(1)}, u32[]{:S(2)}, u32[]{:S(2)}) %collective-permute-start.4) | collective-permute-done | bytes 524320 | tf_op jit(solution)/shard_map/ppermute | solution.py:288
  51.5 4.1 %partners_far.1 = f32[136,1024]{1,0:T(8,128)S(1)} custom-call(s32[1]{0:T(128)} %bitcast.core_ref, s32[1,2]{1,0:T(1,128)S(1)} %pad_add_fusion.here, s32[1,2]{1,0:T(1,128)S(1)} %collective-permute-done.1.there, bf16[128,2048]{1,0:T(8,128)(2,1)S(1)} %get-tuple-element.20.rows_t, f32[1,2048]{1,0:T(1,128)S(1)} %get-tuple-element.21.row_norms, ...), custom_call_target="tpu_custom_call" | custom-call | flops 1073741824 | bytes 3145728 | tf_op jit(solution)/shard_map/partners_far/pallas_call | solution.py:164
  55.6 2.8 %collective-permute-start.10 = (f32[136,1024]{1,0:T(8,128)S(1)}, f32[136,1024]{1,0:T(8,128)S(1)}, u32[]{:S(2)}, u32[]{:S(2)}) collective-permute-start(f32[136,1024]{1,0:T(8,128)S(1)} %partners_far.1), channel_id=1, source_target_pairs={{0,1},{1,0},{2,3},{3,2},{4,5},{5,4},{6,7},{7,6},{8,9},{9,8},{10,11... | collective-permute-start | bytes 1671176 | tf_op jit(solution)/shard_map/ppermute | solution.py:278
  58.4 4.1 %partners_near.1.sums = f32[136,1024]{1,0:T(8,128)S(1)} custom-call(s32[1]{0:T(128)} %bitcast.core_ref, s32[1,2]{1,0:T(1,128)S(1)} %pad_add_fusion.here, s32[1,2]{1,0:T(1,128)S(1)} %collective-permute-done.1.there, bf16[128,2048]{1,0:T(8,128)(2,1)S(1)} %get-tuple-element.20.rows_t, f32[1,2048]{1,0:T(1,128)S(1)} %get-tuple-element.21.row_norms, ...), custom_call_target="tpu_custom_call" | custom-call | flops 1073741824 | bytes 3145728 | tf_op jit(solution)/shard_map/partners_near/pallas_call | solution.py:164
  63.1 1.9 %collective-permute-start.11 = (f32[128,1024]{1,0:T(8,128)S(1)}, f32[128,1024]{1,0:T(8,128)S(1)}, u32[]{:S(2)}, u32[]{:S(2)}) collective-permute-start(f32[128,1024]{1,0:T(8,128)S(1)} %get-tuple-element.24.own), channel_id=1, source_target_pairs={{0,1},{1,0},{2,3},{3,2},{4,5},{5,4},{6,7},{7,6},{8,9},{9,8},{10,11... | collective-permute-start | bytes 1572872 | tf_op jit(solution)/shard_map/ppermute | solution.py:278
  65.0 25.3 %all_to_all.15 = f32[16,8,128]{2,1,0:T(8,128)S(1)} all-to-all(f32[16,8,128]{2,1,0:T(8,128)S(1)} %get-tuple-element.25), channel_id=1, replica_groups={{0,32,64,96,128,160,192,224,256,288,320,352,384,416,448,480},{2,34,66,9..., dimensions={0} | all-to-all | bytes 131072 | tf_op jit(solution)/shard_map/all_to_all | solution.py:263
  90.4 3.8 %collective-permute-start.12 = (f32[8,128]{1,0:T(8,128)S(1)}, f32[8,128]{1,0:T(8,128)S(1)}, u32[]{:S(2)}, u32[]{:S(2)}) collective-permute-start(f32[8,128]{1,0:T(8,128)S(1)} %reduce_sum.18), channel_id=1, source_target_pairs={{0,1},{1,0},{2,3},{3,2},{4,5},{5,4},{6,7},{7,6},{8,9},{9,8},{10,11... | collective-permute-start | bytes 12296 | tf_op jit(solution)/shard_map/ppermute | solution.py:278
  95.1 15.7 %all_to_all.16 = f32[16,8,128]{2,1,0:T(8,128)S(1)} all-to-all(f32[16,8,128]{2,1,0:T(8,128)S(1)} %broadcast_in_dim.6), channel_id=1, replica_groups={{0,2,4,6,8,10,12,14,16,18,20,22,24,26,28,30},{32,34,36,38,40,42,44,46,4..., dimensions={0} | all-to-all | bytes 131072 | tf_op jit(solution)/shard_map/all_to_all | solution.py:263
  110.8 9.4 %all_to_all.17.tiles = f32[16,8,128]{2,1,0:T(8,128)S(1)} all-to-all(f32[16,8,128]{2,1,0:T(8,128)S(1)} %broadcast_in_dim.7), channel_id=1, replica_groups={{0,32,64,96,128,160,192,224,256,288,320,352,384,416,448,480},{2,34,66,9..., dimensions={0} | all-to-all | bytes 131072 | tf_op jit(solution)/shard_map/all_to_all | solution.py:263
  (21 shorter events, 3.6 us)
Async XLA Ops:
  0.6 15.3 %copy-start = (bf16[2048,128]{1,0:T(8,128)(2,1)S(1)}, bf16[2048,128]{1,0:T(8,128)(2,1)}, u32[]{:S(2)}) copy-start(bf16[2048,128]{1,0:T(8,128)(2,1)} %feats_ref.3) | copy-start | bytes 1572868
  3.2 18.6 %collective-permute-start = (bf16[2048,128]{1,0:T(8,128)(2,1)}, bf16[2048,128]{1,0:T(8,128)(2,1)S(1)}, u32[]{:S(2)}, u32[]{:S(2)}) collective-permute-start(bf16[2048,128]{1,0:T(8,128)(2,1)} %get-tuple-element.14), channel_id=1, source_target_pairs={{0,2},{3,1},{2,4},{5,3},{4,6},{7,5},{6,8},{9,7},{8,10},{11,9},{10,... | collective-permute-start | bytes 1572872 | tf_op jit(solution)/shard_map/ppermute | solution.py:288
  5.8 15.9 %collective-permute-start.1 = (s32[1,2]{1,0:T(1,128)S(1)}, s32[1,2]{1,0:T(1,128)S(1)}, u32[]{:S(2)}, u32[]{:S(2)}) collective-permute-start(s32[1,2]{1,0:T(1,128)S(1)} %pad_add_fusion.here), channel_id=1, source_target_pairs={{0,1},{1,0},{2,3},{3,2},{4,5},{5,4},{6,7},{7,6},{8,9},{9,8},{10,11... | collective-permute-start | bytes 32 | tf_op jit(solution)/shard_map/ppermute | solution.py:278
  14.6 10.1 %collective-permute-start.2 = (bf16[2048,128]{1,0:T(8,128)(2,1)}, bf16[2048,128]{1,0:T(8,128)(2,1)S(1)}, u32[]{:S(2)}, u32[]{:S(2)}) collective-permute-start(bf16[2048,128]{1,0:T(8,128)(2,1)} %get-tuple-element.15.packed), channel_id=1, source_target_pairs={{0,2},{3,1},{2,4},{5,3},{4,6},{7,5},{6,8},{9,7},{8,10},{11,9},{10,... | collective-permute-start | bytes 1572872 | tf_op jit(solution)/shard_map/ppermute | solution.py:288
  15.9 1.0 copy-start.1
  21.8 10.6 %collective-permute-start.6 = (bf16[2048,128]{1,0:T(8,128)(2,1)S(1)}, bf16[2048,128]{1,0:T(8,128)(2,1)S(1)}, u32[]{:S(2)}, u32[]{:S(2)}) collective-permute-start(bf16[2048,128]{1,0:T(8,128)(2,1)S(1)} %collective-permute-done), channel_id=1, source_target_pairs={{0,2},{3,1},{2,4},{5,3},{4,6},{7,5},{6,8},{9,7},{8,10},{11,9},{10,... | collective-permute-start | bytes 1572872 | tf_op jit(solution)/shard_map/ppermute | solution.py:288
  24.8 16.1 %collective-permute-start.3 = (bf16[2048,128]{1,0:T(8,128)(2,1)S(1)}, bf16[2048,128]{1,0:T(8,128)(2,1)S(1)}, u32[]{:S(2)}, u32[]{:S(2)}) collective-permute-start(bf16[2048,128]{1,0:T(8,128)(2,1)S(1)} %collective-permute-done.2.refs_0_), channel_id=1, source_target_pairs={{0,2},{3,1},{2,4},{5,3},{4,6},{7,5},{6,8},{9,7},{8,10},{11,9},{10,... | collective-permute-start | bytes 1572872 | tf_op jit(solution)/shard_map/ppermute | solution.py:288
  32.3 11.2 %collective-permute-start.8 = (bf16[2048,128]{1,0:T(8,128)(2,1)S(1)}, bf16[2048,128]{1,0:T(8,128)(2,1)S(1)}, u32[]{:S(2)}, u32[]{:S(2)}) collective-permute-start(bf16[2048,128]{1,0:T(8,128)(2,1)S(1)} %collective-permute-done.6), channel_id=1, source_target_pairs={{0,2},{3,1},{2,4},{5,3},{4,6},{7,5},{6,8},{9,7},{8,10},{11,9},{10,... | collective-permute-start | bytes 1572872 | tf_op jit(solution)/shard_map/ppermute | solution.py:288
  33.6 14.1 %collective-permute-start.5 = (bf16[2048,128]{1,0:T(8,128)(2,1)S(1)}, bf16[2048,128]{1,0:T(8,128)(2,1)S(1)}, u32[]{:S(2)}, u32[]{:S(2)}) collective-permute-start(bf16[2048,128]{1,0:T(8,128)(2,1)S(1)} %collective-permute-done), channel_id=1, source_target_pairs={{0,1},{1,0},{2,3},{3,2},{4,5},{5,4},{6,7},{7,6},{8,9},{9,8},{10,11... | collective-permute-start | bytes 1572872 | tf_op jit(solution)/shard_map/ppermute | solution.py:278
  38.9 12.6 %collective-permute-start.7 = (bf16[2048,128]{1,0:T(8,128)(2,1)S(1)}, bf16[2048,128]{1,0:T(8,128)(2,1)S(1)}, u32[]{:S(2)}, u32[]{:S(2)}) collective-permute-start(bf16[2048,128]{1,0:T(8,128)(2,1)S(1)} %collective-permute-done.6), channel_id=1, source_target_pairs={{0,1},{1,0},{2,3},{3,2},{4,5},{5,4},{6,7},{7,6},{8,9},{9,8},{10,11... | collective-permute-start | bytes 1572872 | tf_op jit(solution)/shard_map/ppermute | solution.py:278
  40.9 10.6 %collective-permute-start.4 = (bf16[2048,128]{1,0:T(8,128)(2,1)S(1)}, bf16[2048,128]{1,0:T(8,128)(2,1)S(1)}, u32[]{:S(2)}, u32[]{:S(2)}) collective-permute-start(bf16[2048,128]{1,0:T(8,128)(2,1)S(1)} %collective-permute-done.3.refs_1_), channel_id=1, source_target_pairs={{0,2},{3,1},{2,4},{5,3},{4,6},{7,5},{6,8},{9,7},{8,10},{11,9},{10,... | collective-permute-start | bytes 1572872 | tf_op jit(solution)/shard_map/ppermute | solution.py:288
  43.6 8.0 %collective-permute-start.9 = (bf16[2048,128]{1,0:T(8,128)(2,1)S(1)}, bf16[2048,128]{1,0:T(8,128)(2,1)S(1)}, u32[]{:S(2)}, u32[]{:S(2)}) collective-permute-start(bf16[2048,128]{1,0:T(8,128)(2,1)S(1)} %collective-permute-done.8), channel_id=1, source_target_pairs={{0,1},{1,0},{2,3},{3,2},{4,5},{5,4},{6,7},{7,6},{8,9},{9,8},{10,11... | collective-permute-start | bytes 1572872 | tf_op jit(solution)/shard_map/ppermute | solution.py:278
  55.6 6.9 %collective-permute-start.10 = (f32[136,1024]{1,0:T(8,128)S(1)}, f32[136,1024]{1,0:T(8,128)S(1)}, u32[]{:S(2)}, u32[]{:S(2)}) collective-permute-start(f32[136,1024]{1,0:T(8,128)S(1)} %partners_far.1), channel_id=1, source_target_pairs={{0,1},{1,0},{2,3},{3,2},{4,5},{5,4},{6,7},{7,6},{8,9},{9,8},{10,11... | collective-permute-start | bytes 1671176 | tf_op jit(solution)/shard_map/ppermute | solution.py:278
  63.1 57.1 %collective-permute-start.11 = (f32[128,1024]{1,0:T(8,128)S(1)}, f32[128,1024]{1,0:T(8,128)S(1)}, u32[]{:S(2)}, u32[]{:S(2)}) collective-permute-start(f32[128,1024]{1,0:T(8,128)S(1)} %get-tuple-element.24.own), channel_id=1, source_target_pairs={{0,1},{1,0},{2,3},{3,2},{4,5},{5,4},{6,7},{7,6},{8,9},{9,8},{10,11... | collective-permute-start | bytes 1572872 | tf_op jit(solution)/shard_map/ppermute | solution.py:278
  90.4 4.6 %collective-permute-start.12 = (f32[8,128]{1,0:T(8,128)S(1)}, f32[8,128]{1,0:T(8,128)S(1)}, u32[]{:S(2)}, u32[]{:S(2)}) collective-permute-start(f32[8,128]{1,0:T(8,128)S(1)} %reduce_sum.18), channel_id=1, source_target_pairs={{0,1},{1,0},{2,3},{3,2},{4,5},{5,4},{6,7},{7,6},{8,9},{9,8},{10,11... | collective-permute-start | bytes 12296 | tf_op jit(solution)/shard_map/ppermute | solution.py:278

commit v7 on v6

--- a/solution.py
+++ b/solution.py
@@ -292,18 +292,20 @@
     block = features.shape[0]
     core = lax.axis_index("pair").astype(jnp.int32).reshape(1)
     here = jnp.concatenate([offsets, counts], axis=1)
-    there = swap(here)
     give, keep = pack(core, features, subspace)
     own_sums, rows_t, row_norms = apply_self(core, features, keep)
     kept, swapped = [], []
     for step in range(REACH):
         give, keep = relay(give), relay(keep)
         if step == 0:
-            give, there, own_sums, rows_t, row_norms = lax.optimization_barrier(
-                (give, there, own_sums, rows_t, row_norms)
+            give, own_sums, rows_t, row_norms = lax.optimization_barrier(
+                (give, own_sums, rows_t, row_norms)
             )
+        if step == 1:
+            give, swapped[0], here = lax.optimization_barrier((give, swapped[0], here))
         kept.append(keep)
         swapped.append(swap(give))
+    there = swap(here)
     near = kept + swapped
     far = apply_partners("far", core, here, there, rows_t, row_norms, own_sums, near)
     far_sums = swap(far)

time: 123 us -> 120 us (0.976)
  starting transfers between devices: 36.4 us -> 32 us
    ppermute x7, starting transfers between devices: 28.7 us -> 24.2 us  [swap(): return lax.ppermute(x, 'pair', [(0, 1), (1, 0)])]
  transfers between devices with their start and end apart: 13 -> 13, of which waited for: 5 -> 6; matrix products, arithmetic and copies ran while one was open for 0% -> 0% of each run, Pallas kernels for 7% -> 7%
where the time goes in v7:
time: 120 us; the launch traced here: 119 us
  blocking collectives  51.6 us (43%)
  starting transfers between devices  32 us (27%)
  Pallas kernels  17.1 us (14%)
  waiting for transfers between devices  14.8 us (12%)
  between operations  2.12 us (2%)
    all_to_all x3, blocking collectives, exchange(): lax.all_to_all(tiles, 'blk', 0, 0, axis_index_groups=groups, tiled=True)  51.6 us
    ppermute x7, starting transfers between devices, swap(): return lax.ppermute(x, 'pair', [(0, 1), (1, 0)])  24.2 us
    ppermute x6, waiting for transfers between devices, relay(): return lax.ppermute(x, ('blk', 'pair'), pairs)  12.9 us
    pallas_call x2, Pallas kernels, apply_partners(): pl.pallas_call(partner_kernel, grid_spec=pltpu.PrefetchScalarGridSpec(num...  8.12 us
    ppermute x6, starting transfers between devices, relay(): return lax.ppermute(x, ('blk', 'pair'), pairs)  7.72 us
    pallas_call x1, Pallas kernels, apply_self(): pl.pallas_call(self_kernel, grid_spec=pltpu.PrefetchScalarGridSpec(num_sc...  4.79 us
    pallas_call x1, Pallas kernels, pack(): pl.pallas_call(pack_kernel, grid_spec=pltpu.PrefetchScalarGridSpec(num_sc...  2.51 us
  transfers between devices with their start and end apart: 13, of which 6 were waited for; matrix products, arithmetic and copies ran while one was open for 0% of the time, Pallas kernels for 7%

profile of v7, /device:TPU:1, one launch (start us, length us, event | category | flops | bytes accessed | tf_op | source)
XLA Modules:
  0.0 118.7 jit_solution(12209899218817511592)
XLA Ops:
  0.6 2.5 %pack.1 = (bf16[2048,128]{1,0:T(8,128)(2,1)}, bf16[2048,128]{1,0:T(8,128)(2,1)}) custom-call(s32[1]{0:T(128)} %bitcast.core_ref, bf16[2048,128]{1,0:T(8,128)(2,1)} %feats_ref.3, f32[128,2048]{1,0:T(8,128)} %field_ref.1), custom_call_target="tpu_custom_call" | custom-call | bytes 2097152 | tf_op jit(solution)/shard_map/pack/pallas_call | solution.py:34
  3.2 1.3 %collective-permute-start = (bf16[2048,128]{1,0:T(8,128)(2,1)}, bf16[2048,128]{1,0:T(8,128)(2,1)S(1)}, u32[]{:S(2)}, u32[]{:S(2)}) collective-permute-start(bf16[2048,128]{1,0:T(8,128)(2,1)} %get-tuple-element.16), channel_id=1, source_target_pairs={{0,2},{3,1},{2,4},{5,3},{4,6},{7,5},{6,8},{9,7},{8,10},{11,9},{10,... | collective-permute-start | bytes 1572872 | tf_op jit(solution)/shard_map/ppermute | solution.py:288
  4.4 1.3 %collective-permute-start.4 = (bf16[2048,128]{1,0:T(8,128)(2,1)}, bf16[2048,128]{1,0:T(8,128)(2,1)S(1)}, u32[]{:S(2)}, u32[]{:S(2)}) collective-permute-start(bf16[2048,128]{1,0:T(8,128)(2,1)} %get-tuple-element.17.packed), channel_id=1, source_target_pairs={{0,2},{3,1},{2,4},{5,3},{4,6},{7,5},{6,8},{9,7},{8,10},{11,9},{10,... | collective-permute-start | bytes 1572872 | tf_op jit(solution)/shard_map/ppermute | solution.py:288
  6.8 4.8 %own_block.1 = (f32[136,2048]{1,0:T(8,128)S(1)}, bf16[128,2048]{1,0:T(8,128)(2,1)S(1)}, f32[1,2048]{1,0:T(1,128)S(1)}) custom-call(s32[1]{0:T(128)} %bitcast.core_ref, bf16[2048,128]{1,0:T(8,128)(2,1)S(1)} %copy-done, bf16[2048,128]{1,0:T(8,128)(2,1)S(1)} %copy-done.1), custom_call_target="tpu_custom_call" | custom-call | flops 1073741824 | bytes 4194304 | tf_op jit(solution)/shard_map/own_block/pallas_call | solution.py:107
  11.6 2.7 %collective-permute-done = bf16[2048,128]{1,0:T(8,128)(2,1)S(1)} collective-permute-done((bf16[2048,128]{1,0:T(8,128)(2,1)}, bf16[2048,128]{1,0:T(8,128)(2,1)S(1)}, u32[]{:S(2)}, u32[]{:S(2)}) %collective-permute-start) | collective-permute-done | bytes 524320 | tf_op jit(solution)/shard_map/ppermute | solution.py:288
  14.3 6.2 %collective-permute-start.2 = (bf16[2048,128]{1,0:T(8,128)(2,1)S(1)}, bf16[2048,128]{1,0:T(8,128)(2,1)S(1)}, u32[]{:S(2)}, u32[]{:S(2)}) collective-permute-start(bf16[2048,128]{1,0:T(8,128)(2,1)S(1)} %collective-permute-done), channel_id=1, source_target_pairs={{0,1},{1,0},{2,3},{3,2},{4,5},{5,4},{6,7},{7,6},{8,9},{9,8},{10,11... | collective-permute-start | bytes 1572872 | tf_op jit(solution)/shard_map/ppermute | solution.py:278
  20.5 1.3 %collective-permute-start.1 = (bf16[2048,128]{1,0:T(8,128)(2,1)S(1)}, bf16[2048,128]{1,0:T(8,128)(2,1)S(1)}, u32[]{:S(2)}, u32[]{:S(2)}) collective-permute-start(bf16[2048,128]{1,0:T(8,128)(2,1)S(1)} %collective-permute-done), channel_id=1, source_target_pairs={{0,2},{3,1},{2,4},{5,3},{4,6},{7,5},{6,8},{9,7},{8,10},{11,9},{10,... | collective-permute-start | bytes 1572872 | tf_op jit(solution)/shard_map/ppermute | solution.py:288
  23.1 1.3 %collective-permute-start.5 = (bf16[2048,128]{1,0:T(8,128)(2,1)S(1)}, bf16[2048,128]{1,0:T(8,128)(2,1)S(1)}, u32[]{:S(2)}, u32[]{:S(2)}) collective-permute-start(bf16[2048,128]{1,0:T(8,128)(2,1)S(1)} %collective-permute-done.4.refs_0_), channel_id=1, source_target_pairs={{0,2},{3,1},{2,4},{5,3},{4,6},{7,5},{6,8},{9,7},{8,10},{11,9},{10,... | collective-permute-start | bytes 1572872 | tf_op jit(solution)/shard_map/ppermute | solution.py:288
  24.4 6.4 %collective-permute-done.1 = bf16[2048,128]{1,0:T(8,128)(2,1)S(1)} collective-permute-done((bf16[2048,128]{1,0:T(8,128)(2,1)S(1)}, bf16[2048,128]{1,0:T(8,128)(2,1)S(1)}, u32[]{:S(2)}, u32[]{:S(2)}) %collective-permute-start.1) | collective-permute-done | bytes 524320 | tf_op jit(solution)/shard_map/ppermute | solution.py:288
  30.8 1.3 %collective-permute-start.8 = (bf16[2048,128]{1,0:T(8,128)(2,1)S(1)}, bf16[2048,128]{1,0:T(8,128)(2,1)S(1)}, u32[]{:S(2)}, u32[]{:S(2)}) collective-permute-start(bf16[2048,128]{1,0:T(8,128)(2,1)S(1)} %collective-permute-done.1), channel_id=1, source_target_pairs={{0,2},{3,1},{2,4},{5,3},{4,6},{7,5},{6,8},{9,7},{8,10},{11,9},{10,... | collective-permute-start | bytes 1572872 | tf_op jit(solution)/shard_map/ppermute | solution.py:288
  32.1 5.5 %collective-permute-start.7 = (bf16[2048,128]{1,0:T(8,128)(2,1)S(1)}, bf16[2048,128]{1,0:T(8,128)(2,1)S(1)}, u32[]{:S(2)}, u32[]{:S(2)}) collective-permute-start(bf16[2048,128]{1,0:T(8,128)(2,1)S(1)} %collective-permute-done.1), channel_id=1, source_target_pairs={{0,1},{1,0},{2,3},{3,2},{4,5},{5,4},{6,7},{7,6},{8,9},{9,8},{10,11... | collective-permute-start | bytes 1572872 | tf_op jit(solution)/shard_map/ppermute | solution.py:278
  37.6 1.3 %collective-permute-start.6 = (bf16[2048,128]{1,0:T(8,128)(2,1)S(1)}, bf16[2048,128]{1,0:T(8,128)(2,1)S(1)}, u32[]{:S(2)}, u32[]{:S(2)}) collective-permute-start(bf16[2048,128]{1,0:T(8,128)(2,1)S(1)} %collective-permute-done.5.refs_1_), channel_id=1, source_target_pairs={{0,2},{3,1},{2,4},{5,3},{4,6},{7,5},{6,8},{9,7},{8,10},{11,9},{10,... | collective-permute-start | bytes 1572872 | tf_op jit(solution)/shard_map/ppermute | solution.py:288
  38.9 3.1 %collective-permute-done.8 = bf16[2048,128]{1,0:T(8,128)(2,1)S(1)} collective-permute-done((bf16[2048,128]{1,0:T(8,128)(2,1)S(1)}, bf16[2048,128]{1,0:T(8,128)(2,1)S(1)}, u32[]{:S(2)}, u32[]{:S(2)}) %collective-permute-start.8) | collective-permute-done | bytes 524320 | tf_op jit(solution)/shard_map/ppermute | solution.py:288
  42.0 2.5 %collective-permute-start.9 = (bf16[2048,128]{1,0:T(8,128)(2,1)S(1)}, bf16[2048,128]{1,0:T(8,128)(2,1)S(1)}, u32[]{:S(2)}, u32[]{:S(2)}) collective-permute-start(bf16[2048,128]{1,0:T(8,128)(2,1)S(1)} %collective-permute-done.8), channel_id=1, source_target_pairs={{0,1},{1,0},{2,3},{3,2},{4,5},{5,4},{6,7},{7,6},{8,9},{9,8},{10,11... | collective-permute-start | bytes 1572872 | tf_op jit(solution)/shard_map/ppermute | solution.py:278
  44.5 1.9 %collective-permute-start.3 = (s32[1,2]{1,0:T(1,128)S(1)}, s32[1,2]{1,0:T(1,128)S(1)}, u32[]{:S(2)}, u32[]{:S(2)}) collective-permute-start(s32[1,2]{1,0:T(1,128)S(1)} %pad_add_fusion.here), channel_id=1, source_target_pairs={{0,1},{1,0},{2,3},{3,2},{4,5},{5,4},{6,7},{7,6},{8,9},{9,8},{10,11... | collective-permute-start | bytes 32 | tf_op jit(solution)/shard_map/ppermute | solution.py:278
  46.5 1.1 collective-permute-done.3.there
  48.3 4.1 %partners_far.1 = f32[136,1024]{1,0:T(8,128)S(1)} custom-call(s32[1]{0:T(128)} %bitcast.core_ref, s32[1,2]{1,0:T(1,128)S(1)} %pad_add_fusion.here, s32[1,2]{1,0:T(1,128)S(1)} %collective-permute-done.3.there, bf16[128,2048]{1,0:T(8,128)(2,1)S(1)} %get-tuple-element.23.rows_t, f32[1,2048]{1,0:T(1,128)S(1)} %get-tuple-element.24.row_norms, ...), custom_call_target="tpu_custom_call" | custom-call | flops 1073741824 | bytes 3145728 | tf_op jit(solution)/shard_map/partners_far/pallas_call | solution.py:164
  52.3 2.3 %collective-permute-start.10 = (f32[136,1024]{1,0:T(8,128)S(1)}, f32[136,1024]{1,0:T(8,128)S(1)}, u32[]{:S(2)}, u32[]{:S(2)}) collective-permute-start(f32[136,1024]{1,0:T(8,128)S(1)} %partners_far.1), channel_id=1, source_target_pairs={{0,1},{1,0},{2,3},{3,2},{4,5},{5,4},{6,7},{7,6},{8,9},{9,8},{10,11... | collective-permute-start | bytes 1671176 | tf_op jit(solution)/shard_map/ppermute | solution.py:278
  54.6 4.1 %partners_near.1.sums = f32[136,1024]{1,0:T(8,128)S(1)} custom-call(s32[1]{0:T(128)} %bitcast.core_ref, s32[1,2]{1,0:T(1,128)S(1)} %pad_add_fusion.here, s32[1,2]{1,0:T(1,128)S(1)} %collective-permute-done.3.there, bf16[128,2048]{1,0:T(8,128)(2,1)S(1)} %get-tuple-element.23.rows_t, f32[1,2048]{1,0:T(1,128)S(1)} %get-tuple-element.24.row_norms, ...), custom_call_target="tpu_custom_call" | custom-call | flops 1073741824 | bytes 3145728 | tf_op jit(solution)/shard_map/partners_near/pallas_call | solution.py:164
  59.4 2.0 %collective-permute-start.11 = (f32[128,1024]{1,0:T(8,128)S(1)}, f32[128,1024]{1,0:T(8,128)S(1)}, u32[]{:S(2)}, u32[]{:S(2)}) collective-permute-start(f32[128,1024]{1,0:T(8,128)S(1)} %get-tuple-element.28.own), channel_id=1, source_target_pairs={{0,1},{1,0},{2,3},{3,2},{4,5},{5,4},{6,7},{7,6},{8,9},{9,8},{10,11... | collective-permute-start | bytes 1572872 | tf_op jit(solution)/shard_map/ppermute | solution.py:278
  61.4 27.3 %all_to_all.15 = f32[16,8,128]{2,1,0:T(8,128)S(1)} all-to-all(f32[16,8,128]{2,1,0:T(8,128)S(1)} %get-tuple-element.29), channel_id=1, replica_groups={{0,32,64,96,128,160,192,224,256,288,320,352,384,416,448,480},{2,34,66,9..., dimensions={0} | all-to-all | bytes 131072 | tf_op jit(solution)/shard_map/all_to_all | solution.py:263
  88.7 3.8 %collective-permute-start.12 = (f32[8,128]{1,0:T(8,128)S(1)}, f32[8,128]{1,0:T(8,128)S(1)}, u32[]{:S(2)}, u32[]{:S(2)}) collective-permute-start(f32[8,128]{1,0:T(8,128)S(1)} %reduce_sum.18), channel_id=1, source_target_pairs={{0,1},{1,0},{2,3},{3,2},{4,5},{5,4},{6,7},{7,6},{8,9},{9,8},{10,11... | collective-permute-start | bytes 12296 | tf_op jit(solution)/shard_map/ppermute | solution.py:278
  93.4 14.9 %all_to_all.16 = f32[16,8,128]{2,1,0:T(8,128)S(1)} all-to-all(f32[16,8,128]{2,1,0:T(8,128)S(1)} %broadcast_in_dim.6), channel_id=1, replica_groups={{0,2,4,6,8,10,12,14,16,18,20,22,24,26,28,30},{32,34,36,38,40,42,44,46,4..., dimensions={0} | all-to-all | bytes 131072 | tf_op jit(solution)/shard_map/all_to_all | solution.py:263
  108.3 9.4 %all_to_all.17.tiles = f32[16,8,128]{2,1,0:T(8,128)S(1)} all-to-all(f32[16,8,128]{2,1,0:T(8,128)S(1)} %broadcast_in_dim.7), channel_id=1, replica_groups={{0,32,64,96,128,160,192,224,256,288,320,352,384,416,448,480},{2,34,66,9..., dimensions={0} | all-to-all | bytes 131072 | tf_op jit(solution)/shard_map/all_to_all | solution.py:263
  (21 shorter events, 4.3 us)
Async XLA Ops:
  0.6 5.1 %copy-start = (bf16[2048,128]{1,0:T(8,128)(2,1)S(1)}, bf16[2048,128]{1,0:T(8,128)(2,1)}, u32[]{:S(2)}) copy-start(bf16[2048,128]{1,0:T(8,128)(2,1)} %feats_ref.3) | copy-start | bytes 1572868
  3.2 11.1 %collective-permute-start = (bf16[2048,128]{1,0:T(8,128)(2,1)}, bf16[2048,128]{1,0:T(8,128)(2,1)S(1)}, u32[]{:S(2)}, u32[]{:S(2)}) collective-permute-start(bf16[2048,128]{1,0:T(8,128)(2,1)} %get-tuple-element.16), channel_id=1, source_target_pairs={{0,2},{3,1},{2,4},{5,3},{4,6},{7,5},{6,8},{9,7},{8,10},{11,9},{10,... | collective-permute-start | bytes 1572872 | tf_op jit(solution)/shard_map/ppermute | solution.py:288
  4.4 18.7 %collective-permute-start.4 = (bf16[2048,128]{1,0:T(8,128)(2,1)}, bf16[2048,128]{1,0:T(8,128)(2,1)S(1)}, u32[]{:S(2)}, u32[]{:S(2)}) collective-permute-start(bf16[2048,128]{1,0:T(8,128)(2,1)} %get-tuple-element.17.packed), channel_id=1, source_target_pairs={{0,2},{3,1},{2,4},{5,3},{4,6},{7,5},{6,8},{9,7},{8,10},{11,9},{10,... | collective-permute-start | bytes 1572872 | tf_op jit(solution)/shard_map/ppermute | solution.py:288
  5.8 1.0 copy-start.1
  14.3 10.1 %collective-permute-start.2 = (bf16[2048,128]{1,0:T(8,128)(2,1)S(1)}, bf16[2048,128]{1,0:T(8,128)(2,1)S(1)}, u32[]{:S(2)}, u32[]{:S(2)}) collective-permute-start(bf16[2048,128]{1,0:T(8,128)(2,1)S(1)} %collective-permute-done), channel_id=1, source_target_pairs={{0,1},{1,0},{2,3},{3,2},{4,5},{5,4},{6,7},{7,6},{8,9},{9,8},{10,11... | collective-permute-start | bytes 1572872 | tf_op jit(solution)/shard_map/ppermute | solution.py:278
  20.5 10.3 %collective-permute-start.1 = (bf16[2048,128]{1,0:T(8,128)(2,1)S(1)}, bf16[2048,128]{1,0:T(8,128)(2,1)S(1)}, u32[]{:S(2)}, u32[]{:S(2)}) collective-permute-start(bf16[2048,128]{1,0:T(8,128)(2,1)S(1)} %collective-permute-done), channel_id=1, source_target_pairs={{0,2},{3,1},{2,4},{5,3},{4,6},{7,5},{6,8},{9,7},{8,10},{11,9},{10,... | collective-permute-start | bytes 1572872 | tf_op jit(solution)/shard_map/ppermute | solution.py:288
  23.1 14.5 %collective-permute-start.5 = (bf16[2048,128]{1,0:T(8,128)(2,1)S(1)}, bf16[2048,128]{1,0:T(8,128)(2,1)S(1)}, u32[]{:S(2)}, u32[]{:S(2)}) collective-permute-start(bf16[2048,128]{1,0:T(8,128)(2,1)S(1)} %collective-permute-done.4.refs_0_), channel_id=1, source_target_pairs={{0,2},{3,1},{2,4},{5,3},{4,6},{7,5},{6,8},{9,7},{8,10},{11,9},{10,... | collective-permute-start | bytes 1572872 | tf_op jit(solution)/shard_map/ppermute | solution.py:288
  30.8 11.2 %collective-permute-start.8 = (bf16[2048,128]{1,0:T(8,128)(2,1)S(1)}, bf16[2048,128]{1,0:T(8,128)(2,1)S(1)}, u32[]{:S(2)}, u32[]{:S(2)}) collective-permute-start(bf16[2048,128]{1,0:T(8,128)(2,1)S(1)} %collective-permute-done.1), channel_id=1, source_target_pairs={{0,2},{3,1},{2,4},{5,3},{4,6},{7,5},{6,8},{9,7},{8,10},{11,9},{10,... | collective-permute-start | bytes 1572872 | tf_op jit(solution)/shard_map/ppermute | solution.py:288
  32.1 16.2 %collective-permute-start.7 = (bf16[2048,128]{1,0:T(8,128)(2,1)S(1)}, bf16[2048,128]{1,0:T(8,128)(2,1)S(1)}, u32[]{:S(2)}, u32[]{:S(2)}) collective-permute-start(bf16[2048,128]{1,0:T(8,128)(2,1)S(1)} %collective-permute-done.1), channel_id=1, source_target_pairs={{0,1},{1,0},{2,3},{3,2},{4,5},{5,4},{6,7},{7,6},{8,9},{9,8},{10,11... | collective-permute-start | bytes 1572872 | tf_op jit(solution)/shard_map/ppermute | solution.py:278
  37.6 10.6 %collective-permute-start.6 = (bf16[2048,128]{1,0:T(8,128)(2,1)S(1)}, bf16[2048,128]{1,0:T(8,128)(2,1)S(1)}, u32[]{:S(2)}, u32[]{:S(2)}) collective-permute-start(bf16[2048,128]{1,0:T(8,128)(2,1)S(1)} %collective-permute-done.5.refs_1_), channel_id=1, source_target_pairs={{0,2},{3,1},{2,4},{5,3},{4,6},{7,5},{6,8},{9,7},{8,10},{11,9},{10,... | collective-permute-start | bytes 1572872 | tf_op jit(solution)/shard_map/ppermute | solution.py:288
  42.0 6.2 %collective-permute-start.9 = (bf16[2048,128]{1,0:T(8,128)(2,1)S(1)}, bf16[2048,128]{1,0:T(8,128)(2,1)S(1)}, u32[]{:S(2)}, u32[]{:S(2)}) collective-permute-start(bf16[2048,128]{1,0:T(8,128)(2,1)S(1)} %collective-permute-done.8), channel_id=1, source_target_pairs={{0,1},{1,0},{2,3},{3,2},{4,5},{5,4},{6,7},{7,6},{8,9},{9,8},{10,11... | collective-permute-start | bytes 1572872 | tf_op jit(solution)/shard_map/ppermute | solution.py:278
  44.5 3.0 %collective-permute-start.3 = (s32[1,2]{1,0:T(1,128)S(1)}, s32[1,2]{1,0:T(1,128)S(1)}, u32[]{:S(2)}, u32[]{:S(2)}) collective-permute-start(s32[1,2]{1,0:T(1,128)S(1)} %pad_add_fusion.here), channel_id=1, source_target_pairs={{0,1},{1,0},{2,3},{3,2},{4,5},{5,4},{6,7},{7,6},{8,9},{9,8},{10,11... | collective-permute-start | bytes 32 | tf_op jit(solution)/shard_map/ppermute | solution.py:278
  52.3 6.4 %collective-permute-start.10 = (f32[136,1024]{1,0:T(8,128)S(1)}, f32[136,1024]{1,0:T(8,128)S(1)}, u32[]{:S(2)}, u32[]{:S(2)}) collective-permute-start(f32[136,1024]{1,0:T(8,128)S(1)} %partners_far.1), channel_id=1, source_target_pairs={{0,1},{1,0},{2,3},{3,2},{4,5},{5,4},{6,7},{7,6},{8,9},{9,8},{10,11... | collective-permute-start | bytes 1671176 | tf_op jit(solution)/shard_map/ppermute | solution.py:278
  59.4 58.3 %collective-permute-start.11 = (f32[128,1024]{1,0:T(8,128)S(1)}, f32[128,1024]{1,0:T(8,128)S(1)}, u32[]{:S(2)}, u32[]{:S(2)}) collective-permute-start(f32[128,1024]{1,0:T(8,128)S(1)} %get-tuple-element.28.own), channel_id=1, source_target_pairs={{0,1},{1,0},{2,3},{3,2},{4,5},{5,4},{6,7},{7,6},{8,9},{9,8},{10,11... | collective-permute-start | bytes 1572872 | tf_op jit(solution)/shard_map/ppermute | solution.py:278
  88.7 4.6 %collective-permute-start.12 = (f32[8,128]{1,0:T(8,128)S(1)}, f32[8,128]{1,0:T(8,128)S(1)}, u32[]{:S(2)}, u32[]{:S(2)}) collective-permute-start(f32[8,128]{1,0:T(8,128)S(1)} %reduce_sum.18), channel_id=1, source_target_pairs={{0,1},{1,0},{2,3},{3,2},{4,5},{5,4},{6,7},{7,6},{8,9},{9,8},{10,11... | collective-permute-start | bytes 12296 | tf_op jit(solution)/shard_map/ppermute | solution.py:278

commit v8 on v7

--- a/solution.py
+++ b/solution.py
@@ -67,7 +67,7 @@
     return jnp.concatenate([first, second], axis=1)
 
 
-def self_kernel(core_ref, feats_ref, packed, sums, rows_t, row_norms, feats, sem):
+def self_kernel(core_ref, feats_ref, packed, sums, rows, wide_norms, feats, rows_t, row_norms, sem):
     block = feats_ref.shape[0]
     half = block // 2
     copy = pltpu.make_async_copy(feats_ref, feats, sem)
@@ -76,6 +76,10 @@
     copy.wait()
     for at in range(0, block, TILE):
         wide = feats[at : at + TILE, :].astype(jnp.float32).T
+        rows[at : at + TILE, :] = feats[at : at + TILE, :] * (1.0 / 128.0)
+        wide_norms[at : at + TILE, :] = jnp.broadcast_to(
+            norms_of(feats[at : at + TILE, :]), (TILE, wide_norms.shape[1])
+        )
         row_norms[:, at : at + TILE] = jnp.sum(wide * wide, axis=0, keepdims=True) * (1.0 / 256.0)
         rows_t[:, at : at + TILE] = (wide * (1.0 / 128.0)).astype(jnp.bfloat16)
 
@@ -100,8 +104,8 @@
     block, feat = features.shape
     outs = [
         jax.ShapeDtypeStruct((feat + 8, block), jnp.float32),
-        jax.ShapeDtypeStruct((feat, block), jnp.bfloat16),
-        jax.ShapeDtypeStruct((1, block), jnp.float32),
+        jax.ShapeDtypeStruct((block, feat), jnp.bfloat16),
+        jax.ShapeDtypeStruct((block, feat), jnp.float32),
     ]
     whole = lambda i, core: (0, 0)
     return pl.pallas_call(
@@ -111,7 +115,12 @@
             grid=(1,),
             in_specs=[pl.BlockSpec(memory_space=pltpu.HBM), pl.BlockSpec(packed.shape, whole)],
             out_specs=[pl.BlockSpec(x.shape, whole) for x in outs],
-            scratch_shapes=[pltpu.VMEM((block, feat), jnp.bfloat16), pltpu.SemaphoreType.DMA],
+            scratch_shapes=[
+                pltpu.VMEM((block, feat), jnp.bfloat16),
+                pltpu.VMEM((feat, block), jnp.bfloat16),
+                pltpu.VMEM((1, block), jnp.float32),
+                pltpu.SemaphoreType.DMA,
+            ],
         ),
         out_shape=outs,
         compiler_params=PARAMS,
@@ -124,9 +133,10 @@
     )(core, features, packed)
 
 
-def partner_kernel(core_ref, here, there, rows_t, row_norms, own_sums, *refs):
+def partner_kernel(core_ref, here, there, rows, wide_norms, own_sums, *refs):
     near = refs[: 2 * REACH]
-    sums, held, sems = refs[2 * REACH :]
+    sums, acc, deg, held, sems = refs[2 * REACH :]
+    feat = rows.shape[1]
     half = held.shape[1] // 2
     picks = (here, there)
     for turn in range(2):
@@ -139,7 +149,8 @@
             def _():
                 pltpu.make_async_copy(near[slot], held.at[turn], sems.at[turn]).start()
 
-    sums[...] = own_sums[...]
+    acc[...] = jnp.zeros_like(acc)
+    deg[...] = jnp.zeros_like(deg)
     for turn in range(2):
         pltpu.make_async_copy(near[0], held.at[turn], sems.at[turn]).wait()
 
@@ -147,19 +158,34 @@
         def _(step):
             at = pl.multiple_of(step * TILE, TILE)
             part = held[turn, pl.ds(at, TILE), :]
-            ids = core_ref[0] * half + at + lax.broadcasted_iota(jnp.int32, (TILE, 1), 0)
-            norms = jnp.where(ids < picks[turn][0, 1], norms_of(part), FAR)
-            vals = values_at(held.at[turn], half + at)
-            add_columns(part, vals, norms, rows_t[...], row_norms[...], sums)
-
-
-def apply_partners(which, core, here, there, rows_t, row_norms, own_sums, near):
-    feat, block = rows_t.shape
+            wide = part.astype(jnp.float32)
+            norms = jnp.sum((wide * wide).T, axis=0, keepdims=True) * (1.0 / 256.0)
+            ids = core_ref[0] * half + at + lax.broadcasted_iota(jnp.int32, (1, TILE), 1)
+            norms = jnp.where(ids < picks[turn][0, 1], norms, FAR)
+            inner = lax.dot_general(rows[...], part, NT, preferred_element_type=jnp.float32)
+            both = jnp.concatenate([wide_norms[...], wide_norms[...]], axis=1)
+            weight = jnp.exp(inner - norms - both)
+            deg[...] += weight[:, :feat] + weight[:, feat:]
+            acc[...] += lax.dot_general(
+                weight.astype(jnp.bfloat16),
+                values_at(held.at[turn], half + at),
+                NT,
+                preferred_element_type=jnp.float32,
+            )
+
+    sums[:feat, :] = own_sums[:feat, :] + acc[...].T
+    sums[feat:, :] = own_sums[feat:, :] + jnp.sum(
+        deg[...].T.reshape(feat // 8, 8, deg.shape[0]), axis=0
+    )
+
+
+def apply_partners(which, core, here, there, rows, wide_norms, own_sums, near):
+    block, feat = rows.shape
     half = block // 2
     if which == "far":
-        picked = lambda i, core, here, there: (0, 1 - core[0])
+        choose = lambda core: 1 - core[0]
     else:
-        picked = lambda i, core, here, there: (0, core[0])
+        choose = lambda core: core[0]
     out = jax.ShapeDtypeStruct((feat + 8, half), jnp.float32)
     return pl.pallas_call(
         partner_kernel,
@@ -167,13 +193,15 @@
             num_scalar_prefetch=3,
             grid=(1,),
             in_specs=[
-                pl.BlockSpec((feat, half), picked),
-                pl.BlockSpec((1, half), picked),
-                pl.BlockSpec((feat + 8, half), picked),
+                pl.BlockSpec((half, feat), lambda i, core, here, there: (choose(core), 0)),
+                pl.BlockSpec((half, feat), lambda i, core, here, there: (choose(core), 0)),
+                pl.BlockSpec((feat + 8, half), lambda i, core, here, there: (0, choose(core))),
             ]
             + [pl.BlockSpec(memory_space=pl.ANY)] * len(near),
             out_specs=pl.BlockSpec(out.shape, lambda i, core, here, there: (0, 0)),
             scratch_shapes=[
+                pltpu.VMEM((half, feat), jnp.float32),
+                pltpu.VMEM((half, feat), jnp.float32),
                 pltpu.VMEM((2, *near[0].shape), jnp.bfloat16),
                 pltpu.SemaphoreType.DMA((2,)),
             ],
@@ -186,7 +214,7 @@
             transcendentals=half * block,
         ),
         name="partners_" + which,
-    )(core, here, there, rows_t, row_norms, own_sums, *near)
+    )(core, here, there, rows, wide_norms, own_sums, *near)
 
 
 def field_kernel(scale, sums, far_sums, field, gram):
@@ -293,13 +321,13 @@
     core = lax.axis_index("pair").astype(jnp.int32).reshape(1)
     here = jnp.concatenate([offsets, counts], axis=1)
     give, keep = pack(core, features, subspace)
-    own_sums, rows_t, row_norms = apply_self(core, features, keep)
+    own_sums, rows, wide_norms = apply_self(core, features, keep)
     kept, swapped = [], []
     for step in range(REACH):
         give, keep = relay(give), relay(keep)
         if step == 0:
-            give, own_sums, rows_t, row_norms = lax.optimization_barrier(
-                (give, own_sums, rows_t, row_norms)
+            give, own_sums, rows, wide_norms = lax.optimization_barrier(
+                (give, own_sums, rows, wide_norms)
             )
         if step == 1:
             give, swapped[0], here = lax.optimization_barrier((give, swapped[0], here))
@@ -307,9 +335,9 @@
         swapped.append(swap(give))
     there = swap(here)
     near = kept + swapped
-    far = apply_partners("far", core, here, there, rows_t, row_norms, own_sums, near)
+    far = apply_partners("far", core, here, there, rows, wide_norms, own_sums, near)
     far_sums = swap(far)
-    sums = apply_partners("near", core, here, there, rows_t, row_norms, own_sums, near)
+    sums = apply_partners("near", core, here, there, rows, wide_norms, own_sums, near)
     field, gram = make_field(float(lax.axis_size("blk") * block), sums, far_sums)
     other = swap(field)
     return tuple(join(core, field, other, sum_over_all(gram)))

time: 120 us -> 120 us (level)
  no operation moved by 1% of the time
where the time goes in v8:
time: 120 us; the launch traced here: 118 us
  blocking collectives  51.6 us (43%)
  starting transfers between devices  32.8 us (27%)
  Pallas kernels  16.2 us (14%)
  waiting for transfers between devices  13.9 us (12%)
  between operations  2.12 us (2%)
    all_to_all x3, blocking collectives, exchange(): lax.all_to_all(tiles, 'blk', 0, 0, axis_index_groups=groups, tiled=True)  51.6 us
    ppermute x7, starting transfers between devices, swap(): return lax.ppermute(x, 'pair', [(0, 1), (1, 0)])  25.1 us
    ppermute x6, waiting for transfers between devices, relay(): return lax.ppermute(x, ('blk', 'pair'), pairs)  12 us
    ppermute x6, starting transfers between devices, relay(): return lax.ppermute(x, ('blk', 'pair'), pairs)  7.72 us
    pallas_call x2, Pallas kernels, apply_partners(): pl.pallas_call(partner_kernel, grid_spec=pltpu.PrefetchScalarGridSpec(num...  6.98 us
    pallas_call x1, Pallas kernels, apply_self(): pl.pallas_call(self_kernel, grid_spec=pltpu.PrefetchScalarGridSpec(num_sc...  5.1 us
    pallas_call x1, Pallas kernels, pack(): pl.pallas_call(pack_kernel, grid_spec=pltpu.PrefetchScalarGridSpec(num_sc...  2.51 us
  transfers between devices with their start and end apart: 13, of which 6 were waited for; matrix products, arithmetic and copies ran while one was open for 0% of the time, Pallas kernels for 7%

profile of v8, /device:TPU:1, one launch (start us, length us, event | category | flops | bytes accessed | tf_op | source)
XLA Modules:
  0.0 117.9 jit_solution(2877423725446218621)
XLA Ops:
  0.6 2.5 %pack.1 = (bf16[2048,128]{1,0:T(8,128)(2,1)}, bf16[2048,128]{1,0:T(8,128)(2,1)}) custom-call(s32[1]{0:T(128)} %bitcast.core_ref, bf16[2048,128]{1,0:T(8,128)(2,1)} %feats_ref.3, f32[128,2048]{1,0:T(8,128)} %field_ref.1), custom_call_target="tpu_custom_call" | custom-call | bytes 2097152 | tf_op jit(solution)/shard_map/pack/pallas_call | solution.py:34
  3.2 1.3 %collective-permute-start = (bf16[2048,128]{1,0:T(8,128)(2,1)}, bf16[2048,128]{1,0:T(8,128)(2,1)S(1)}, u32[]{:S(2)}, u32[]{:S(2)}) collective-permute-start(bf16[2048,128]{1,0:T(8,128)(2,1)} %get-tuple-element.16), channel_id=1, source_target_pairs={{0,2},{3,1},{2,4},{5,3},{4,6},{7,5},{6,8},{9,7},{8,10},{11,9},{10,... | collective-permute-start | bytes 1572872 | tf_op jit(solution)/shard_map/ppermute | solution.py:316
  4.4 1.3 %collective-permute-start.4 = (bf16[2048,128]{1,0:T(8,128)(2,1)}, bf16[2048,128]{1,0:T(8,128)(2,1)S(1)}, u32[]{:S(2)}, u32[]{:S(2)}) collective-permute-start(bf16[2048,128]{1,0:T(8,128)(2,1)} %get-tuple-element.17.packed), channel_id=1, source_target_pairs={{0,2},{3,1},{2,4},{5,3},{4,6},{7,5},{6,8},{9,7},{8,10},{11,9},{10,... | collective-permute-start | bytes 1572872 | tf_op jit(solution)/shard_map/ppermute | solution.py:316
  6.8 5.1 %own_block.1 = (f32[136,2048]{1,0:T(8,128)S(1)}, bf16[2048,128]{1,0:T(8,128)(2,1)S(1)}, f32[2048,128]{1,0:T(8,128)S(1)}) custom-call(s32[1]{0:T(128)} %bitcast.core_ref, bf16[2048,128]{1,0:T(8,128)(2,1)S(1)} %copy-done, bf16[2048,128]{1,0:T(8,128)(2,1)S(1)} %copy-done.1), custom_call_target="tpu_custom_call" | custom-call | flops 1073741824 | bytes 4194304 | tf_op jit(solution)/shard_map/own_block/pallas_call | solution.py:111
  11.9 2.4 %collective-permute-done = bf16[2048,128]{1,0:T(8,128)(2,1)S(1)} collective-permute-done((bf16[2048,128]{1,0:T(8,128)(2,1)}, bf16[2048,128]{1,0:T(8,128)(2,1)S(1)}, u32[]{:S(2)}, u32[]{:S(2)}) %collective-permute-start) | collective-permute-done | bytes 524320 | tf_op jit(solution)/shard_map/ppermute | solution.py:316
  14.3 6.5 %collective-permute-start.2 = (bf16[2048,128]{1,0:T(8,128)(2,1)S(1)}, bf16[2048,128]{1,0:T(8,128)(2,1)S(1)}, u32[]{:S(2)}, u32[]{:S(2)}) collective-permute-start(bf16[2048,128]{1,0:T(8,128)(2,1)S(1)} %collective-permute-done), channel_id=1, source_target_pairs={{0,1},{1,0},{2,3},{3,2},{4,5},{5,4},{6,7},{7,6},{8,9},{9,8},{10,11... | collective-permute-start | bytes 1572872 | tf_op jit(solution)/shard_map/ppermute | solution.py:306
  20.8 1.3 %collective-permute-start.1 = (bf16[2048,128]{1,0:T(8,128)(2,1)S(1)}, bf16[2048,128]{1,0:T(8,128)(2,1)S(1)}, u32[]{:S(2)}, u32[]{:S(2)}) collective-permute-start(bf16[2048,128]{1,0:T(8,128)(2,1)S(1)} %collective-permute-done), channel_id=1, source_target_pairs={{0,2},{3,1},{2,4},{5,3},{4,6},{7,5},{6,8},{9,7},{8,10},{11,9},{10,... | collective-permute-start | bytes 1572872 | tf_op jit(solution)/shard_map/ppermute | solution.py:316
  23.5 1.3 %collective-permute-start.5 = (bf16[2048,128]{1,0:T(8,128)(2,1)S(1)}, bf16[2048,128]{1,0:T(8,128)(2,1)S(1)}, u32[]{:S(2)}, u32[]{:S(2)}) collective-permute-start(bf16[2048,128]{1,0:T(8,128)(2,1)S(1)} %collective-permute-done.4.refs_0_), channel_id=1, source_target_pairs={{0,2},{3,1},{2,4},{5,3},{4,6},{7,5},{6,8},{9,7},{8,10},{11,9},{10,... | collective-permute-start | bytes 1572872 | tf_op jit(solution)/shard_map/ppermute | solution.py:316
  24.8 6.0 %collective-permute-done.1 = bf16[2048,128]{1,0:T(8,128)(2,1)S(1)} collective-permute-done((bf16[2048,128]{1,0:T(8,128)(2,1)S(1)}, bf16[2048,128]{1,0:T(8,128)(2,1)S(1)}, u32[]{:S(2)}, u32[]{:S(2)}) %collective-permute-start.1) | collective-permute-done | bytes 524320 | tf_op jit(solution)/shard_map/ppermute | solution.py:316
  30.8 1.3 %collective-permute-start.8 = (bf16[2048,128]{1,0:T(8,128)(2,1)S(1)}, bf16[2048,128]{1,0:T(8,128)(2,1)S(1)}, u32[]{:S(2)}, u32[]{:S(2)}) collective-permute-start(bf16[2048,128]{1,0:T(8,128)(2,1)S(1)} %collective-permute-done.1), channel_id=1, source_target_pairs={{0,2},{3,1},{2,4},{5,3},{4,6},{7,5},{6,8},{9,7},{8,10},{11,9},{10,... | collective-permute-start | bytes 1572872 | tf_op jit(solution)/shard_map/ppermute | solution.py:316
  32.1 5.8 %collective-permute-start.7 = (bf16[2048,128]{1,0:T(8,128)(2,1)S(1)}, bf16[2048,128]{1,0:T(8,128)(2,1)S(1)}, u32[]{:S(2)}, u32[]{:S(2)}) collective-permute-start(bf16[2048,128]{1,0:T(8,128)(2,1)S(1)} %collective-permute-done.1), channel_id=1, source_target_pairs={{0,1},{1,0},{2,3},{3,2},{4,5},{5,4},{6,7},{7,6},{8,9},{9,8},{10,11... | collective-permute-start | bytes 1572872 | tf_op jit(solution)/shard_map/ppermute | solution.py:306
  37.9 1.3 %collective-permute-start.6 = (bf16[2048,128]{1,0:T(8,128)(2,1)S(1)}, bf16[2048,128]{1,0:T(8,128)(2,1)S(1)}, u32[]{:S(2)}, u32[]{:S(2)}) collective-permute-start(bf16[2048,128]{1,0:T(8,128)(2,1)S(1)} %collective-permute-done.5.refs_1_), channel_id=1, source_target_pairs={{0,2},{3,1},{2,4},{5,3},{4,6},{7,5},{6,8},{9,7},{8,10},{11,9},{10,... | collective-permute-start | bytes 1572872 | tf_op jit(solution)/shard_map/ppermute | solution.py:316
  39.2 2.9 %collective-permute-done.8 = bf16[2048,128]{1,0:T(8,128)(2,1)S(1)} collective-permute-done((bf16[2048,128]{1,0:T(8,128)(2,1)S(1)}, bf16[2048,128]{1,0:T(8,128)(2,1)S(1)}, u32[]{:S(2)}, u32[]{:S(2)}) %collective-permute-start.8) | collective-permute-done | bytes 524320 | tf_op jit(solution)/shard_map/ppermute | solution.py:316
  42.1 2.7 %collective-permute-start.9 = (bf16[2048,128]{1,0:T(8,128)(2,1)S(1)}, bf16[2048,128]{1,0:T(8,128)(2,1)S(1)}, u32[]{:S(2)}, u32[]{:S(2)}) collective-permute-start(bf16[2048,128]{1,0:T(8,128)(2,1)S(1)} %collective-permute-done.8), channel_id=1, source_target_pairs={{0,1},{1,0},{2,3},{3,2},{4,5},{5,4},{6,7},{7,6},{8,9},{9,8},{10,11... | collective-permute-start | bytes 1572872 | tf_op jit(solution)/shard_map/ppermute | solution.py:306
  44.9 1.9 %collective-permute-start.3 = (s32[1,2]{1,0:T(1,128)S(1)}, s32[1,2]{1,0:T(1,128)S(1)}, u32[]{:S(2)}, u32[]{:S(2)}) collective-permute-start(s32[1,2]{1,0:T(1,128)S(1)} %pad_add_fusion.here), channel_id=1, source_target_pairs={{0,1},{1,0},{2,3},{3,2},{4,5},{5,4},{6,7},{7,6},{8,9},{9,8},{10,11... | collective-permute-start | bytes 32 | tf_op jit(solution)/shard_map/ppermute | solution.py:306
  46.8 1.1 collective-permute-done.3.there
  48.6 3.5 %partners_far.1 = f32[136,1024]{1,0:T(8,128)S(1)} custom-call(s32[1]{0:T(128)} %bitcast.core_ref, s32[1,2]{1,0:T(1,128)S(1)} %pad_add_fusion.here, s32[1,2]{1,0:T(1,128)S(1)} %collective-permute-done.3.there, bf16[2048,128]{1,0:T(8,128)(2,1)S(1)} %get-tuple-element.23.rows, f32[2048,128]{1,0:T(8,128)S(1)} %get-tuple-element.24.wide_norms, ...), custom_call_target="tpu_custom_call" | custom-call | flops 1073741824 | bytes 3145728 | tf_op jit(solution)/shard_map/partners_far/pallas_call | solution.py:190
  52.1 2.3 %collective-permute-start.10 = (f32[136,1024]{1,0:T(8,128)S(1)}, f32[136,1024]{1,0:T(8,128)S(1)}, u32[]{:S(2)}, u32[]{:S(2)}) collective-permute-start(f32[136,1024]{1,0:T(8,128)S(1)} %partners_far.1), channel_id=1, source_target_pairs={{0,1},{1,0},{2,3},{3,2},{4,5},{5,4},{6,7},{7,6},{8,9},{9,8},{10,11... | collective-permute-start | bytes 1671176 | tf_op jit(solution)/shard_map/ppermute | solution.py:306
  54.4 3.5 %partners_near.1.sums = f32[136,1024]{1,0:T(8,128)S(1)} custom-call(s32[1]{0:T(128)} %bitcast.core_ref, s32[1,2]{1,0:T(1,128)S(1)} %pad_add_fusion.here, s32[1,2]{1,0:T(1,128)S(1)} %collective-permute-done.3.there, bf16[2048,128]{1,0:T(8,128)(2,1)S(1)} %get-tuple-element.23.rows, f32[2048,128]{1,0:T(8,128)S(1)} %get-tuple-element.24.wide_norms, ...), custom_call_target="tpu_custom_call" | custom-call | flops 1073741824 | bytes 3145728 | tf_op jit(solution)/shard_map/partners_near/pallas_call | solution.py:190
  58.5 2.0 %collective-permute-start.11 = (f32[128,1024]{1,0:T(8,128)S(1)}, f32[128,1024]{1,0:T(8,128)S(1)}, u32[]{:S(2)}, u32[]{:S(2)}) collective-permute-start(f32[128,1024]{1,0:T(8,128)S(1)} %get-tuple-element.28.own), channel_id=1, source_target_pairs={{0,1},{1,0},{2,3},{3,2},{4,5},{5,4},{6,7},{7,6},{8,9},{9,8},{10,11... | collective-permute-start | bytes 1572872 | tf_op jit(solution)/shard_map/ppermute | solution.py:306
  60.6 27.0 %all_to_all.15 = f32[16,8,128]{2,1,0:T(8,128)S(1)} all-to-all(f32[16,8,128]{2,1,0:T(8,128)S(1)} %get-tuple-element.29), channel_id=1, replica_groups={{0,32,64,96,128,160,192,224,256,288,320,352,384,416,448,480},{2,34,66,9..., dimensions={0} | all-to-all | bytes 131072 | tf_op jit(solution)/shard_map/all_to_all | solution.py:291
  87.6 3.8 %collective-permute-start.12 = (f32[8,128]{1,0:T(8,128)S(1)}, f32[8,128]{1,0:T(8,128)S(1)}, u32[]{:S(2)}, u32[]{:S(2)}) collective-permute-start(f32[8,128]{1,0:T(8,128)S(1)} %reduce_sum.18), channel_id=1, source_target_pairs={{0,1},{1,0},{2,3},{3,2},{4,5},{5,4},{6,7},{7,6},{8,9},{9,8},{10,11... | collective-permute-start | bytes 12296 | tf_op jit(solution)/shard_map/ppermute | solution.py:306
  92.2 15.2 %all_to_all.16 = f32[16,8,128]{2,1,0:T(8,128)S(1)} all-to-all(f32[16,8,128]{2,1,0:T(8,128)S(1)} %broadcast_in_dim.6), channel_id=1, replica_groups={{0,2,4,6,8,10,12,14,16,18,20,22,24,26,28,30},{32,34,36,38,40,42,44,46,4..., dimensions={0} | all-to-all | bytes 131072 | tf_op jit(solution)/shard_map/all_to_all | solution.py:291
  107.5 9.4 %all_to_all.17.tiles = f32[16,8,128]{2,1,0:T(8,128)S(1)} all-to-all(f32[16,8,128]{2,1,0:T(8,128)S(1)} %broadcast_in_dim.7), channel_id=1, replica_groups={{0,32,64,96,128,160,192,224,256,288,320,352,384,416,448,480},{2,34,66,9..., dimensions={0} | all-to-all | bytes 131072 | tf_op jit(solution)/shard_map/all_to_all | solution.py:291
  (21 shorter events, 4.3 us)
Async XLA Ops:
  0.6 5.1 %copy-start = (bf16[2048,128]{1,0:T(8,128)(2,1)S(1)}, bf16[2048,128]{1,0:T(8,128)(2,1)}, u32[]{:S(2)}) copy-start(bf16[2048,128]{1,0:T(8,128)(2,1)} %feats_ref.3) | copy-start | bytes 1572868
  3.2 11.1 %collective-permute-start = (bf16[2048,128]{1,0:T(8,128)(2,1)}, bf16[2048,128]{1,0:T(8,128)(2,1)S(1)}, u32[]{:S(2)}, u32[]{:S(2)}) collective-permute-start(bf16[2048,128]{1,0:T(8,128)(2,1)} %get-tuple-element.16), channel_id=1, source_target_pairs={{0,2},{3,1},{2,4},{5,3},{4,6},{7,5},{6,8},{9,7},{8,10},{11,9},{10,... | collective-permute-start | bytes 1572872 | tf_op jit(solution)/shard_map/ppermute | solution.py:316
  4.4 19.0 %collective-permute-start.4 = (bf16[2048,128]{1,0:T(8,128)(2,1)}, bf16[2048,128]{1,0:T(8,128)(2,1)S(1)}, u32[]{:S(2)}, u32[]{:S(2)}) collective-permute-start(bf16[2048,128]{1,0:T(8,128)(2,1)} %get-tuple-element.17.packed), channel_id=1, source_target_pairs={{0,2},{3,1},{2,4},{5,3},{4,6},{7,5},{6,8},{9,7},{8,10},{11,9},{10,... | collective-permute-start | bytes 1572872 | tf_op jit(solution)/shard_map/ppermute | solution.py:316
  5.8 1.0 copy-start.1
  14.3 10.5 %collective-permute-start.2 = (bf16[2048,128]{1,0:T(8,128)(2,1)S(1)}, bf16[2048,128]{1,0:T(8,128)(2,1)S(1)}, u32[]{:S(2)}, u32[]{:S(2)}) collective-permute-start(bf16[2048,128]{1,0:T(8,128)(2,1)S(1)} %collective-permute-done), channel_id=1, source_target_pairs={{0,1},{1,0},{2,3},{3,2},{4,5},{5,4},{6,7},{7,6},{8,9},{9,8},{10,11... | collective-permute-start | bytes 1572872 | tf_op jit(solution)/shard_map/ppermute | solution.py:306
  20.8 10.0 %collective-permute-start.1 = (bf16[2048,128]{1,0:T(8,128)(2,1)S(1)}, bf16[2048,128]{1,0:T(8,128)(2,1)S(1)}, u32[]{:S(2)}, u32[]{:S(2)}) collective-permute-start(bf16[2048,128]{1,0:T(8,128)(2,1)S(1)} %collective-permute-done), channel_id=1, source_target_pairs={{0,2},{3,1},{2,4},{5,3},{4,6},{7,5},{6,8},{9,7},{8,10},{11,9},{10,... | collective-permute-start | bytes 1572872 | tf_op jit(solution)/shard_map/ppermute | solution.py:316
  23.5 14.4 %collective-permute-start.5 = (bf16[2048,128]{1,0:T(8,128)(2,1)S(1)}, bf16[2048,128]{1,0:T(8,128)(2,1)S(1)}, u32[]{:S(2)}, u32[]{:S(2)}) collective-permute-start(bf16[2048,128]{1,0:T(8,128)(2,1)S(1)} %collective-permute-done.4.refs_0_), channel_id=1, source_target_pairs={{0,2},{3,1},{2,4},{5,3},{4,6},{7,5},{6,8},{9,7},{8,10},{11,9},{10,... | collective-permute-start | bytes 1572872 | tf_op jit(solution)/shard_map/ppermute | solution.py:316
  30.8 11.3 %collective-permute-start.8 = (bf16[2048,128]{1,0:T(8,128)(2,1)S(1)}, bf16[2048,128]{1,0:T(8,128)(2,1)S(1)}, u32[]{:S(2)}, u32[]{:S(2)}) collective-permute-start(bf16[2048,128]{1,0:T(8,128)(2,1)S(1)} %collective-permute-done.1), channel_id=1, source_target_pairs={{0,2},{3,1},{2,4},{5,3},{4,6},{7,5},{6,8},{9,7},{8,10},{11,9},{10,... | collective-permute-start | bytes 1572872 | tf_op jit(solution)/shard_map/ppermute | solution.py:316
  32.1 16.5 %collective-permute-start.7 = (bf16[2048,128]{1,0:T(8,128)(2,1)S(1)}, bf16[2048,128]{1,0:T(8,128)(2,1)S(1)}, u32[]{:S(2)}, u32[]{:S(2)}) collective-permute-start(bf16[2048,128]{1,0:T(8,128)(2,1)S(1)} %collective-permute-done.1), channel_id=1, source_target_pairs={{0,1},{1,0},{2,3},{3,2},{4,5},{5,4},{6,7},{7,6},{8,9},{9,8},{10,11... | collective-permute-start | bytes 1572872 | tf_op jit(solution)/shard_map/ppermute | solution.py:306
  37.9 10.6 %collective-permute-start.6 = (bf16[2048,128]{1,0:T(8,128)(2,1)S(1)}, bf16[2048,128]{1,0:T(8,128)(2,1)S(1)}, u32[]{:S(2)}, u32[]{:S(2)}) collective-permute-start(bf16[2048,128]{1,0:T(8,128)(2,1)S(1)} %collective-permute-done.5.refs_1_), channel_id=1, source_target_pairs={{0,2},{3,1},{2,4},{5,3},{4,6},{7,5},{6,8},{9,7},{8,10},{11,9},{10,... | collective-permute-start | bytes 1572872 | tf_op jit(solution)/shard_map/ppermute | solution.py:316
  42.1 6.4 %collective-permute-start.9 = (bf16[2048,128]{1,0:T(8,128)(2,1)S(1)}, bf16[2048,128]{1,0:T(8,128)(2,1)S(1)}, u32[]{:S(2)}, u32[]{:S(2)}) collective-permute-start(bf16[2048,128]{1,0:T(8,128)(2,1)S(1)} %collective-permute-done.8), channel_id=1, source_target_pairs={{0,1},{1,0},{2,3},{3,2},{4,5},{5,4},{6,7},{7,6},{8,9},{9,8},{10,11... | collective-permute-start | bytes 1572872 | tf_op jit(solution)/shard_map/ppermute | solution.py:306
  44.9 3.0 %collective-permute-start.3 = (s32[1,2]{1,0:T(1,128)S(1)}, s32[1,2]{1,0:T(1,128)S(1)}, u32[]{:S(2)}, u32[]{:S(2)}) collective-permute-start(s32[1,2]{1,0:T(1,128)S(1)} %pad_add_fusion.here), channel_id=1, source_target_pairs={{0,1},{1,0},{2,3},{3,2},{4,5},{5,4},{6,7},{7,6},{8,9},{9,8},{10,11... | collective-permute-start | bytes 32 | tf_op jit(solution)/shard_map/ppermute | solution.py:306
  52.1 5.8 %collective-permute-start.10 = (f32[136,1024]{1,0:T(8,128)S(1)}, f32[136,1024]{1,0:T(8,128)S(1)}, u32[]{:S(2)}, u32[]{:S(2)}) collective-permute-start(f32[136,1024]{1,0:T(8,128)S(1)} %partners_far.1), channel_id=1, source_target_pairs={{0,1},{1,0},{2,3},{3,2},{4,5},{5,4},{6,7},{7,6},{8,9},{9,8},{10,11... | collective-permute-start | bytes 1671176 | tf_op jit(solution)/shard_map/ppermute | solution.py:306
  58.5 58.3 %collective-permute-start.11 = (f32[128,1024]{1,0:T(8,128)S(1)}, f32[128,1024]{1,0:T(8,128)S(1)}, u32[]{:S(2)}, u32[]{:S(2)}) collective-permute-start(f32[128,1024]{1,0:T(8,128)S(1)} %get-tuple-element.28.own), channel_id=1, source_target_pairs={{0,1},{1,0},{2,3},{3,2},{4,5},{5,4},{6,7},{7,6},{8,9},{9,8},{10,11... | collective-permute-start | bytes 1572872 | tf_op jit(solution)/shard_map/ppermute | solution.py:306
  87.6 4.6 %collective-permute-start.12 = (f32[8,128]{1,0:T(8,128)S(1)}, f32[8,128]{1,0:T(8,128)S(1)}, u32[]{:S(2)}, u32[]{:S(2)}) collective-permute-start(f32[8,128]{1,0:T(8,128)S(1)} %reduce_sum.18), channel_id=1, source_target_pairs={{0,1},{1,0},{2,3},{3,2},{4,5},{5,4},{6,7},{7,6},{8,9},{9,8},{10,11... | collective-permute-start | bytes 12296 | tf_op jit(solution)/shard_map/ppermute | solution.py:306

commit v9 on v8

--- a/solution.py
+++ b/solution.py
@@ -322,17 +322,19 @@
     here = jnp.concatenate([offsets, counts], axis=1)
     give, keep = pack(core, features, subspace)
     own_sums, rows, wide_norms = apply_self(core, features, keep)
-    kept, swapped = [], []
+    kept, given = [], []
     for step in range(REACH):
         give, keep = relay(give), relay(keep)
         if step == 0:
             give, own_sums, rows, wide_norms = lax.optimization_barrier(
                 (give, own_sums, rows, wide_norms)
             )
+        kept.append(keep)
+        given.append(give)
         if step == 1:
-            give, swapped[0], here = lax.optimization_barrier((give, swapped[0], here))
-        kept.append(keep)
-        swapped.append(swap(give))
+            keep, given[0], given[1], here = lax.optimization_barrier((keep, *given, here))
+            kept[1] = keep
+    swapped = [swap(x) for x in given]
     there = swap(here)
     near = kept + swapped
     far = apply_partners("far", core, here, there, rows, wide_norms, own_sums, near)

time: 120 us -> 120 us (level)
  waiting for transfers between devices: 13.9 us -> 16.7 us
  blocking collectives: 51.6 us -> 50.2 us
    ppermute x6, waiting for transfers between devices: 12 us -> 14.8 us  [relay(): return lax.ppermute(x, ('blk', 'pair'), pairs)]
    all_to_all x3, blocking collectives: 51.6 us -> 50.2 us  [exchange(): lax.all_to_all(tiles, 'blk', 0, 0, axis_index_groups=groups, tiled=True)]
  transfers between devices with their start and end apart: 13 -> 13, of which waited for: 6 -> 7; matrix products, arithmetic and copies ran while one was open for 0% -> 0% of each run, Pallas kernels for 7% -> 7%
where the time goes in v9:
time: 120 us; the launch traced here: 118 us
  blocking collectives  50.2 us (42%)
  starting transfers between devices  31.8 us (26%)
  waiting for transfers between devices  16.7 us (14%)
  Pallas kernels  16.2 us (14%)
  between operations  2.11 us (2%)
    all_to_all x3, blocking collectives, exchange(): lax.all_to_all(tiles, 'blk', 0, 0, axis_index_groups=groups, tiled=True)  50.2 us
    ppermute x7, starting transfers between devices, swap(): return lax.ppermute(x, 'pair', [(0, 1), (1, 0)])  24.1 us
    ppermute x6, waiting for transfers between devices, relay(): return lax.ppermute(x, ('blk', 'pair'), pairs)  14.8 us
    ppermute x6, starting transfers between devices, relay(): return lax.ppermute(x, ('blk', 'pair'), pairs)  7.71 us
    pallas_call x2, Pallas kernels, apply_partners(): pl.pallas_call(partner_kernel, grid_spec=pltpu.PrefetchScalarGridSpec(num...  6.98 us
    pallas_call x1, Pallas kernels, apply_self(): pl.pallas_call(self_kernel, grid_spec=pltpu.PrefetchScalarGridSpec(num_sc...  5.1 us
    pallas_call x1, Pallas kernels, pack(): pl.pallas_call(pack_kernel, grid_spec=pltpu.PrefetchScalarGridSpec(num_sc...  2.51 us
  transfers between devices with their start and end apart: 13, of which 7 were waited for; matrix products, arithmetic and copies ran while one was open for 0% of the time, Pallas kernels for 7%

profile of v9, /device:TPU:1, one launch (start us, length us, event | category | flops | bytes accessed | tf_op | source)
XLA Modules:
  0.0 118.3 jit_solution(13583077925657276751)
XLA Ops:
  0.6 2.5 %pack.1 = (bf16[2048,128]{1,0:T(8,128)(2,1)}, bf16[2048,128]{1,0:T(8,128)(2,1)}) custom-call(s32[1]{0:T(128)} %bitcast.core_ref, bf16[2048,128]{1,0:T(8,128)(2,1)} %feats_ref.3, f32[128,2048]{1,0:T(8,128)} %field_ref.1), custom_call_target="tpu_custom_call" | custom-call | bytes 2097152 | tf_op jit(solution)/shard_map/pack/pallas_call | solution.py:34
  3.2 1.3 %collective-permute-start.2 = (bf16[2048,128]{1,0:T(8,128)(2,1)}, bf16[2048,128]{1,0:T(8,128)(2,1)S(1)}, u32[]{:S(2)}, u32[]{:S(2)}) collective-permute-start(bf16[2048,128]{1,0:T(8,128)(2,1)} %get-tuple-element.18), channel_id=1, source_target_pairs={{0,2},{3,1},{2,4},{5,3},{4,6},{7,5},{6,8},{9,7},{8,10},{11,9},{10,... | collective-permute-start | bytes 1572872 | tf_op jit(solution)/shard_map/ppermute | solution.py:316
  4.4 1.3 %collective-permute-start = (bf16[2048,128]{1,0:T(8,128)(2,1)}, bf16[2048,128]{1,0:T(8,128)(2,1)S(1)}, u32[]{:S(2)}, u32[]{:S(2)}) collective-permute-start(bf16[2048,128]{1,0:T(8,128)(2,1)} %get-tuple-element.17.packed), channel_id=1, source_target_pairs={{0,2},{3,1},{2,4},{5,3},{4,6},{7,5},{6,8},{9,7},{8,10},{11,9},{10,... | collective-permute-start | bytes 1572872 | tf_op jit(solution)/shard_map/ppermute | solution.py:316
  6.8 5.1 %own_block.1 = (f32[136,2048]{1,0:T(8,128)S(1)}, bf16[2048,128]{1,0:T(8,128)(2,1)S(1)}, f32[2048,128]{1,0:T(8,128)S(1)}) custom-call(s32[1]{0:T(128)} %bitcast.core_ref, bf16[2048,128]{1,0:T(8,128)(2,1)S(1)} %copy-done, bf16[2048,128]{1,0:T(8,128)(2,1)S(1)} %copy-done.1), custom_call_target="tpu_custom_call" | custom-call | flops 1073741824 | bytes 4194304 | tf_op jit(solution)/shard_map/own_block/pallas_call | solution.py:111
  11.9 2.4 %collective-permute-done.2 = bf16[2048,128]{1,0:T(8,128)(2,1)S(1)} collective-permute-done((bf16[2048,128]{1,0:T(8,128)(2,1)}, bf16[2048,128]{1,0:T(8,128)(2,1)S(1)}, u32[]{:S(2)}, u32[]{:S(2)}) %collective-permute-start.2) | collective-permute-done | bytes 524320 | tf_op jit(solution)/shard_map/ppermute | solution.py:316
  14.3 1.3 %collective-permute-start.3 = (bf16[2048,128]{1,0:T(8,128)(2,1)S(1)}, bf16[2048,128]{1,0:T(8,128)(2,1)S(1)}, u32[]{:S(2)}, u32[]{:S(2)}) collective-permute-start(bf16[2048,128]{1,0:T(8,128)(2,1)S(1)} %collective-permute-done.2), channel_id=1, source_target_pairs={{0,2},{3,1},{2,4},{5,3},{4,6},{7,5},{6,8},{9,7},{8,10},{11,9},{10,... | collective-permute-start | bytes 1572872 | tf_op jit(solution)/shard_map/ppermute | solution.py:316
  15.6 4.3 %collective-permute-done.refs_0_ = bf16[2048,128]{1,0:T(8,128)(2,1)S(1)} collective-permute-done((bf16[2048,128]{1,0:T(8,128)(2,1)}, bf16[2048,128]{1,0:T(8,128)(2,1)S(1)}, u32[]{:S(2)}, u32[]{:S(2)}) %collective-permute-start) | collective-permute-done | bytes 524320 | tf_op jit(solution)/shard_map/ppermute | solution.py:316
  19.9 1.3 %collective-permute-start.1 = (bf16[2048,128]{1,0:T(8,128)(2,1)S(1)}, bf16[2048,128]{1,0:T(8,128)(2,1)S(1)}, u32[]{:S(2)}, u32[]{:S(2)}) collective-permute-start(bf16[2048,128]{1,0:T(8,128)(2,1)S(1)} %collective-permute-done.refs_0_), channel_id=1, source_target_pairs={{0,2},{3,1},{2,4},{5,3},{4,6},{7,5},{6,8},{9,7},{8,10},{11,9},{10,... | collective-permute-start | bytes 1572872 | tf_op jit(solution)/shard_map/ppermute | solution.py:316
  21.2 4.3 %collective-permute-done.3 = bf16[2048,128]{1,0:T(8,128)(2,1)S(1)} collective-permute-done((bf16[2048,128]{1,0:T(8,128)(2,1)S(1)}, bf16[2048,128]{1,0:T(8,128)(2,1)S(1)}, u32[]{:S(2)}, u32[]{:S(2)}) %collective-permute-start.3) | collective-permute-done | bytes 524320 | tf_op jit(solution)/shard_map/ppermute | solution.py:316
  25.5 1.3 %collective-permute-start.8 = (bf16[2048,128]{1,0:T(8,128)(2,1)S(1)}, bf16[2048,128]{1,0:T(8,128)(2,1)S(1)}, u32[]{:S(2)}, u32[]{:S(2)}) collective-permute-start(bf16[2048,128]{1,0:T(8,128)(2,1)S(1)} %collective-permute-done.3), channel_id=1, source_target_pairs={{0,2},{3,1},{2,4},{5,3},{4,6},{7,5},{6,8},{9,7},{8,10},{11,9},{10,... | collective-permute-start | bytes 1572872 | tf_op jit(solution)/shard_map/ppermute | solution.py:316
  28.2 3.0 %collective-permute-done.1.refs_1_ = bf16[2048,128]{1,0:T(8,128)(2,1)S(1)} collective-permute-done((bf16[2048,128]{1,0:T(8,128)(2,1)S(1)}, bf16[2048,128]{1,0:T(8,128)(2,1)S(1)}, u32[]{:S(2)}, u32[]{:S(2)}) %collective-permute-start.1) | collective-permute-done | bytes 524320 | tf_op jit(solution)/shard_map/ppermute | solution.py:316
  31.1 6.2 %collective-permute-start.6 = (bf16[2048,128]{1,0:T(8,128)(2,1)S(1)}, bf16[2048,128]{1,0:T(8,128)(2,1)S(1)}, u32[]{:S(2)}, u32[]{:S(2)}) collective-permute-start(bf16[2048,128]{1,0:T(8,128)(2,1)S(1)} %collective-permute-done.2), channel_id=1, source_target_pairs={{0,1},{1,0},{2,3},{3,2},{4,5},{5,4},{6,7},{7,6},{8,9},{9,8},{10,11... | collective-permute-start | bytes 1572872 | tf_op jit(solution)/shard_map/ppermute | solution.py:306
  37.3 1.9 %collective-permute-start.7 = (bf16[2048,128]{1,0:T(8,128)(2,1)S(1)}, bf16[2048,128]{1,0:T(8,128)(2,1)S(1)}, u32[]{:S(2)}, u32[]{:S(2)}) collective-permute-start(bf16[2048,128]{1,0:T(8,128)(2,1)S(1)} %collective-permute-done.3), channel_id=1, source_target_pairs={{0,1},{1,0},{2,3},{3,2},{4,5},{5,4},{6,7},{7,6},{8,9},{9,8},{10,11... | collective-permute-start | bytes 1572872 | tf_op jit(solution)/shard_map/ppermute | solution.py:306
  39.3 1.3 %collective-permute-start.5 = (bf16[2048,128]{1,0:T(8,128)(2,1)S(1)}, bf16[2048,128]{1,0:T(8,128)(2,1)S(1)}, u32[]{:S(2)}, u32[]{:S(2)}) collective-permute-start(bf16[2048,128]{1,0:T(8,128)(2,1)S(1)} %collective-permute-done.1.refs_1_), channel_id=1, source_target_pairs={{0,2},{3,1},{2,4},{5,3},{4,6},{7,5},{6,8},{9,7},{8,10},{11,9},{10,... | collective-permute-start | bytes 1572872 | tf_op jit(solution)/shard_map/ppermute | solution.py:316
  40.6 5.5 %collective-permute-start.9 = (bf16[2048,128]{1,0:T(8,128)(2,1)S(1)}, bf16[2048,128]{1,0:T(8,128)(2,1)S(1)}, u32[]{:S(2)}, u32[]{:S(2)}) collective-permute-start(bf16[2048,128]{1,0:T(8,128)(2,1)S(1)} %collective-permute-done.8), channel_id=1, source_target_pairs={{0,1},{1,0},{2,3},{3,2},{4,5},{5,4},{6,7},{7,6},{8,9},{9,8},{10,11... | collective-permute-start | bytes 1572872 | tf_op jit(solution)/shard_map/ppermute | solution.py:306
  46.1 1.9 %collective-permute-start.4 = (s32[1,2]{1,0:T(1,128)S(1)}, s32[1,2]{1,0:T(1,128)S(1)}, u32[]{:S(2)}, u32[]{:S(2)}) collective-permute-start(s32[1,2]{1,0:T(1,128)S(1)} %pad_add_fusion.here), channel_id=1, source_target_pairs={{0,1},{1,0},{2,3},{3,2},{4,5},{5,4},{6,7},{7,6},{8,9},{9,8},{10,11... | collective-permute-start | bytes 32 | tf_op jit(solution)/shard_map/ppermute | solution.py:306
  49.9 3.5 %partners_far.1 = f32[136,1024]{1,0:T(8,128)S(1)} custom-call(s32[1]{0:T(128)} %bitcast.core_ref, s32[1,2]{1,0:T(1,128)S(1)} %pad_add_fusion.here, s32[1,2]{1,0:T(1,128)S(1)} %collective-permute-done.4.there, bf16[2048,128]{1,0:T(8,128)(2,1)S(1)} %get-tuple-element.24.rows, f32[2048,128]{1,0:T(8,128)S(1)} %get-tuple-element.25.wide_norms, ...), custom_call_target="tpu_custom_call" | custom-call | flops 1073741824 | bytes 3145728 | tf_op jit(solution)/shard_map/partners_far/pallas_call | solution.py:190
  53.4 2.8 %collective-permute-start.10 = (f32[136,1024]{1,0:T(8,128)S(1)}, f32[136,1024]{1,0:T(8,128)S(1)}, u32[]{:S(2)}, u32[]{:S(2)}) collective-permute-start(f32[136,1024]{1,0:T(8,128)S(1)} %partners_far.1), channel_id=1, source_target_pairs={{0,1},{1,0},{2,3},{3,2},{4,5},{5,4},{6,7},{7,6},{8,9},{9,8},{10,11... | collective-permute-start | bytes 1671176 | tf_op jit(solution)/shard_map/ppermute | solution.py:306
  56.2 3.5 %partners_near.1.sums = f32[136,1024]{1,0:T(8,128)S(1)} custom-call(s32[1]{0:T(128)} %bitcast.core_ref, s32[1,2]{1,0:T(1,128)S(1)} %pad_add_fusion.here, s32[1,2]{1,0:T(1,128)S(1)} %collective-permute-done.4.there, bf16[2048,128]{1,0:T(8,128)(2,1)S(1)} %get-tuple-element.24.rows, f32[2048,128]{1,0:T(8,128)S(1)} %get-tuple-element.25.wide_norms, ...), custom_call_target="tpu_custom_call" | custom-call | flops 1073741824 | bytes 3145728 | tf_op jit(solution)/shard_map/partners_near/pallas_call | solution.py:190
  60.4 1.9 %collective-permute-start.11 = (f32[128,1024]{1,0:T(8,128)S(1)}, f32[128,1024]{1,0:T(8,128)S(1)}, u32[]{:S(2)}, u32[]{:S(2)}) collective-permute-start(f32[128,1024]{1,0:T(8,128)S(1)} %get-tuple-element.30.own), channel_id=1, source_target_pairs={{0,1},{1,0},{2,3},{3,2},{4,5},{5,4},{6,7},{7,6},{8,9},{9,8},{10,11... | collective-permute-start | bytes 1572872 | tf_op jit(solution)/shard_map/ppermute | solution.py:306
  62.3 26.6 %all_to_all.15 = f32[16,8,128]{2,1,0:T(8,128)S(1)} all-to-all(f32[16,8,128]{2,1,0:T(8,128)S(1)} %get-tuple-element.31), channel_id=1, replica_groups={{0,32,64,96,128,160,192,224,256,288,320,352,384,416,448,480},{2,34,66,9..., dimensions={0} | all-to-all | bytes 131072 | tf_op jit(solution)/shard_map/all_to_all | solution.py:291
  88.9 3.8 %collective-permute-start.12 = (f32[8,128]{1,0:T(8,128)S(1)}, f32[8,128]{1,0:T(8,128)S(1)}, u32[]{:S(2)}, u32[]{:S(2)}) collective-permute-start(f32[8,128]{1,0:T(8,128)S(1)} %reduce_sum.18), channel_id=1, source_target_pairs={{0,1},{1,0},{2,3},{3,2},{4,5},{5,4},{6,7},{7,6},{8,9},{9,8},{10,11... | collective-permute-start | bytes 12296 | tf_op jit(solution)/shard_map/ppermute | solution.py:306
  93.6 14.3 %all_to_all.16 = f32[16,8,128]{2,1,0:T(8,128)S(1)} all-to-all(f32[16,8,128]{2,1,0:T(8,128)S(1)} %broadcast_in_dim.6), channel_id=1, replica_groups={{0,2,4,6,8,10,12,14,16,18,20,22,24,26,28,30},{32,34,36,38,40,42,44,46,4..., dimensions={0} | all-to-all | bytes 131072 | tf_op jit(solution)/shard_map/all_to_all | solution.py:291
  107.9 9.4 %all_to_all.17.tiles = f32[16,8,128]{2,1,0:T(8,128)S(1)} all-to-all(f32[16,8,128]{2,1,0:T(8,128)S(1)} %broadcast_in_dim.7), channel_id=1, replica_groups={{0,32,64,96,128,160,192,224,256,288,320,352,384,416,448,480},{2,34,66,9..., dimensions={0} | all-to-all | bytes 131072 | tf_op jit(solution)/shard_map/all_to_all | solution.py:291
  (21 shorter events, 5.5 us)
Async XLA Ops:
  0.6 5.1 %copy-start = (bf16[2048,128]{1,0:T(8,128)(2,1)S(1)}, bf16[2048,128]{1,0:T(8,128)(2,1)}, u32[]{:S(2)}) copy-start(bf16[2048,128]{1,0:T(8,128)(2,1)} %feats_ref.3) | copy-start | bytes 1572868
  3.2 11.1 %collective-permute-start.2 = (bf16[2048,128]{1,0:T(8,128)(2,1)}, bf16[2048,128]{1,0:T(8,128)(2,1)S(1)}, u32[]{:S(2)}, u32[]{:S(2)}) collective-permute-start(bf16[2048,128]{1,0:T(8,128)(2,1)} %get-tuple-element.18), channel_id=1, source_target_pairs={{0,2},{3,1},{2,4},{5,3},{4,6},{7,5},{6,8},{9,7},{8,10},{11,9},{10,... | collective-permute-start | bytes 1572872 | tf_op jit(solution)/shard_map/ppermute | solution.py:316
  4.4 15.5 %collective-permute-start = (bf16[2048,128]{1,0:T(8,128)(2,1)}, bf16[2048,128]{1,0:T(8,128)(2,1)S(1)}, u32[]{:S(2)}, u32[]{:S(2)}) collective-permute-start(bf16[2048,128]{1,0:T(8,128)(2,1)} %get-tuple-element.17.packed), channel_id=1, source_target_pairs={{0,2},{3,1},{2,4},{5,3},{4,6},{7,5},{6,8},{9,7},{8,10},{11,9},{10,... | collective-permute-start | bytes 1572872 | tf_op jit(solution)/shard_map/ppermute | solution.py:316
  5.8 1.0 copy-start.1
  14.3 11.2 %collective-permute-start.3 = (bf16[2048,128]{1,0:T(8,128)(2,1)S(1)}, bf16[2048,128]{1,0:T(8,128)(2,1)S(1)}, u32[]{:S(2)}, u32[]{:S(2)}) collective-permute-start(bf16[2048,128]{1,0:T(8,128)(2,1)S(1)} %collective-permute-done.2), channel_id=1, source_target_pairs={{0,2},{3,1},{2,4},{5,3},{4,6},{7,5},{6,8},{9,7},{8,10},{11,9},{10,... | collective-permute-start | bytes 1572872 | tf_op jit(solution)/shard_map/ppermute | solution.py:316
  19.9 11.2 %collective-permute-start.1 = (bf16[2048,128]{1,0:T(8,128)(2,1)S(1)}, bf16[2048,128]{1,0:T(8,128)(2,1)S(1)}, u32[]{:S(2)}, u32[]{:S(2)}) collective-permute-start(bf16[2048,128]{1,0:T(8,128)(2,1)S(1)} %collective-permute-done.refs_0_), channel_id=1, source_target_pairs={{0,2},{3,1},{2,4},{5,3},{4,6},{7,5},{6,8},{9,7},{8,10},{11,9},{10,... | collective-permute-start | bytes 1572872 | tf_op jit(solution)/shard_map/ppermute | solution.py:316
  25.5 15.0 %collective-permute-start.8 = (bf16[2048,128]{1,0:T(8,128)(2,1)S(1)}, bf16[2048,128]{1,0:T(8,128)(2,1)S(1)}, u32[]{:S(2)}, u32[]{:S(2)}) collective-permute-start(bf16[2048,128]{1,0:T(8,128)(2,1)S(1)} %collective-permute-done.3), channel_id=1, source_target_pairs={{0,2},{3,1},{2,4},{5,3},{4,6},{7,5},{6,8},{9,7},{8,10},{11,9},{10,... | collective-permute-start | bytes 1572872 | tf_op jit(solution)/shard_map/ppermute | solution.py:316
  31.1 18.0 %collective-permute-start.6 = (bf16[2048,128]{1,0:T(8,128)(2,1)S(1)}, bf16[2048,128]{1,0:T(8,128)(2,1)S(1)}, u32[]{:S(2)}, u32[]{:S(2)}) collective-permute-start(bf16[2048,128]{1,0:T(8,128)(2,1)S(1)} %collective-permute-done.2), channel_id=1, source_target_pairs={{0,1},{1,0},{2,3},{3,2},{4,5},{5,4},{6,7},{7,6},{8,9},{9,8},{10,11... | collective-permute-start | bytes 1572872 | tf_op jit(solution)/shard_map/ppermute | solution.py:306
  37.3 11.8 %collective-permute-start.7 = (bf16[2048,128]{1,0:T(8,128)(2,1)S(1)}, bf16[2048,128]{1,0:T(8,128)(2,1)S(1)}, u32[]{:S(2)}, u32[]{:S(2)}) collective-permute-start(bf16[2048,128]{1,0:T(8,128)(2,1)S(1)} %collective-permute-done.3), channel_id=1, source_target_pairs={{0,1},{1,0},{2,3},{3,2},{4,5},{5,4},{6,7},{7,6},{8,9},{9,8},{10,11... | collective-permute-start | bytes 1572872 | tf_op jit(solution)/shard_map/ppermute | solution.py:306
  39.3 10.6 %collective-permute-start.5 = (bf16[2048,128]{1,0:T(8,128)(2,1)S(1)}, bf16[2048,128]{1,0:T(8,128)(2,1)S(1)}, u32[]{:S(2)}, u32[]{:S(2)}) collective-permute-start(bf16[2048,128]{1,0:T(8,128)(2,1)S(1)} %collective-permute-done.1.refs_1_), channel_id=1, source_target_pairs={{0,2},{3,1},{2,4},{5,3},{4,6},{7,5},{6,8},{9,7},{8,10},{11,9},{10,... | collective-permute-start | bytes 1572872 | tf_op jit(solution)/shard_map/ppermute | solution.py:316
  40.6 9.3 %collective-permute-start.9 = (bf16[2048,128]{1,0:T(8,128)(2,1)S(1)}, bf16[2048,128]{1,0:T(8,128)(2,1)S(1)}, u32[]{:S(2)}, u32[]{:S(2)}) collective-permute-start(bf16[2048,128]{1,0:T(8,128)(2,1)S(1)} %collective-permute-done.8), channel_id=1, source_target_pairs={{0,1},{1,0},{2,3},{3,2},{4,5},{5,4},{6,7},{7,6},{8,9},{9,8},{10,11... | collective-permute-start | bytes 1572872 | tf_op jit(solution)/shard_map/ppermute | solution.py:306
  46.1 3.0 %collective-permute-start.4 = (s32[1,2]{1,0:T(1,128)S(1)}, s32[1,2]{1,0:T(1,128)S(1)}, u32[]{:S(2)}, u32[]{:S(2)}) collective-permute-start(s32[1,2]{1,0:T(1,128)S(1)} %pad_add_fusion.here), channel_id=1, source_target_pairs={{0,1},{1,0},{2,3},{3,2},{4,5},{5,4},{6,7},{7,6},{8,9},{9,8},{10,11... | collective-permute-start | bytes 32 | tf_op jit(solution)/shard_map/ppermute | solution.py:306
  53.4 6.3 %collective-permute-start.10 = (f32[136,1024]{1,0:T(8,128)S(1)}, f32[136,1024]{1,0:T(8,128)S(1)}, u32[]{:S(2)}, u32[]{:S(2)}) collective-permute-start(f32[136,1024]{1,0:T(8,128)S(1)} %partners_far.1), channel_id=1, source_target_pairs={{0,1},{1,0},{2,3},{3,2},{4,5},{5,4},{6,7},{7,6},{8,9},{9,8},{10,11... | collective-permute-start | bytes 1671176 | tf_op jit(solution)/shard_map/ppermute | solution.py:306
  60.4 56.9 %collective-permute-start.11 = (f32[128,1024]{1,0:T(8,128)S(1)}, f32[128,1024]{1,0:T(8,128)S(1)}, u32[]{:S(2)}, u32[]{:S(2)}) collective-permute-start(f32[128,1024]{1,0:T(8,128)S(1)} %get-tuple-element.30.own), channel_id=1, source_target_pairs={{0,1},{1,0},{2,3},{3,2},{4,5},{5,4},{6,7},{7,6},{8,9},{9,8},{10,11... | collective-permute-start | bytes 1572872 | tf_op jit(solution)/shard_map/ppermute | solution.py:306
  88.9 4.6 %collective-permute-start.12 = (f32[8,128]{1,0:T(8,128)S(1)}, f32[8,128]{1,0:T(8,128)S(1)}, u32[]{:S(2)}, u32[]{:S(2)}) collective-permute-start(f32[8,128]{1,0:T(8,128)S(1)} %reduce_sum.18), channel_id=1, source_target_pairs={{0,1},{1,0},{2,3},{3,2},{4,5},{5,4},{6,7},{7,6},{8,9},{9,8},{10,11... | collective-permute-start | bytes 12296 | tf_op jit(solution)/shard_map/ppermute | solution.py:306
